TPU v7x, 128 devices: a whole 4x4x4 slice. The times are simulated.
128 devices in a mesh: pipe: 2 (over x_hi), group: 8 (over z, x_lo), rep: 8 (over y, core).
Axes of the slice: x: 4 (x_hi: 2, x_lo: 2; x = x_hi * 2 + x_lo), y: 4, z: 4, core: 2. Of those that a mesh axis runs over, the one named last changes fastest.
Arguments:
- block_input: bfloat16 [2, 8, 1024, 1088], P(None, 'rep', 'group'), may hold values from -6 to 6
- out_grad: bfloat16 [2, 8, 1024, 1088], P(None, 'rep', 'group'), may hold values from -6 to 6
- w_qkv: bfloat16 [2, 1088, 3264], P('pipe', 'group'), may hold values from -0.1875 to 0.1875
- w_proj: bfloat16 [2, 1088, 1088], P('pipe', 'group'), may hold values from -0.5 to 0.5
- w_up: bfloat16 [2, 1088, 4352], P('pipe', 'group'), may hold values from -0.1875 to 0.1875
- w_down: bfloat16 [2, 4352, 1088], P('pipe', 'group'), may hold values from -0.09375 to 0.09375
- vectors: bfloat16 [2, 8, 1088], P('pipe', None, 'group'), as said below
- b_up: bfloat16 [2, 4352], P('pipe', 'group'), may hold values from -3 to 3
- seq_lengths: int32 [16], replicated, may hold values from 512 to 1024, as said below
- slot_of_seq: int32 [16], replicated, may hold values from 0 to 15, as said below
Outputs:
- section_edges: float32 [2, 2, 8, 1024, 1088], P('pipe', None, 'rep', 'group')
- grad_qkv: float32 [2, 1088, 3264], P('pipe', 'group')
- grad_proj: float32 [2, 1088, 1088], P('pipe', 'group')
- grad_up: float32 [2, 1088, 4352], P('pipe', 'group')
- grad_down: float32 [2, 4352, 1088], P('pipe', 'group')
- grad_vectors: float32 [2, 8, 1088], P('pipe', None, 'group')
- grad_b_up: float32 [2, 4352], P('pipe', 'group')
Inputs may be any that keep to these rules, and one draw needn't show every extreme that they name: `seq_lengths`: lengths of whole sequences; in every replica group one of its 2 sequences has exactly 1024 tokens. `slot_of_seq`: A permutation of the slots: each slot holds exactly one sequence. `vectors`: rows 0 and 5 are norm gains near one, the other rows biases.
All inputs are finite; a program needn't handle non-finite values.
Results may differ from a plain program's by a relative error of at most 0.013.
Values may be sent and summed in bfloat16 or wider, within the bound.
A program may use at most 320 MiB of HBM per device.

v0:
```python
import jax
import jax.numpy as jnp
from jax import lax
from jax.sharding import PartitionSpec as P

HEAD = 64


EPSILON = 1e-05
MASKED = -1e30


def from_behind(value, axis, steps):
    count = lax.axis_size(axis)
    leading, last = (max(0, -steps), min(count, count - steps))
    return lax.ppermute(value, axis, [(source, source + steps) for source in range(leading, last)])


def norm_rows(inputs, gain_row, bias_row):
    average = jnp.mean(inputs, -1, keepdims=True)
    centered = inputs - average
    variance = jnp.mean(centered * centered, -1, keepdims=True)
    return centered * lax.rsqrt(variance + EPSILON) * gain_row + bias_row


def gelu_tanh(inputs):
    return jax.nn.gelu(inputs, approximate=True)


def run_active(active, function, operand, totals):
    new_totals, pieces = function(operand, totals)
    kept_totals = jax.tree.map(
        lambda fresh, older: jnp.where(active, fresh, older), new_totals, totals
    )
    kept_pieces = jax.tree.map(
        lambda fresh: jnp.where(active, fresh, jnp.zeros_like(fresh)), pieces
    )
    return (kept_totals, kept_pieces)


def split_heads(matrix):
    return matrix.reshape(matrix.shape[0], matrix.shape[1] // HEAD, HEAD)


def masked_scores(queries, key_rows, query_pos, key_pos, length):
    scores = jnp.einsum(
        "qhd,khd->hqk",
        split_heads(queries),
        split_heads(key_rows),
        preferred_element_type=jnp.float32,
    ) * HEAD ** (-0.5)
    allowed = (key_pos[None, :] <= query_pos[:, None]) & (key_pos[None, :] < length)
    return jnp.where(allowed[None], scores, MASKED)


def attend(queries, key_rows, values, query_pos, key_pos, length):
    scores = masked_scores(queries, key_rows, query_pos, key_pos, length)
    row_max = jnp.max(scores, -1, keepdims=True)
    log_total = row_max + jnp.log(jnp.sum(jnp.exp(scores - row_max), -1, keepdims=True))
    attn_probs = jnp.exp(scores - log_total).astype(jnp.bfloat16)
    attn_mixed = jnp.einsum(
        "hqk,khd->qhd", attn_probs, split_heads(values), preferred_element_type=jnp.float32
    )
    return (attn_mixed.reshape(queries.shape).astype(jnp.bfloat16), log_total)


def finish(inputs, attn_mixed, proj_weight, up_weight, down_weight, vector_rows, up_bias):
    hidden_in = (
        inputs
        + jnp.dot(attn_mixed, proj_weight, preferred_element_type=jnp.float32)
        + vector_rows[4]
    )
    normed = norm_rows(hidden_in, vector_rows[5], vector_rows[6]).astype(jnp.bfloat16)
    pre_act = jnp.dot(normed, up_weight, preferred_element_type=jnp.float32) + up_bias
    activated = gelu_tanh(pre_act).astype(jnp.bfloat16)
    output = (
        hidden_in
        + jnp.dot(activated, down_weight, preferred_element_type=jnp.float32)
        + vector_rows[7]
    )
    return (hidden_in, pre_act, output)


def mlp_back(hidden_in, pre_act, grad_output, up_weight, down_weight, vector_rows):
    grad_branch = grad_output.astype(jnp.bfloat16)
    activated = gelu_tanh(pre_act).astype(jnp.bfloat16)
    grad_down = jnp.dot(activated.T, grad_branch, preferred_element_type=jnp.float32)
    grad_act = jnp.dot(grad_branch, down_weight.T, preferred_element_type=jnp.float32)
    gelu_value, gelu_pull = jax.vjp(gelu_tanh, pre_act)
    grad_pre = gelu_pull(grad_act)[0].astype(jnp.bfloat16)
    normed, norm_pull = jax.vjp(norm_rows, hidden_in, vector_rows[5], vector_rows[6])
    grad_up = jnp.dot(normed.astype(jnp.bfloat16).T, grad_pre, preferred_element_type=jnp.float32)
    grad_normed = jnp.dot(grad_pre, up_weight.T, preferred_element_type=jnp.float32)
    grad_hidden, grad_gain, grad_shift = norm_pull(grad_normed)
    vector_grads = jnp.stack([grad_gain, grad_shift, jnp.sum(grad_branch.astype(jnp.float32), 0)])
    return (
        grad_output + grad_hidden,
        grad_up,
        grad_down,
        jnp.sum(grad_pre.astype(jnp.float32), 0),
        vector_grads,
    )


def proj_back(grad_hidden, attn_mixed, proj_weight):
    grad_branch = grad_hidden.astype(jnp.bfloat16)
    grad_proj = jnp.dot(attn_mixed.T, grad_branch, preferred_element_type=jnp.float32)
    grad_mixed = jnp.dot(grad_branch, proj_weight.T, preferred_element_type=jnp.float32).astype(
        jnp.bfloat16
    )
    return (grad_proj, jnp.sum(grad_branch.astype(jnp.float32), 0), grad_mixed)


def score_back(queries, key_rows, values, grad_mixed, log_total, query_pos, key_pos, length):
    scores = masked_scores(queries, key_rows, query_pos, key_pos, length)
    soft_probs = jnp.exp(scores - log_total)
    grad_probs = jnp.einsum(
        "qhd,khd->hqk",
        split_heads(grad_mixed),
        split_heads(values),
        preferred_element_type=jnp.float32,
    )
    inner = jnp.sum(soft_probs * grad_probs, -1, keepdims=True)
    grad_scores = (soft_probs * (grad_probs - inner)).astype(jnp.bfloat16)
    grad_query = HEAD ** (-0.5) * jnp.einsum(
        "hqk,khd->qhd", grad_scores, split_heads(key_rows), preferred_element_type=jnp.float32
    )
    return (grad_scores, soft_probs.astype(jnp.bfloat16), grad_query.reshape(queries.shape), inner)


def input_back(inputs, grad_hidden, grad_query, key_grads, qkv_weight, vector_rows):
    model_width = inputs.shape[1]
    grad_qkv = jnp.concatenate(
        [
            grad_query.astype(jnp.bfloat16),
            key_grads[:, :model_width].astype(jnp.bfloat16),
            key_grads[:, model_width:].astype(jnp.bfloat16),
        ],
        1,
    )
    normed, norm_pull = jax.vjp(norm_rows, inputs, vector_rows[0], vector_rows[1])
    grad_weight = jnp.dot(
        normed.astype(jnp.bfloat16).T, grad_qkv, preferred_element_type=jnp.float32
    )
    grad_normed = jnp.dot(grad_qkv, qkv_weight.T, preferred_element_type=jnp.float32)
    grad_in, grad_gain, grad_shift = norm_pull(grad_normed)
    column_sums = jnp.sum(grad_qkv.astype(jnp.float32), 0)
    vector_grads = jnp.stack(
        [grad_gain, grad_shift, column_sums[:model_width], column_sums[2 * model_width :]]
    )
    return (grad_hidden + grad_in, grad_weight, vector_grads)


def body(
    block_input, out_grad, w_qkv, w_proj, w_up, w_down, vectors, b_up, seq_lengths, slot_of_seq
):
    section_index = lax.axis_index("pipe")
    replica = lax.axis_index("rep")
    member = lax.axis_index("group")
    rep_count = lax.axis_size("rep")
    row_count = block_input.shape[2]
    micro_count = block_input.shape[0]
    slot_rows = row_count * lax.axis_size("group")
    seq_count = seq_lengths.shape[0]
    slot_ids = jnp.arange(seq_count, dtype=jnp.int32)
    slot_len = jnp.sum(
        seq_lengths[:, None] * (slot_of_seq[:, None] == slot_ids[None, :]).astype(jnp.int32), axis=0
    )
    query_pos = member * row_count + jnp.arange(row_count, dtype=jnp.int32)
    key_pos = jnp.arange(slot_rows, dtype=jnp.int32)
    attn_full = (
        lax.all_gather(w_qkv, "group", axis=1, tiled=True),
        lax.all_gather(w_proj, "group", axis=1, tiled=True),
        lax.all_gather(vectors, "group", axis=2, tiled=True),
    )
    qkv_weight = attn_full[0][0]
    proj_weight = attn_full[1][0]
    vector_rows = attn_full[2][0].astype(jnp.float32)
    mlp_full = (
        lax.all_gather(w_up, "group", axis=1, tiled=True),
        lax.all_gather(w_down, "group", axis=1, tiled=True),
        lax.all_gather(b_up, "group", axis=1, tiled=True),
    )
    up_weight = mlp_full[0][0]
    down_weight = mlp_full[1][0]
    up_bias = mlp_full[2][0].astype(jnp.float32)
    model_width = qkv_weight.shape[0]

    def length_of(micro_index):
        slot_index = jnp.clip(micro_index, 0, micro_count - 1) * rep_count + replica
        return jnp.sum(slot_len * (slot_ids == slot_index).astype(jnp.int32))

    received = jnp.zeros((row_count, model_width), jnp.bfloat16)
    saved = []
    produced = []
    for tick_index in range(micro_count + 1):
        micro_index = tick_index - section_index
        active = (micro_index >= 0) & (micro_index < micro_count)
        length = length_of(micro_index)
        first_in = block_input[min(tick_index, micro_count - 1), 0].astype(jnp.float32)
        inputs = jnp.where(section_index == 0, first_in, received.astype(jnp.float32))

        def project_step(operand, totals):
            normed = norm_rows(operand, vector_rows[0], vector_rows[1]).astype(jnp.bfloat16)
            qkv_bias = jnp.concatenate(
                [vector_rows[2], jnp.zeros_like(vector_rows[2]), vector_rows[3]]
            )
            return (
                totals,
                (jnp.dot(normed, qkv_weight, preferred_element_type=jnp.float32) + qkv_bias).astype(
                    jnp.bfloat16
                ),
            )

        qkv_rows = run_active(active, project_step, inputs, ())[1]
        gathered = (
            lax.all_gather(qkv_rows[:, model_width : 2 * model_width], "group", axis=0, tiled=True),
            lax.all_gather(qkv_rows[:, 2 * model_width :], "group", axis=0, tiled=True),
        )

        def attend_step(operand, totals):
            return (totals, attend(operand[0], operand[1], operand[2], query_pos, key_pos, length))

        attn_mixed, log_total = run_active(
            active, attend_step, (qkv_rows[:, :model_width], gathered[0], gathered[1]), ()
        )[1]

        def finish_step(operand, totals):
            return (
                totals,
                finish(
                    operand[0],
                    operand[1],
                    proj_weight,
                    up_weight,
                    down_weight,
                    vector_rows,
                    up_bias,
                ),
            )

        hidden_in, pre_act, output = run_active(active, finish_step, (inputs, attn_mixed), ())[1]
        received = from_behind(output.astype(jnp.bfloat16), "pipe", 1)
        saved.append((inputs, qkv_rows, log_total, attn_mixed, hidden_in, pre_act, gathered))
        produced.append(output)
    input_totals = (
        jnp.zeros(qkv_weight.shape, jnp.float32),
        jnp.zeros((4, model_width), jnp.float32),
    )
    proj_totals = (
        jnp.zeros(proj_weight.shape, jnp.float32),
        jnp.zeros((model_width,), jnp.float32),
    )
    mlp_totals = (
        jnp.zeros(up_weight.shape, jnp.float32),
        jnp.zeros(down_weight.shape, jnp.float32),
        jnp.zeros(up_bias.shape, jnp.float32),
        jnp.zeros((3, model_width), jnp.float32),
    )
    back_received = jnp.zeros((row_count, model_width), jnp.bfloat16)
    grad_inputs = []
    for back_index in range(micro_count + 1):
        tick_index = micro_count - back_index
        micro_index = tick_index - section_index
        active = (micro_index >= 0) & (micro_index < micro_count)
        length = length_of(micro_index)
        inputs, qkv_rows, log_total, attn_mixed, hidden_in, pre_act, gathered = saved[tick_index]
        valid = (query_pos < length).astype(jnp.float32)[:, None]
        last_grad = out_grad[max(tick_index - 1, 0), 0].astype(jnp.float32) * valid
        grad_output = jnp.where(section_index == 1, last_grad, back_received.astype(jnp.float32))

        def mlp_step(operand, totals):
            grad_hidden, grad_up, grad_down, grad_upbias, vector_grads = mlp_back(
                operand[0], operand[1], operand[2], up_weight, down_weight, vector_rows
            )
            return (
                (
                    totals[0] + grad_up,
                    totals[1] + grad_down,
                    totals[2] + grad_upbias,
                    totals[3] + vector_grads,
                ),
                grad_hidden,
            )

        mlp_totals, grad_hidden = run_active(
            active, mlp_step, (hidden_in, pre_act, grad_output), mlp_totals
        )
        if back_index == micro_count:
            mlp_shards = (
                lax.psum_scatter(mlp_totals[0], ("group", "rep"), scatter_dimension=0, tiled=True),
                lax.psum_scatter(mlp_totals[1], ("group", "rep"), scatter_dimension=0, tiled=True),
                lax.psum_scatter(mlp_totals[2], ("group", "rep"), scatter_dimension=0, tiled=True),
            )

        def proj_step(operand, totals):
            grad_proj, grad_bias, grad_mixed = proj_back(operand[0], operand[1], proj_weight)
            return ((totals[0] + grad_proj, totals[1] + grad_bias), grad_mixed)

        proj_totals, grad_mixed = run_active(
            active, proj_step, (grad_hidden, attn_mixed), proj_totals
        )
        key_rows, value_rows = (
            lax.all_gather(qkv_rows[:, model_width : 2 * model_width], "group", axis=0, tiled=True),
            lax.all_gather(qkv_rows[:, 2 * model_width :], "group", axis=0, tiled=True),
        )

        def score_step(operand, totals):
            return (
                totals,
                score_back(
                    operand[0],
                    operand[1],
                    operand[2],
                    operand[3],
                    operand[4],
                    query_pos,
                    key_pos,
                    length,
                ),
            )

        grad_scores, attn_probs, grad_query, inner = run_active(
            active,
            score_step,
            (qkv_rows[:, :model_width], key_rows, value_rows, grad_mixed, log_total),
            (),
        )[1]
        query_heads = split_heads(qkv_rows[:, :model_width])
        grad_heads = split_heads(grad_mixed)
        grad_key = HEAD ** (-0.5) * jnp.einsum(
            "hqk,qhd->khd", grad_scores, query_heads, preferred_element_type=jnp.float32
        )
        grad_value = jnp.einsum(
            "hqk,qhd->khd", attn_probs, grad_heads, preferred_element_type=jnp.float32
        )
        key_grads = lax.psum_scatter(
            jnp.concatenate(
                [
                    grad_key.reshape(row_count * lax.axis_size("group"), -1),
                    grad_value.reshape(row_count * lax.axis_size("group"), -1),
                ],
                1,
            ).astype(jnp.bfloat16),
            "group",
            scatter_dimension=0,
            tiled=True,
        ).astype(jnp.float32)

        def input_step(operand, totals):
            grad_in, grad_weight, vector_grads = input_back(
                operand[0], operand[1], operand[2], operand[3], qkv_weight, vector_rows
            )
            return ((totals[0] + grad_weight, totals[1] + vector_grads), grad_in)

        input_totals, grad_in = run_active(
            active, input_step, (inputs, grad_hidden, grad_query, key_grads), input_totals
        )
        back_received = from_behind(grad_in.astype(jnp.bfloat16), "pipe", -1)
        grad_inputs.append(grad_in)
    vector_total = jnp.concatenate([input_totals[1], proj_totals[1][None], mlp_totals[3]], 0)
    attn_shards = (
        lax.psum_scatter(input_totals[0], ("group", "rep"), scatter_dimension=0, tiled=True),
        lax.psum_scatter(proj_totals[0], ("group", "rep"), scatter_dimension=0, tiled=True),
        lax.psum_scatter(vector_total, ("group", "rep"), scatter_dimension=1, tiled=True),
    )
    final = (
        lax.all_gather(attn_shards[0].astype(jnp.bfloat16), "rep", axis=0, tiled=True).astype(
            jnp.float32
        ),
        lax.all_gather(attn_shards[1].astype(jnp.bfloat16), "rep", axis=0, tiled=True).astype(
            jnp.float32
        ),
        lax.all_gather(attn_shards[2].astype(jnp.bfloat16), "rep", axis=1, tiled=True).astype(
            jnp.float32
        ),
        lax.all_gather(mlp_shards[0].astype(jnp.bfloat16), "rep", axis=0, tiled=True).astype(
            jnp.float32
        ),
        lax.all_gather(mlp_shards[1].astype(jnp.bfloat16), "rep", axis=0, tiled=True).astype(
            jnp.float32
        ),
        lax.all_gather(mlp_shards[2].astype(jnp.bfloat16), "rep", axis=0, tiled=True).astype(
            jnp.float32
        ),
    )
    grad_stack = jnp.stack(
        [grad_inputs[micro_count - micro_slot] for micro_slot in range(micro_count)]
    )
    output_stack = jnp.stack([produced[micro_slot + 1] for micro_slot in range(micro_count)])
    section_edges = jnp.where(section_index == 0, grad_stack, output_stack)[None, :, None]
    return (
        section_edges,
        final[0][None],
        final[1][None],
        final[3][None],
        final[4][None],
        final[2][None],
        final[5][None],
    )


def solution(mesh):
    in_specs = (
        P(None, "rep", "group", None),
        P(None, "rep", "group", None),
        P("pipe", "group", None),
        P("pipe", "group", None),
        P("pipe", "group", None),
        P("pipe", "group", None),
        P("pipe", None, "group"),
        P("pipe", "group"),
        P(),
        P(),
    )
    out_specs = (
        P("pipe", None, "rep", "group", None),
        P("pipe", "group", None),
        P("pipe", "group", None),
        P("pipe", "group", None),
        P("pipe", "group", None),
        P("pipe", None, "group"),
        P("pipe", "group"),
    )
    return jax.shard_map(body, mesh=mesh, in_specs=in_specs, out_specs=out_specs, check_vma=False)
```

profile of v0, /device:TPU:1, one launch (start us, length us, event | category | flops | bytes accessed | tf_op | source)
XLA Modules:
  0.0 2449.1 jit_solution(16908047018885956435)
XLA Ops:
  8.8 29.4 %all_gather.61 = bf16[1,8,1088]{1,0,2:T(2,128)(2,1)S(1)} all-gather(bf16[1,8,136]{1,0,2:T(2,128)(2,1)S(1)} %copy.31), channel_id=1, replica_groups=mesh['pipe'=2,'group'=8,'rep'=8] {'group'}, dimensions={2}, use_global_device_ids=true | all-gather | bytes 19584 | tf_op jit(solution)/shard_map/all_gather | solution.py:174
  38.8 27.6 %slice_reduce_fusion = (f32[1088]{0:T(1024)S(1)}, f32[1088]{0:T(1024)S(1)}, f32[1088]{0:T(1024)S(1)}, f32[1088]{0:T(1024)S(1)}, f32[1088]{0:T(1024)S(1)}, /*inde...) fusion(f32[1,8,1088]{1,0,2:T(1,128)S(1)} %convert_element_type.352), kind=kLoop, calls=%fused_computation.290 | loop fusion | bytes 69632 | tf_op jit(solution)/shard_map/slice | solution.py:79
  66.8 98.9 %all-gather.20.cloned.1.call-done = bf16[1,1088,3264]{2,1,0:T(8,128)(2,1)} async-done(((bf16[1,136,3264]{2,1,0:T(8,128)(2,1)}), bf16[1,1088,3264]{2,1,0:T(8,128)(2,1)}) %all-gather.20.cloned.1.call-update) | async-done | bytes 7102480 | tf_op jit(solution)/shard_map/all_gather | solution.py:172
  165.7 6.4 fusion.70
  177.2 28.0 %all-reduce = bf16[4352]{0:T(1024)(128)(2,1)S(1)} all-reduce(bf16[4352]{0:T(1024)(128)(2,1)S(1)} %dynamic-update-slice), channel_id=1, replica_groups=mesh['pipe'=2,'group'=8,'rep'=8] {'group'}, use_global_device_ids=true, to_apply=%add | all-reduce | flops 4352 | bytes 17408
  208.2 19.5 all-gather.24.cloned.1.call-done
  235.1 49.6 %all-gather.22.cloned.1.call-done = bf16[1024,1088]{0,1:T(8,128)(2,1)} async-done(((bf16[128,1088]{0,1:T(8,128)(2,1)}), bf16[1024,1088]{0,1:T(8,128)(2,1)}) %all-gather.22.cloned.1.call-update) | async-done | bytes 2228240 | tf_op jit(solution)/shard_map/all_gather | solution.py:218
  284.6 6.0 fusion.286
  290.6 56.8 %all-gather.26.cloned.1.call-done = bf16[1,1088,1088]{2,1,0:T(8,128)(2,1)} async-done(((bf16[1,136,1088]{2,1,0:T(8,128)(2,1)}), bf16[1,1088,1088]{2,1,0:T(8,128)(2,1)}) %all-gather.26.cloned.1.call-update) | async-done | bytes 2367504 | tf_op jit(solution)/shard_map/all_gather | solution.py:173
  351.0 185.9 %all-gather.28.cloned.1.call-done = bf16[1,1088,4352]{2,1,0:T(8,128)(2,1)} async-done(((bf16[1,136,4352]{2,1,0:T(8,128)(2,1)}), bf16[1,1088,4352]{2,1,0:T(8,128)(2,1)}) %all-gather.28.cloned.1.call-update) | async-done | bytes 9469968 | tf_op jit(solution)/shard_map/all_gather | solution.py:180
  537.0 6.8 fusion.43
  543.8 194.8 %all-gather.18.cloned.1.call-done = bf16[1,4352,1088]{2,1,0:T(8,128)(2,1)} async-done(((bf16[1,544,1088]{2,1,0:T(8,128)(2,1)}), bf16[1,4352,1088]{2,1,0:T(8,128)(2,1)}) %all-gather.18.cloned.1.call-update) | async-done | bytes 9469968 | tf_op jit(solution)/shard_map/all_gather | solution.py:181
  738.6 8.1 fusion.151
  746.7 15.4 collective-permute-start
  762.1 5.2 collective-permute-done
  767.7 6.5 fusion.73
  775.9 55.2 %all-gather.32.cloned.1.call-done = bf16[1024,1088]{0,1:T(8,128)(2,1)} async-done(((bf16[128,1088]{0,1:T(8,128)(2,1)}), bf16[1024,1088]{0,1:T(8,128)(2,1)}) %all-gather.32.cloned.1.call-update) | async-done | bytes 2228240 | tf_op jit(solution)/shard_map/all_gather | solution.py:217
  838.0 49.4 %all-gather.30.cloned.1.call-done = bf16[1024,1088]{0,1:T(8,128)(2,1)} async-done(((bf16[128,1088]{0,1:T(8,128)(2,1)}), bf16[1024,1088]{0,1:T(8,128)(2,1)}) %all-gather.30.cloned.1.call-update) | async-done | bytes 2228240 | tf_op jit(solution)/shard_map/all_gather | solution.py:218
  887.4 6.1 fusion.287
  894.9 5.7 fusion.46
  900.6 4.8 fusion.451
  914.0 6.5 fusion.76
  922.6 55.4 %all-gather.36.cloned.1.call-done = bf16[1024,1088]{0,1:T(8,128)(2,1)} async-done(((bf16[128,1088]{0,1:T(8,128)(2,1)}), bf16[1024,1088]{0,1:T(8,128)(2,1)}) %all-gather.36.cloned.1.call-update) | async-done | bytes 2228240 | tf_op jit(solution)/shard_map/all_gather | solution.py:217
  984.9 49.2 %all-gather.34.cloned.1.call-done = bf16[1024,1088]{0,1:T(8,128)(2,1)} async-done(((bf16[128,1088]{0,1:T(8,128)(2,1)}), bf16[1024,1088]{0,1:T(8,128)(2,1)}) %all-gather.34.cloned.1.call-update) | async-done | bytes 2228240 | tf_op jit(solution)/shard_map/all_gather | solution.py:218
  1034.1 6.1 fusion.288
  1041.7 7.0 fusion.49
  1048.7 8.7 convert_reduce_fusion.2
  1076.0 6.6 copy.36
  1082.6 5.3 fusion.247
  1088.0 93.1 %reduce-scatter.16.cloned.1.call-done = bf16[128,2176]{1,0:T(8,128)(2,1)} async-done(((bf16[1024,2176]{1,0:T(8,128)(2,1)}), bf16[128,2176]{1,0:T(8,128)(2,1)}) %reduce-scatter.16.cloned.1.call-update) | async-done | bytes 557072
  1182.4 5.4 multiply_reduce_fusion.15
  1191.3 8.5 collective-permute-done.2
  1200.5 9.4 convert_reduce_fusion.1
  1227.7 6.5 copy.38
  1237.2 9.8 convolution_select_fusion.1
  1247.0 7.9 convolution_select_fusion
  1256.7 73.5 %reduce-scatter.18.cloned.1.call-done = bf16[128,2176]{1,0:T(8,128)(2,1)} async-done(((bf16[1024,2176]{1,0:T(8,128)(2,1)}), bf16[128,2176]{1,0:T(8,128)(2,1)}) %reduce-scatter.18.cloned.1.call-update) | async-done | bytes 557072
  1331.6 6.1 multiply_reduce_fusion.7
  1350.0 8.4 convert_reduce_fusion
  1375.5 6.5 copy.40
  1393.9 12.6 add_select_fusion.3
  1406.5 16.4 add_select_fusion.1
  1426.1 8.8 add_select_fusion.5
  1438.5 12.9 add_select_fusion
  1453.4 12.4 add_select_fusion.2
  1465.8 12.2 reduce-scatter.20.cloned.1.call-done
  1479.7 5.1 multiply_reduce_fusion.9
  1485.0 9.8 add_select_fusion.4
  1495.5 373.3 %all-reduce.13 = (bf16[1088,1088]{1,0:T(8,128)(2,1)}, bf16[4352,1088]{0,1:T(8,128)(2,1)}, bf16[8,1088]{1,0:T(8,128)(2,1)S(1)}, bf16[4352]{0:T(1024)(128)(2,1)S(1)}) all-reduce(f32[1088,1088]{1,0:T(8,128)} %fusion.2, f32[4352,1088]{0,1:T(8,128)} %add_select_fusion, ...), channel_id=6, replica_groups=mesh['pipe'=2,'group'=8,'rep'=8] {'group','rep'}, use_global_device_ids=true, to_apply=%region_47.48.clone | all-reduce | flops 5931776 | bytes 35590656
  1871.0 268.1 %fusion.431 = (f32[24,3264]{1,0:T(8,128)}, f32[24,4352]{1,0:T(8,128)}) fusion(f32[1088,3264]{1,0:T(8,128)} %add_select_fusion.4, f32[1088,4352]{1,0:T(8,128)} %add_select_fusion.2), kind=kCustom, calls=%all-reduce-scatter.2 | all-reduce-scatter fusion | flops 11698177 | bytes 33876480
  2157.6 10.3 collective-permute-start.35
  2178.5 4.8 collective-permute-start.30
  2189.3 8.2 fusion.148
  2200.7 5.2 collective-permute-start.26
  2205.9 4.7 collective-permute-start.25
  2225.7 5.2 collective-permute-start.18
  2232.9 61.0 %concatenate.55 = bf16[465,4352]{1,0:T(8,128)(2,1)} concatenate(bf16[9,4352]{1,0:T(8,128)(2,1)} %copy-done.97, bf16[24,4352]{1,0:T(8,128)(2,1)} %collective-permute-done.40, bf16[24,4352]{1,0:T(8,128)(2,1)} %collective-permute-done.39, bf16[24,4352]{1,0:T(8,128)(2,1)} %collective-permute-done.38, bf16[24,4352]{1,0:T(8,128)(2,1)} %collective-permute-done.37, ...), dimensions={0} | concatenate | bytes 8303616
  2313.1 9.1 collective-permute-start.10
  2324.4 12.7 all-gather.1
  2338.2 12.1 all-gather.4
  2351.2 12.0 all-reduce.1
  2371.4 5.1 collective-permute-start.6
  2386.1 33.8 %concatenate.54 = bf16[465,3264]{1,0:T(8,128)(2,1)S(1)} concatenate(bf16[9,3264]{1,0:T(8,128)(2,1)} %collective-permute-done.22, bf16[24,3264]{1,0:T(8,128)(2,1)} %collective-permute-done.21, bf16[24,3264]{1,0:T(8,128)(2,1)} %collective-permute-done.20, bf16[24,3264]{1,0:T(8,128)(2,1)} %collective-permute-done.19, bf16[24,3264]{1,0:T(8,128)(2,1)} %collective-permute-done.18, ...), dimensions={0} | concatenate | bytes 6227712
  2420.0 14.8 all-gather
  (669 shorter events, 252.5 us)
Async XLA Ops:
  7.2 158.5 %all-gather.20.cloned.1.call-start = ((), (), s32[]{:S(2)}) async-start(), calls=%async_computation.4 | async-start | bytes 8146944 | tf_op jit(solution)/shard_map/all_gather | solution.py:172
  7.9 219.8 %all-gather.24.cloned.1.call-start = ((), (), s32[]{:S(2)}) async-start(), calls=%async_computation.6 | async-start | bytes 2506752 | tf_op jit(solution)/shard_map/all_gather | solution.py:217
  66.4 834.2 %copy-start.131 = (f32[1088]{0:T(1024)}, f32[1088]{0:T(1024)S(1)}, u32[]{:S(2)}) copy-start(f32[1088]{0:T(1024)S(1)} %get-tuple-element.37) | copy-start | bytes 13060
  66.4 847.6 %copy-start.81 = (f32[1088]{0:T(1024)}, f32[1088]{0:T(1024)S(1)}, u32[]{:S(2)}) copy-start(f32[1088]{0:T(1024)S(1)} %get-tuple-element.43) | copy-start | bytes 13060
  173.1 111.5 %all-gather.22.cloned.1.call-start = ((), (), s32[]{:S(2)}) async-start(), calls=%async_computation.5 | async-start | bytes 2506752 | tf_op jit(solution)/shard_map/all_gather | solution.py:218
  173.8 173.5 %all-gather.26.cloned.1.call-start = ((), (), s32[]{:S(2)}) async-start(), calls=%async_computation.7 | async-start | bytes 2820096 | tf_op jit(solution)/shard_map/all_gather | solution.py:173
  174.4 362.5 %all-gather.28.cloned.1.call-start = ((), (), s32[]{:S(2)}) async-start(), calls=%async_computation.8 | async-start | bytes 10653696 | tf_op jit(solution)/shard_map/all_gather | solution.py:180
  175.0 563.6 %all-gather.18.cloned.1.call-start = ((), (), s32[]{:S(2)}) async-start(), calls=%async_computation.3 | async-start | bytes 11280384 | tf_op jit(solution)/shard_map/all_gather | solution.py:181
  175.6 655.5 %all-gather.32.cloned.1.call-start = ((), (), s32[]{:S(2)}) async-start(), calls=%async_computation.10 | async-start | bytes 2506752 | tf_op jit(solution)/shard_map/all_gather | solution.py:217
  350.3 388.4 %copy-start.7 = (f32[128,1088]{0,1:T(8,128)}, f32[128,1088]{0,1:T(8,128)S(1)}, u32[]{:S(2)}) copy-start(f32[128,1088]{0,1:T(8,128)S(1)} %get-tuple-element.142) | copy-start | bytes 1671172
  746.7 20.7 collective-permute-start
  767.4 570.3 %copy-start.18 = (bf16[128,1088]{0,1:T(8,128)(2,1)}, bf16[128,1088]{0,1:T(8,128)(2,1)S(1)}, u32[]{:S(2)}) copy-start(bf16[128,1088]{0,1:T(8,128)(2,1)S(1)} %collective-permute-done) | copy-start | bytes 835588
  775.1 112.2 %all-gather.30.cloned.1.call-start = ((), (), s32[]{:S(2)}) async-start(), calls=%async_computation.9 | async-start | bytes 2506752 | tf_op jit(solution)/shard_map/all_gather | solution.py:218
  775.9 202.2 %all-gather.36.cloned.1.call-start = ((), (), s32[]{:S(2)}) async-start(), calls=%async_computation.12 | async-start | bytes 2506752 | tf_op jit(solution)/shard_map/all_gather | solution.py:217
  894.7 319.8 %copy-start.5 = (f32[128,1088]{0,1:T(8,128)}, f32[128,1088]{0,1:T(8,128)S(1)}, u32[]{:S(2)}) copy-start(f32[128,1088]{0,1:T(8,128)S(1)} %get-tuple-element.146) | copy-start | bytes 1671172
  905.4 8.2 collective-permute-start.1
  921.3 112.8 %all-gather.34.cloned.1.call-start = ((), (), s32[]{:S(2)}) async-start(), calls=%async_computation.11 | async-start | bytes 2506752 | tf_op jit(solution)/shard_map/all_gather | solution.py:218
  921.9 259.1 %reduce-scatter.16.cloned.1.call-start = ((), (), s32[]{:S(2)}) async-start(), calls=%async_computation.15 | async-start | bytes 5013504
  1082.6 247.6 %reduce-scatter.18.cloned.1.call-start = ((), (), s32[]{:S(2)}) async-start(), calls=%async_computation.16 | async-start | bytes 5013504
  1188.9 10.9 collective-permute-start.2
  1234.3 243.8 %reduce-scatter.20.cloned.1.call-start = ((), (), s32[]{:S(2)}) async-start(), calls=%async_computation.17 | async-start | bytes 5013504
  1338.8 10.8 collective-permute-start.3
  1382.0 1054.4 %all-gather.40.cloned.1.call-start = ((), (), s32[]{:S(2)}) async-start(), calls=%async_computation.14 | async-start | bytes 1492992 | tf_op jit(solution)/shard_map/all_gather | solution.py:380
  1870.9 318.4 %copy-start.11 = (f32[128,1088]{0,1:T(8,128)S(1)}, f32[128,1088]{0,1:T(8,128)}, u32[]{:S(2)}) copy-start(f32[128,1088]{0,1:T(8,128)} %copy-done.10) | copy-start | bytes 1671172
  1870.9 318.4 %copy-start.20 = (f32[128,4352]{1,0:T(8,128)S(1)}, f32[128,4352]{1,0:T(8,128)}, u32[]{:S(2)}) copy-start(f32[128,4352]{1,0:T(8,128)} %fusion.49) | copy-start | bytes 6684676
  1871.0 568.2 %all-gather.38.cloned.1.call-start = ((), (), s32[]{:S(2)}) async-start(), calls=%async_computation.13 | async-start | bytes 1880064 | tf_op jit(solution)/shard_map/all_gather | solution.py:377
  2140.8 16.8 collective-permute-start.40
  2142.8 25.1 %collective-permute-start.39 = (bf16[24,4352]{1,0:T(8,128)(2,1)}, bf16[24,4352]{1,0:T(8,128)(2,1)}, u32[]{:S(2)}, u32[]{:S(2)}) collective-permute-start(bf16[24,4352]{1,0:T(8,128)(2,1)} %convert.197), channel_id=1, source_target_pairs={{0,17},{1,18},{2,19},{3,20},{4,21},{5,22},{6,23},{7,24},{8,25},{9,... | collective-permute-start | bytes 626696
  2144.7 25.1 %collective-permute-start.38 = (bf16[24,4352]{1,0:T(8,128)(2,1)}, bf16[24,4352]{1,0:T(8,128)(2,1)}, u32[]{:S(2)}, u32[]{:S(2)}) collective-permute-start(bf16[24,4352]{1,0:T(8,128)(2,1)} %convert.197), channel_id=1, source_target_pairs={{0,16},{1,17},{2,18},{3,19},{4,20},{5,21},{6,22},{7,23},{8,24},{9,... | collective-permute-start | bytes 626696
  2147.7 7.3 collective-permute-start.41
  2149.0 25.2 %collective-permute-start.37 = (bf16[24,4352]{1,0:T(8,128)(2,1)}, bf16[24,4352]{1,0:T(8,128)(2,1)}, u32[]{:S(2)}, u32[]{:S(2)}) collective-permute-start(bf16[24,4352]{1,0:T(8,128)(2,1)} %convert.197), channel_id=1, source_target_pairs={{0,15},{1,16},{2,17},{3,18},{4,19},{5,20},{6,21},{7,22},{8,23},{9,... | collective-permute-start | bytes 626696
  2155.6 20.8 collective-permute-start.36
  2157.6 20.9 collective-permute-start.35
  2167.9 15.4 collective-permute-start.34
  2169.9 15.0 collective-permute-start.33
  2174.2 24.0 collective-permute-start.32
  2176.4 24.3 collective-permute-start.31
  2178.5 27.4 %collective-permute-start.30 = (bf16[24,4352]{1,0:T(8,128)(2,1)}, bf16[24,4352]{1,0:T(8,128)(2,1)S(1)}, u32[]{:S(2)}, u32[]{:S(2)}) collective-permute-start(bf16[24,4352]{1,0:T(8,128)(2,1)} %convert.197), channel_id=1, source_target_pairs={{0,8},{1,9},{2,10},{3,11},{4,12},{5,13},{6,14},{7,15},{8,16},{9,17... | collective-permute-start | bytes 626696
  2183.3 27.4 %collective-permute-start.29 = (bf16[24,4352]{1,0:T(8,128)(2,1)}, bf16[24,4352]{1,0:T(8,128)(2,1)S(1)}, u32[]{:S(2)}, u32[]{:S(2)}) collective-permute-start(bf16[24,4352]{1,0:T(8,128)(2,1)} %convert.197), channel_id=1, source_target_pairs={{0,7},{1,8},{2,9},{3,10},{4,11},{5,12},{6,13},{7,14},{8,15},{9,16}... | collective-permute-start | bytes 626696
  2184.9 29.2 %collective-permute-start.28 = (bf16[24,4352]{1,0:T(8,128)(2,1)}, bf16[24,4352]{1,0:T(8,128)(2,1)S(1)}, u32[]{:S(2)}, u32[]{:S(2)}) collective-permute-start(bf16[24,4352]{1,0:T(8,128)(2,1)} %convert.197), channel_id=1, source_target_pairs={{0,6},{1,7},{2,8},{3,9},{4,10},{5,11},{6,12},{7,13},{8,14},{9,15},... | collective-permute-start | bytes 626696
  2198.3 18.4 collective-permute-start.27
  2200.7 18.7 collective-permute-start.26
  2205.9 15.5 collective-permute-start.25
  2210.7 15.0 collective-permute-start.24
  2214.1 16.8 collective-permute-start.23
  2216.7 83.5 %collective-permute-start.21 = (bf16[24,3264]{1,0:T(8,128)(2,1)S(1)}, bf16[24,3264]{1,0:T(8,128)(2,1)}, u32[]{:S(2)}, u32[]{:S(2)}) collective-permute-start(bf16[24,3264]{1,0:T(8,128)(2,1)S(1)} %convert.198), channel_id=1, source_target_pairs={{0,18},{1,19},{2,20},{3,21},{4,22},{5,23},{6,24},{7,25},{8,26},{9,... | collective-permute-start | bytes 470024
  2219.4 82.2 %collective-permute-start.20 = (bf16[24,3264]{1,0:T(8,128)(2,1)S(1)}, bf16[24,3264]{1,0:T(8,128)(2,1)}, u32[]{:S(2)}, u32[]{:S(2)}) collective-permute-start(bf16[24,3264]{1,0:T(8,128)(2,1)S(1)} %convert.198), channel_id=1, source_target_pairs={{0,17},{1,18},{2,19},{3,20},{4,21},{5,22},{6,23},{7,24},{8,25},{9,... | collective-permute-start | bytes 470024
  2221.4 83.6 %collective-permute-start.19 = (bf16[24,3264]{1,0:T(8,128)(2,1)S(1)}, bf16[24,3264]{1,0:T(8,128)(2,1)}, u32[]{:S(2)}, u32[]{:S(2)}) collective-permute-start(bf16[24,3264]{1,0:T(8,128)(2,1)S(1)} %convert.198), channel_id=1, source_target_pairs={{0,16},{1,17},{2,18},{3,19},{4,20},{5,21},{6,22},{7,23},{8,24},{9,... | collective-permute-start | bytes 470024
  2225.7 82.1 %collective-permute-start.18 = (bf16[24,3264]{1,0:T(8,128)(2,1)S(1)}, bf16[24,3264]{1,0:T(8,128)(2,1)}, u32[]{:S(2)}, u32[]{:S(2)}) collective-permute-start(bf16[24,3264]{1,0:T(8,128)(2,1)S(1)} %convert.198), channel_id=1, source_target_pairs={{0,15},{1,16},{2,17},{3,18},{4,19},{5,20},{6,21},{7,22},{8,23},{9,... | collective-permute-start | bytes 470024
  2230.9 65.9 %collective-permute-start.22 = (bf16[9,3264]{1,0:T(8,128)(2,1)}, bf16[9,3264]{1,0:T(8,128)(2,1)}, u32[]{:S(2)}, u32[]{:S(2)}) collective-permute-start(bf16[9,3264]{1,0:T(8,128)(2,1)} %slice.196), channel_id=1, source_target_pairs={{0,19},{1,20},{2,21},{3,22},{4,23},{5,24},{6,25},{7,26},{8,27},{9,... | collective-permute-start | bytes 176264
  2296.8 12.3 collective-permute-start.17
  2300.2 11.2 collective-permute-start.16
  2301.6 11.5 collective-permute-start.15
  2305.1 17.1 collective-permute-start.14
  2307.8 56.0 %collective-permute-start.13 = (bf16[24,3264]{1,0:T(8,128)(2,1)S(1)}, bf16[24,3264]{1,0:T(8,128)(2,1)S(1)}, u32[]{:S(2)}, u32[]{:S(2)}) collective-permute-start(bf16[24,3264]{1,0:T(8,128)(2,1)S(1)} %convert.198), channel_id=1, source_target_pairs={{0,10},{1,11},{2,12},{3,13},{4,14},{5,15},{6,16},{7,17},{8,18},{9,... | collective-permute-start | bytes 470024
  2309.1 57.9 %collective-permute-start.12 = (bf16[24,3264]{1,0:T(8,128)(2,1)S(1)}, bf16[24,3264]{1,0:T(8,128)(2,1)S(1)}, u32[]{:S(2)}, u32[]{:S(2)}) collective-permute-start(bf16[24,3264]{1,0:T(8,128)(2,1)S(1)} %convert.198), channel_id=1, source_target_pairs={{0,9},{1,10},{2,11},{3,12},{4,13},{5,14},{6,15},{7,16},{8,17},{9,1... | collective-permute-start | bytes 470024
  2311.5 59.9 %collective-permute-start.11 = (bf16[24,3264]{1,0:T(8,128)(2,1)S(1)}, bf16[24,3264]{1,0:T(8,128)(2,1)S(1)}, u32[]{:S(2)}, u32[]{:S(2)}) collective-permute-start(bf16[24,3264]{1,0:T(8,128)(2,1)S(1)} %convert.198), channel_id=1, source_target_pairs={{0,8},{1,9},{2,10},{3,11},{4,12},{5,13},{6,14},{7,15},{8,16},{9,17... | collective-permute-start | bytes 470024
  2313.1 63.4 %collective-permute-start.10 = (bf16[24,3264]{1,0:T(8,128)(2,1)S(1)}, bf16[24,3264]{1,0:T(8,128)(2,1)S(1)}, u32[]{:S(2)}, u32[]{:S(2)}) collective-permute-start(bf16[24,3264]{1,0:T(8,128)(2,1)S(1)} %convert.198), channel_id=1, source_target_pairs={{0,7},{1,8},{2,9},{3,10},{4,11},{5,12},{6,13},{7,14},{8,15},{9,16}... | collective-permute-start | bytes 470024
  2322.2 56.3 %collective-permute-start.9 = (bf16[24,3264]{1,0:T(8,128)(2,1)S(1)}, bf16[24,3264]{1,0:T(8,128)(2,1)S(1)}, u32[]{:S(2)}, u32[]{:S(2)}) collective-permute-start(bf16[24,3264]{1,0:T(8,128)(2,1)S(1)} %convert.198), channel_id=1, source_target_pairs={{0,6},{1,7},{2,8},{3,9},{4,10},{5,11},{6,12},{7,13},{8,14},{9,15},... | collective-permute-start | bytes 470024
  2363.8 20.9 collective-permute-start.8
  2367.1 17.6 collective-permute-start.7
  2371.4 13.3 collective-permute-start.6
  2376.6 8.2 collective-permute-start.5
  2378.5 7.6 collective-permute-start.4
  (184 other events, 5205.3 us)
Sparse Core Ops, SparseCore 0:
  9.6 156.0 all-gather.19
  173.2 54.3 all-gather.23
  229.8 54.7 all-gather.21
  286.1 61.1 all-gather.25
  348.9 188.0 all-gather.27
  538.5 200.1 all-gather.17
  775.2 55.8 all-gather.31
  833.2 54.0 all-gather.29
  921.4 56.5 all-gather.35
  980.0 54.0 all-gather.33
  1082.7 98.2 reduce-scatter.15
  1234.4 95.7 reduce-scatter.17
  1382.1 95.8 reduce-scatter.19
  1871.0 247.1 all-gather.39
  2295.7 33.5 all-gather.37
where the time goes:
time: 2460 us; the launch traced here: 2450 us
  waiting for transfers between devices  1020 us (41%)
  blocking collectives  750 us (30%)
  matrix products  279 us (11%)
  local copies, waits for them, and re-layouts  191 us (8%)
  starting transfers between devices  144 us (6%)
  other arithmetic  41.7 us (2%)
    unnamed x4, blocking collectives  681 us
    all_gather x1, waiting for transfers between devices, body(): lax.all_gather(w_down, 'group', axis=1, tiled=True)  195 us
    unnamed x56, waiting for transfers between devices  187 us
    all_gather x1, waiting for transfers between devices, body(): lax.all_gather(w_up, 'group', axis=1, tiled=True)  186 us
    all_gather x3, waiting for transfers between devices, body(): lax.all_gather(qkv_rows[:, 2 * model_width:], 'group', axis=0, tiled=True)  148 us
    unnamed x407, local copies, waits for them, and re-layouts  143 us
    all_gather x3, waiting for transfers between devices, body(): lax.all_gather(qkv_rows[:, model_width:2 * model_width], 'group', axis=0,...  130 us
    unnamed x41, starting transfers between devices  120 us
  transfers between devices with their start and end apart: 57, of which 18 were waited for; matrix products, arithmetic and copies ran while one was open for 23% of the time, Pallas kernels for 0%

commit v1 on v0

v1 whole, which is shorter than its diff:
```python
import functools
import jax
import jax.numpy as jnp
from jax import lax
from jax.experimental import pallas as pl
from jax.experimental.pallas import tpu as pltpu
from jax.sharding import PartitionSpec as P

HEAD = 64
LANES = 128
EPSILON = 1e-05
MASKED = -1e30
MESH = pl.DeviceIdType.MESH
RING = 4


def remote(src, dst, send_sem, recv_sem, device):
    return pltpu.make_async_remote_copy(
        src_ref=src,
        dst_ref=dst,
        send_sem=send_sem,
        recv_sem=recv_sem,
        device_id=device,
        device_id_type=MESH,
    )


def greet(devices):
    barrier = pltpu.get_barrier_semaphore()
    for device in devices:
        pl.semaphore_signal(barrier, inc=1, device_id=device, device_id_type=MESH)
    pl.semaphore_wait(barrier, len(devices))


def place():
    member, replica = lax.axis_index("group"), lax.axis_index("rep")
    return (member // 2, member % 2, replica // 2, replica % 2)


def gather_kernel(count, *refs):
    ins, outs = refs[:count], refs[count : 2 * count]
    send, recv, local = refs[2 * count :]
    z, x, y, c = place()
    me = 2 * z + x
    xc = (x + c) % 2
    zp, zm, zo = (z + 1) % RING, (z + 3) % RING, (z + 2) % RING
    base, above, below, across = 2 * z + xc, 2 * zp + xc, 2 * zm + xc, 2 * zo + xc
    to_above = {"group": 2 * zp + x}
    to_below = {"group": 2 * zm + x}
    sibling = {"rep": 2 * y + 1 - c}
    partner = {"group": 2 * z + 1 - x}
    greet([to_above, to_below, sibling, partner])

    def part(array, slot, kind):
        half = ins[array].shape[0] // 2
        ref = outs[array].at[slot]
        if kind == "low":
            return ref.at[pl.ds(0, half)]
        if kind == "high":
            return ref.at[pl.ds(half, ins[array].shape[0] - half)]
        return ref

    def across_x(i):
        return remote(ins[i], part(i, me, ""), send.at[i, 0], recv.at[i, 0], partner)

    def first_up(i):
        src = part(i, base, "")
        return remote(src, part(i, base, ""), send.at[i, 1], recv.at[i, 1], to_above)

    def first_down(i):
        src = part(i, base, "")
        return remote(src, part(i, base, ""), send.at[i, 2], recv.at[i, 2], to_below)

    def second_up(i):
        src = part(i, below, "low")
        return remote(src, src, send.at[i, 3], recv.at[i, 3], to_above)

    def second_down(i):
        src = part(i, above, "high")
        return remote(src, src, send.at[i, 4], recv.at[i, 4], to_below)

    def hand(i, slot, kind, sem):
        src = part(i, slot, kind)
        return remote(src, src, send.at[i, sem], recv.at[i, sem], sibling)

    def own(i):
        return pltpu.make_async_copy(ins[i], part(i, me, ""), local.at[i])

    def own_up(i):
        return remote(ins[i], part(i, me, ""), send.at[i, 1], recv.at[i, 1], to_above)

    def own_down(i):
        return remote(ins[i], part(i, me, ""), send.at[i, 2], recv.at[i, 2], to_below)

    arrays = range(count)

    @pl.when(c == 0)
    def _():
        for i in arrays:
            own_up(i).start()
            own_down(i).start()

    @pl.when(c == 1)
    def _():
        for i in arrays:
            across_x(i).start()

    for i in arrays:
        own(i).start()

    @pl.when(c == 1)
    def _():
        for i in arrays:
            remote(ins[i], part(i, base, ""), send.at[i, 0], recv.at[i, 0], partner).wait_recv()
            first_up(i).start()
            first_down(i).start()
            hand(i, base, "", 5).start()

    for i in arrays:
        remote(ins[i], part(i, below, ""), send.at[i, 1], recv.at[i, 1], to_above).wait_recv()
        second_up(i).start()
        hand(i, below, "", 6).start()
        remote(ins[i], part(i, above, ""), send.at[i, 2], recv.at[i, 2], to_below).wait_recv()
        second_down(i).start()
        hand(i, above, "", 7).start()
    for i in arrays:
        src = part(i, across, "low")
        remote(src, src, send.at[i, 3], recv.at[i, 3], to_above).wait_recv()
        hand(i, across, "low", 8).start()
        src = part(i, across, "high")
        remote(src, src, send.at[i, 4], recv.at[i, 4], to_below).wait_recv()
        hand(i, across, "high", 9).start()

    @pl.when(c == 0)
    def _():
        for i in arrays:
            hand(i, 2 * z + 1 - xc, "", 5).wait_recv()
            own_up(i).wait_send()
            own_down(i).wait_send()

    @pl.when(c == 1)
    def _():
        for i in arrays:
            across_x(i).wait_send()
            first_up(i).wait_send()
            first_down(i).wait_send()
            hand(i, base, "", 5).wait_send()

    for i in arrays:
        hand(i, 2 * zm + 1 - xc, "", 6).wait_recv()
        hand(i, 2 * zp + 1 - xc, "", 7).wait_recv()
        hand(i, 2 * zo + 1 - xc, "low", 8).wait_recv()
        hand(i, 2 * zo + 1 - xc, "high", 9).wait_recv()
        second_up(i).wait_send()
        second_down(i).wait_send()
        hand(i, below, "", 6).wait_send()
        hand(i, above, "", 7).wait_send()
        hand(i, across, "low", 8).wait_send()
        hand(i, across, "high", 9).wait_send()
        own(i).wait()


def gather_weights(shards):
    count = len(shards)
    return pl.pallas_call(
        functools.partial(gather_kernel, count),
        out_shape=[jax.ShapeDtypeStruct((8,) + s.shape, s.dtype) for s in shards],
        in_specs=[pl.BlockSpec(memory_space=pl.ANY)] * count,
        out_specs=[pl.BlockSpec(memory_space=pl.ANY)] * count,
        scratch_shapes=[
            pltpu.SemaphoreType.DMA((count, 10)),
            pltpu.SemaphoreType.DMA((count, 10)),
            pltpu.SemaphoreType.DMA((count,)),
        ],
        compiler_params=pltpu.CompilerParams(collective_id=0, has_side_effects=True),
        name="gather_weights",
    )(*shards)


def piece_rows(blocks):
    starts = [i * blocks // RING for i in range(RING + 1)]
    return max(starts[i + 1] - starts[i] for i in range(RING))


def add_blocks(count, dst, terms):
    def step(b, carry):
        total = dst[b].astype(jnp.float32)
        for term in terms:
            total = total + term[b].astype(jnp.float32)
        dst[b] = total.astype(dst.dtype)
        return carry

    lax.fori_loop(0, count, step, 0)


PER_ARRAY = 9


def sum_kernel(count, *refs):
    ins, outs = refs[:count], refs[count : 2 * count]
    buffers = refs[2 * count : 2 * count + PER_ARRAY * count]
    send, recv, local = refs[2 * count + PER_ARRAY * count :]
    z, x, y, c = place()
    xc = (x + c) % 2
    zp, zm = (z + 1) % RING, (z + 3) % RING
    to_above = {"group": 2 * zp + x}
    to_below = {"group": 2 * zm + x}
    sibling = {"rep": 2 * y + 1 - c}
    partner = {"group": 2 * z + 1 - x, "rep": 2 * y + 1 - c}
    others = [{"rep": 2 * ((y + j) % RING) + c} for j in range(1, RING)]
    greet([to_above, to_below, sibling, partner] + others)

    def parts(i):
        return buffers[PER_ARRAY * i : PER_ARRAY * (i + 1)]

    def swap(i, k):
        own, came = ins[i].at[2 * ((z + k) % RING) + 1 - xc], parts(i)[1].at[k]
        return remote(own, came, send.at[i, k], recv.at[i, k], sibling)

    def load(i, k):
        return pltpu.make_async_copy(
            ins[i].at[2 * ((z + k) % RING) + xc], parts(i)[0].at[k], local.at[i, k]
        )

    def sizes(i):
        blocks = ins[i].shape[1]
        return (blocks, blocks // 2, piece_rows(blocks))

    def far_up(i):
        blocks, half, _ = sizes(i)
        src = parts(i)[0].at[2, pl.ds(0, half)]
        return remote(src, parts(i)[2], send.at[i, 4], recv.at[i, 4], to_above)

    def far_down(i):
        blocks, half, _ = sizes(i)
        src = parts(i)[0].at[2, pl.ds(half, blocks - half)]
        return remote(src, parts(i)[3], send.at[i, 5], recv.at[i, 5], to_below)

    def near_up(i):
        return remote(parts(i)[0].at[1], parts(i)[4], send.at[i, 6], recv.at[i, 6], to_above)

    def near_down(i):
        return remote(parts(i)[0].at[3], parts(i)[5], send.at[i, 7], recv.at[i, 7], to_below)

    def over_x(i):
        return remote(parts(i)[0].at[0], parts(i)[6], send.at[i, 8], recv.at[i, 8], partner)

    def own_piece(i, owner):
        blocks, _, rows = sizes(i)
        return parts(i)[0].at[0, pl.ds((owner * blocks) // RING, rows)]

    def over_y(i, j):
        src = own_piece(i, (y + j) % RING)
        dst = parts(i)[7].at[j - 1]
        return remote(src, dst, send.at[i, 8 + j], recv.at[i, 8 + j], others[j - 1])

    def share_y(i, j, slot):
        dst = outs[i].at[slot]
        return remote(parts(i)[8], dst, send.at[i, 11 + j], recv.at[i, 11 + j], others[j - 1])

    def keep(i):
        return pltpu.make_async_copy(parts(i)[8], outs[i].at[y], local.at[i, 4])

    def hand(i):
        return remote(outs[i], outs[i], send.at[i, 15], recv.at[i, 15], sibling)

    for i in range(count):
        for k in (2, 1, 3, 0):
            swap(i, k).start()
            load(i, k).start()

    def step_cores(i):
        blocks, half, _ = sizes(i)
        total, came = parts(i)[0], parts(i)[1]
        for k in (2, 1, 3, 0):
            load(i, k).wait()
            swap(i, k).wait_recv()
            add_blocks(blocks, total.at[k], [came.at[k]])
            if k == 2:
                far_up(i).start()
                far_down(i).start()

    def step_far(i):
        blocks, half, _ = sizes(i)
        total = parts(i)[0]
        far_up(i).wait_recv()
        add_blocks(half, total.at[1, pl.ds(0, half)], [parts(i)[2]])
        near_up(i).start()
        far_down(i).wait_recv()
        add_blocks(blocks - half, total.at[3, pl.ds(half, blocks - half)], [parts(i)[3]])
        near_down(i).start()

    def step_near(i):
        blocks, half, _ = sizes(i)
        near_up(i).wait_recv()
        near_down(i).wait_recv()
        add_blocks(blocks, parts(i)[0].at[0], [parts(i)[4], parts(i)[5]])

        @pl.when(c == 1)
        def _():
            over_x(i).start()

    def step_x(i):
        blocks, half, _ = sizes(i)

        @pl.when(c == 0)
        def _():
            over_x(i).wait_recv()
            add_blocks(blocks, parts(i)[0].at[0], [parts(i)[6]])
            for j in (2, 1, 3):
                over_y(i, j).start()

    def step_y(i):
        _, _, rows = sizes(i)

        @pl.when(c == 0)
        def _():
            for j in (1, 2, 3):
                over_y(i, j).wait_recv()
            own, came, result = own_piece(i, y), parts(i)[7], parts(i)[8]

            def step(b, carry):
                total = own[b].astype(jnp.float32)
                for j in range(RING - 1):
                    total = total + came[j, b].astype(jnp.float32)
                result[b] = total.astype(result.dtype)
                return carry

            lax.fori_loop(0, rows, step, 0)
            for j in (2, 1, 3):
                share_y(i, j, y).start()
            keep(i).start()

    def step_hand(i):
        @pl.when(c == 0)
        def _():
            keep(i).wait()
            for j in (1, 2, 3):
                share_y(i, j, (y + RING - j) % RING).wait_recv()
            hand(i).start()

    def step_last(i):
        @pl.when(c == 1)
        def _():
            hand(i).wait_recv()

    steps = [step_cores, step_far, step_near, step_x, step_y, step_hand, step_last]
    for tick in range(count + len(steps) - 1):
        for i in range(count):
            at = tick - i
            if 0 <= at < len(steps):
                steps[at](i)
    for i in range(count):
        for k in range(RING):
            swap(i, k).wait_send()
        for copy in (far_up, far_down, near_up, near_down):
            copy(i).wait_send()

        @pl.when(c == 1)
        def _():
            over_x(i).wait_send()

        @pl.when(c == 0)
        def _():
            for j in (1, 2, 3):
                over_y(i, j).wait_send()
                share_y(i, j, y).wait_send()
            hand(i).wait_send()


def sum_gradients(grads):
    count = len(grads)
    scratch = []
    for grad in grads:
        _, blocks, rows, width = grad.shape
        half, piece = blocks // 2, piece_rows(blocks)
        for lead in (
            (RING, blocks),
            (RING, blocks),
            (half,),
            (blocks - half,),
            (blocks,),
            (blocks,),
            (blocks,),
            (RING - 1, piece),
            (piece,),
        ):
            scratch.append(pltpu.VMEM(lead + (rows, width), grad.dtype))
    return pl.pallas_call(
        functools.partial(sum_kernel, count),
        out_shape=[
            jax.ShapeDtypeStruct((RING, piece_rows(g.shape[1])) + g.shape[2:], g.dtype)
            for g in grads
        ],
        in_specs=[pl.BlockSpec(memory_space=pl.ANY)] * count,
        out_specs=[pl.BlockSpec(memory_space=pl.ANY)] * count,
        scratch_shapes=scratch
        + [
            pltpu.SemaphoreType.DMA((count, 16)),
            pltpu.SemaphoreType.DMA((count, 16)),
            pltpu.SemaphoreType.DMA((count, 5)),
        ],
        compiler_params=pltpu.CompilerParams(
            collective_id=1, has_side_effects=True, vmem_limit_bytes=60 * 1024 * 1024
        ),
        name="sum_gradients",
    )(*grads)


def assemble(pieces, blocks):
    starts = [i * blocks // RING for i in range(RING + 1)]
    joined = jnp.concatenate(
        [pieces[i, : starts[i + 1] - starts[i]] for i in range(RING)], 0
    ).astype(jnp.float32)
    return joined.reshape(-1, pieces.shape[-1])


def lane_head(shape):
    return lax.broadcasted_iota(jnp.int32, shape, len(shape) - 1) // HEAD


def one_head(matrix, head):
    return jnp.where(lane_head(matrix.shape) == head, matrix, jnp.zeros_like(matrix))


def over_lanes(left, right):
    return lax.dot_general(left, right, (((1,), (1,)), ((), ())), preferred_element_type=jnp.float32)


def over_rows(left, right):
    return lax.dot_general(left, right, (((0,), (0,)), ((), ())), preferred_element_type=jnp.float32)


def plain(left, right):
    return jnp.dot(left, right, preferred_element_type=jnp.float32)


def soft_columns(key_rows, queries, first_query, length):
    scores = over_lanes(key_rows, queries) * HEAD ** (-0.5)
    key_pos = lax.broadcasted_iota(jnp.int32, scores.shape, 0)
    query_pos = first_query + lax.broadcasted_iota(jnp.int32, scores.shape, 1)
    scores = jnp.where((key_pos <= query_pos) & (key_pos < length), scores, MASKED)
    exponent = jnp.exp(scores - jnp.max(scores, 0, keepdims=True))
    return exponent * (1.0 / jnp.sum(exponent, 0, keepdims=True))


def peers(count):
    member = lax.axis_index("group")
    ahead = [(member + j) % count for j in range(1, count)]
    behind = [(member + count - j) % count for j in range(1, count)]
    return (member, ahead, behind)


def attend_kernel(
    lengths, pack, last_kv, last_q, mixed, last_mixed, kept, kept_last,
    held, held_last, staged, send, recv, send_last, recv_last, send_back, recv_back, local,
):
    count, micros, _, rows, lanes = pack.shape
    member, ahead, behind = peers(count)
    greet([{"group": peer} for peer in ahead])

    def out(m, j):
        return remote(
            pack.at[ahead[j], m], held.at[member, m], send.at[m, j], recv.at[m, j], {"group": ahead[j]}
        )

    def out_last(m, j):
        return remote(
            last_kv.at[m],
            held_last.at[member, m],
            send_last.at[m, j],
            recv_last.at[m, j],
            {"group": ahead[j]},
        )

    def back(m, j):
        return remote(
            staged.at[ahead[j], m],
            mixed.at[member, m],
            send_back.at[m, j],
            recv_back.at[m, j],
            {"group": ahead[j]},
        )

    def own(m):
        return (
            pltpu.make_async_copy(pack.at[member, m], held.at[member, m], local.at[m, 0]),
            pltpu.make_async_copy(last_kv.at[m], held_last.at[member, m], local.at[m, 1]),
        )

    def own_back(m):
        return pltpu.make_async_copy(staged.at[member, m], mixed.at[member, m], local.at[m, 2])

    def keep():
        return (
            pltpu.make_async_copy(held, kept, local.at[0, 3]),
            pltpu.make_async_copy(held_last, kept_last, local.at[1, 3]),
        )

    peer_range = range(count - 1)
    for m in range(micros):
        for j in peer_range:
            out(m, j).start()
            out_last(m, j).start()
        for copy in own(m):
            copy.start()

    def micro(m, carry):
        for copy in own(m):
            copy.wait()
        for j in peer_range:
            out(m, j).wait_recv()
            out_last(m, j).wait_recv()
        length = lengths[m]
        wide = 2
        for block in range(count // wide):
            reach = wide * (block + 1)
            queries = held[wide * block : reach, m, 0].reshape(wide * rows, lanes)
            key_rows = held[0:reach, m, 1].reshape(reach * rows, lanes)
            values = held[0:reach, m, 2].reshape(reach * rows, lanes)

            def head_step(head, total):
                probs = soft_columns(
                    key_rows, one_head(queries, head), wide * block * rows, length
                ).astype(jnp.bfloat16)
                return total + over_rows(one_head(values, head), probs)

            total = lax.fori_loop(0, 2, head_step, jnp.zeros((lanes, wide * rows), jnp.float32))
            staged[wide * block : reach, m] = (
                total.T.astype(jnp.bfloat16).reshape(wide, rows, lanes)
            )
        for j in peer_range:
            back(m, j).start()
        own_back(m).start()
        both = held_last[:, m].reshape(count * rows, lanes)
        probs = soft_columns(both, last_q[m], member * rows, length).astype(jnp.bfloat16)
        last_mixed[m] = over_rows(both, probs).T.astype(jnp.bfloat16)
        return carry

    lax.fori_loop(0, micros, micro, 0)
    for copy in keep():
        copy.start()
    for m in range(micros):
        own_back(m).wait()
        for j in peer_range:
            out(m, j).wait_send()
            out_last(m, j).wait_send()
            back(m, j).wait()
    for copy in keep():
        copy.wait()


def attend(lengths, pack, last_kv, last_q):
    count, micros, _, rows, lanes = pack.shape
    bf16 = jnp.bfloat16
    vmem, hbm = pl.BlockSpec(memory_space=pltpu.VMEM), pl.BlockSpec(memory_space=pl.ANY)
    dma = pltpu.SemaphoreType.DMA
    return pl.pallas_call(
        attend_kernel,
        out_shape=[
            jax.ShapeDtypeStruct((count, micros, rows, lanes), bf16),
            jax.ShapeDtypeStruct((micros, rows, lanes), bf16),
            jax.ShapeDtypeStruct(pack.shape, bf16),
            jax.ShapeDtypeStruct((count, micros, rows, lanes), bf16),
        ],
        in_specs=[pl.BlockSpec(memory_space=pltpu.SMEM), hbm, vmem, vmem],
        out_specs=[hbm, vmem, hbm, hbm],
        scratch_shapes=[
            pltpu.VMEM(pack.shape, bf16),
            pltpu.VMEM((count, micros, rows, lanes), bf16),
            pltpu.VMEM((count, micros, rows, lanes), bf16),
        ]
        + [dma((micros, count - 1))] * 6
        + [dma((micros, 4))],
        compiler_params=pltpu.CompilerParams(
            collective_id=2, has_side_effects=True, vmem_limit_bytes=48 * 1024 * 1024
        ),
        name="attend",
    )(lengths, pack, last_kv, last_q)


def attend_back_kernel(
    lengths, held, held_last, last_q, grad_pack, last_grad, grads, last_key_grad, last_query_grad,
    came, staged, staged_last, parts_last, key_total, value_total,
    send, recv, send_back, recv_back, send_last, recv_last, local,
):
    count, micros, _, rows, lanes = held.shape
    member, ahead, behind = peers(count)
    greet([{"group": peer} for peer in ahead])
    scale = HEAD ** (-0.5)

    def out(m, j):
        return remote(
            grad_pack.at[ahead[j], m],
            came.at[member, m],
            send.at[m, j],
            recv.at[m, j],
            {"group": ahead[j]},
        )

    def back(m, j):
        return remote(
            staged.at[ahead[j], m],
            grads.at[member, m],
            send_back.at[m, j],
            recv_back.at[m, j],
            {"group": ahead[j]},
        )

    def back_last(m, j):
        return remote(
            staged_last.at[ahead[j], m],
            parts_last.at[member, m],
            send_last.at[m, j],
            recv_last.at[m, j],
            {"group": ahead[j]},
        )

    def own(m):
        return pltpu.make_async_copy(grad_pack.at[member, m], came.at[member, m], local.at[m, 0])

    def own_back(m):
        return (
            pltpu.make_async_copy(staged.at[member, m], grads.at[member, m], local.at[m, 1]),
            pltpu.make_async_copy(
                staged_last.at[member, m], parts_last.at[member, m], local.at[m, 2]
            ),
        )

    peer_range = range(count - 1)
    for m in range(micros):
        for j in peer_range:
            out(m, j).start()
        own(m).start()

    def micro(m, carry):
        length = lengths[m]
        both = held_last[:, m].reshape(count * rows, lanes)
        probs = soft_columns(both, last_q[m], member * rows, length)
        grad_probs = over_lanes(both, last_grad[m])
        inner = jnp.sum(probs * grad_probs, 0, keepdims=True)
        grad_scores = (probs * (grad_probs - inner)).astype(jnp.bfloat16)
        last_query_grad[m] = (scale * over_rows(both, grad_scores)).T.astype(jnp.bfloat16)
        both_grad = scale * plain(grad_scores, last_q[m]) + plain(
            probs.astype(jnp.bfloat16), last_grad[m]
        )
        staged_last[:, m] = both_grad.astype(jnp.bfloat16).reshape(count, rows, lanes)
        for j in peer_range:
            back_last(m, j).start()
        own(m).wait()
        for j in peer_range:
            out(m, j).wait_recv()
        key_total[...] = jnp.zeros_like(key_total)
        value_total[...] = jnp.zeros_like(value_total)
        wide = 2
        for block in range(count // wide):
            reach = wide * (block + 1)
            queries = held[wide * block : reach, m, 0].reshape(wide * rows, lanes)
            grad_out = came[wide * block : reach, m].reshape(wide * rows, lanes)
            key_rows = held[0:reach, m, 1].reshape(reach * rows, lanes)
            values = held[0:reach, m, 2].reshape(reach * rows, lanes)

            def head_step(head, total):
                head_queries, head_grad = one_head(queries, head), one_head(grad_out, head)
                probs = soft_columns(key_rows, head_queries, wide * block * rows, length)
                grad_probs = over_lanes(values, head_grad)
                inner = jnp.sum(probs * grad_probs, 0, keepdims=True)
                grad_scores = (probs * (grad_probs - inner)).astype(jnp.bfloat16)
                value_total[0 : reach * rows] += plain(probs.astype(jnp.bfloat16), head_grad)
                key_total[0 : reach * rows] += plain(grad_scores, head_queries)
                return total + over_rows(one_head(key_rows, head), grad_scores)

            total = lax.fori_loop(0, 2, head_step, jnp.zeros((lanes, wide * rows), jnp.float32))
            staged[wide * block : reach, m, 0] = (
                (scale * total).T.astype(jnp.bfloat16).reshape(wide, rows, lanes)
            )
        staged[:, m, 1] = (scale * key_total[...]).astype(jnp.bfloat16).reshape(count, rows, lanes)
        staged[:, m, 2] = value_total[...].astype(jnp.bfloat16).reshape(count, rows, lanes)
        for j in peer_range:
            back(m, j).start()
        for copy in own_back(m):
            copy.start()
        return carry

    lax.fori_loop(0, micros, micro, 0)
    for m in range(micros):
        for copy in own_back(m):
            copy.wait()
        for j in peer_range:
            back_last(m, j).wait_recv()
        last_key_grad[m] = jnp.sum(parts_last[:, m].astype(jnp.float32), 0).astype(jnp.bfloat16)
    for m in range(micros):
        for j in peer_range:
            out(m, j).wait_send()
            back_last(m, j).wait_send()
            back(m, j).wait()


def attend_back(lengths, held, held_last, last_q, grad_pack, last_grad):
    count, micros, _, rows, lanes = held.shape
    bf16 = jnp.bfloat16
    vmem, hbm = pl.BlockSpec(memory_space=pltpu.VMEM), pl.BlockSpec(memory_space=pl.ANY)
    dma = pltpu.SemaphoreType.DMA
    return pl.pallas_call(
        attend_back_kernel,
        out_shape=[
            jax.ShapeDtypeStruct(held.shape, bf16),
            jax.ShapeDtypeStruct((micros, rows, lanes), bf16),
            jax.ShapeDtypeStruct((micros, rows, lanes), bf16),
        ],
        in_specs=[pl.BlockSpec(memory_space=pltpu.SMEM), vmem, vmem, vmem, hbm, vmem],
        out_specs=[hbm, vmem, vmem],
        scratch_shapes=[
            pltpu.VMEM((count, micros, rows, lanes), bf16),
            pltpu.VMEM(held.shape, bf16),
            pltpu.VMEM((count, micros, rows, lanes), bf16),
            pltpu.VMEM((count, micros, rows, lanes), bf16),
            pltpu.VMEM((count * rows, lanes), jnp.float32),
            pltpu.VMEM((count * rows, lanes), jnp.float32),
        ]
        + [dma((micros, count - 1))] * 6
        + [dma((micros, 3))],
        compiler_params=pltpu.CompilerParams(
            collective_id=3, has_side_effects=True, vmem_limit_bytes=48 * 1024 * 1024
        ),
        name="attend_back",
    )(lengths, held, held_last, last_q, grad_pack, last_grad)


def norm_rows(inputs, gain_row, bias_row):
    average = jnp.mean(inputs, -1, keepdims=True)
    centered = inputs - average
    variance = jnp.mean(centered * centered, -1, keepdims=True)
    return centered * lax.rsqrt(variance + EPSILON) * gain_row + bias_row


def gelu_tanh(inputs):
    return jax.nn.gelu(inputs, approximate=True)


def by_heads(matrix, micros, rows, count):
    return matrix.reshape(micros, rows, count, LANES).transpose(2, 0, 1, 3)


def by_rows(blocks):
    count, micros, rows, lanes = blocks.shape
    return blocks.transpose(1, 2, 0, 3).reshape(micros * rows, count * lanes)


def in_blocks(matrix):
    return matrix.reshape(matrix.shape[0] // 8, 8, matrix.shape[1])


def body(
    block_input, out_grad, w_qkv, w_proj, w_up, w_down, vectors, b_up, seq_lengths, slot_of_seq
):
    section = lax.axis_index("pipe")
    replica = lax.axis_index("rep")
    member = lax.axis_index("group")
    rep_count = lax.axis_size("rep")
    count = lax.axis_size("group")
    micros, rows, width = block_input.shape[0], block_input.shape[2], block_input.shape[3]
    wide = count * LANES
    slot_ids = jnp.arange(seq_lengths.shape[0], dtype=jnp.int32)
    slot_len = jnp.sum(
        seq_lengths[:, None] * (slot_of_seq[:, None] == slot_ids[None, :]).astype(jnp.int32), axis=0
    )
    mine = jnp.arange(micros, dtype=jnp.int32) * rep_count + replica
    lengths = jnp.sum(
        slot_len[None, :] * (slot_ids[None, :] == mine[:, None]).astype(jnp.int32), axis=1
    )
    query_pos = member * rows + jnp.arange(rows, dtype=jnp.int32)
    valid = (query_pos[None, :] < lengths[:, None]).astype(jnp.float32)[:, :, None]
    cotangent = (out_grad[:, 0].astype(jnp.float32) * valid).reshape(micros * rows, width)

    bias_rows = b_up.shape[1] // vectors.shape[2]
    small = jnp.concatenate(
        [
            vectors[0],
            b_up[0].reshape(bias_rows, -1),
            jnp.zeros((8 - bias_rows, vectors.shape[2]), vectors.dtype),
        ],
        0,
    )
    full = gather_weights(
        [
            in_blocks(small),
            in_blocks(w_qkv[0]),
            in_blocks(w_proj[0]),
            in_blocks(w_up[0]),
            in_blocks(w_down[0]),
        ]
    )
    vector_rows = full[0][:, 0].transpose(1, 0, 2).reshape(8, width).astype(jnp.float32)
    up_bias = full[0][:, 1, :bias_rows].reshape(-1).astype(jnp.float32)
    qkv_weight, proj_weight, up_weight, down_weight = (
        array.reshape(-1, array.shape[-1]) for array in full[1:]
    )
    qkv_bias = jnp.concatenate([vector_rows[2], jnp.zeros_like(vector_rows[2]), vector_rows[3]])

    def pad_last(matrix, before):
        block = matrix.reshape(micros, rows, HEAD)
        return jnp.pad(block, ((0, 0), (0, 0), (before, LANES - HEAD - before)))

    def forward(inputs):
        normed = norm_rows(inputs, vector_rows[0], vector_rows[1]).astype(jnp.bfloat16)
        qkv = (plain(normed, qkv_weight) + qkv_bias).astype(jnp.bfloat16)
        thirds = [qkv[:, i * width : (i + 1) * width] for i in range(3)]
        pack = jnp.stack([by_heads(t[:, :wide], micros, rows, count) for t in thirds], 2)
        last_kv = jnp.concatenate([thirds[1][:, wide:], thirds[2][:, wide:]], 1).reshape(
            micros, rows, LANES
        )
        last_q = pad_last(thirds[0][:, wide:], 0)
        mixed, last_mixed, held, held_last = attend(lengths, pack, last_kv, last_q)
        attn_mixed = jnp.concatenate(
            [by_rows(mixed), last_mixed[:, :, HEAD:].reshape(micros * rows, HEAD)], 1
        )
        hidden = inputs + plain(attn_mixed, proj_weight) + vector_rows[4]
        normed_two = norm_rows(hidden, vector_rows[5], vector_rows[6]).astype(jnp.bfloat16)
        pre_act = plain(normed_two, up_weight) + up_bias
        activated = gelu_tanh(pre_act).astype(jnp.bfloat16)
        output = hidden + plain(activated, down_weight) + vector_rows[7]
        return (output, (inputs, held, held_last, last_q, attn_mixed, hidden, pre_act, activated))

    def backward(grad_output, saved):
        inputs, held, held_last, last_q, attn_mixed, hidden, pre_act, activated = saved
        grad_two = grad_output.astype(jnp.bfloat16)
        grad_act = plain(grad_two, down_weight.T)
        grad_pre = jax.vjp(gelu_tanh, pre_act)[1](grad_act)[0].astype(jnp.bfloat16)
        normed_two, pull_two = jax.vjp(norm_rows, hidden, vector_rows[5], vector_rows[6])
        from_norm, gain_two, shift_two = pull_two(plain(grad_pre, up_weight.T))
        grad_hidden = grad_output + from_norm
        grad_one = grad_hidden.astype(jnp.bfloat16)
        grad_mixed = plain(grad_one, proj_weight.T).astype(jnp.bfloat16)
        grads, last_key_grad, last_query_grad = attend_back(
            lengths,
            held,
            held_last,
            last_q,
            by_heads(grad_mixed[:, :wide], micros, rows, count),
            pad_last(grad_mixed[:, wide:], HEAD),
        )

        def last(block, first):
            return block[:, :, first : first + HEAD].reshape(micros * rows, HEAD)

        grad_qkv = jnp.concatenate(
            [
                by_rows(grads[:, :, 0]),
                last(last_query_grad, 0),
                by_rows(grads[:, :, 1]),
                last(last_key_grad, 0),
                by_rows(grads[:, :, 2]),
                last(last_key_grad, HEAD),
            ],
            1,
        )
        normed, pull = jax.vjp(norm_rows, inputs, vector_rows[0], vector_rows[1])
        from_norm, gain, shift = pull(plain(grad_qkv, qkv_weight.T))
        grad_in = grad_hidden + from_norm

        def weight_grads():
            def outer(left, right):
                return over_rows(left, right).astype(jnp.bfloat16)

            sums = jnp.sum(grad_qkv.astype(jnp.float32), 0)
            rows_of_vectors = jnp.stack(
                [
                    gain,
                    shift,
                    sums[:width],
                    sums[2 * width :],
                    jnp.sum(grad_one.astype(jnp.float32), 0),
                    gain_two,
                    shift_two,
                    jnp.sum(grad_two.astype(jnp.float32), 0),
                ]
            )
            return (
                outer(normed.astype(jnp.bfloat16), grad_qkv),
                outer(attn_mixed, grad_one),
                outer(normed_two.astype(jnp.bfloat16), grad_pre),
                outer(activated, grad_two),
                rows_of_vectors,
                jnp.sum(grad_pre.astype(jnp.float32), 0),
            )

        return (grad_in, weight_grads)

    first_in = block_input[:, 0].reshape(micros * rows, width).astype(jnp.float32)
    first_out, _ = forward(first_in)
    arrived = lax.ppermute(first_out.astype(jnp.bfloat16), "pipe", [(0, 1)])
    output, saved = forward(jnp.where(section == 0, first_in, arrived.astype(jnp.float32)))
    last_grad, _ = backward(cotangent, saved)
    arrived = lax.ppermute(last_grad.astype(jnp.bfloat16), "pipe", [(1, 0)])
    grad_in, weight_grads = backward(
        jnp.where(section == 1, cotangent, arrived.astype(jnp.float32)), saved
    )
    grad_qkv, grad_proj, grad_up, grad_down, grad_vectors, grad_bias = weight_grads()

    def shards(matrix):
        return matrix.reshape(count, -1, 8, matrix.shape[-1])

    small_grads = jnp.concatenate(
        [
            grad_vectors.reshape(8, count, -1).transpose(1, 0, 2),
            grad_bias.reshape(count, bias_rows, -1),
            jnp.zeros((count, 24 - bias_rows, width // count), jnp.float32),
        ],
        1,
    ).reshape(count, RING, 8, width // count)
    sums = sum_gradients(
        [shards(grad_down), shards(grad_up), shards(grad_qkv), small_grads, shards(grad_proj)]
    )
    totals = [
        assemble(total, grad.shape[0] // count // 8)
        for total, grad in zip(
            (sums[2], sums[4], sums[1], sums[0]), (grad_qkv, grad_proj, grad_up, grad_down)
        )
    ]
    small_total = sums[3].reshape(RING * 8, -1)
    edges = jnp.where(section == 0, grad_in, output).reshape(1, micros, 1, rows, width)
    return (
        edges,
        totals[0][None],
        totals[1][None],
        totals[2][None],
        totals[3][None],
        small_total[None, :8],
        small_total[8 : 8 + bias_rows].reshape(1, -1),
    )


def solution(mesh):
    in_specs = (
        P(None, "rep", "group", None),
        P(None, "rep", "group", None),
        P("pipe", "group", None),
        P("pipe", "group", None),
        P("pipe", "group", None),
        P("pipe", "group", None),
        P("pipe", None, "group"),
        P("pipe", "group"),
        P(),
        P(),
    )
    out_specs = (
        P("pipe", None, "rep", "group", None),
        P("pipe", "group", None),
        P("pipe", "group", None),
        P("pipe", "group", None),
        P("pipe", "group", None),
        P("pipe", None, "group"),
        P("pipe", "group"),
    )
    return jax.shard_map(body, mesh=mesh, in_specs=in_specs, out_specs=out_specs, check_vma=False)
```

time: 2460 us -> 677 us (0.28)
  waiting for transfers between devices: 1020 us -> 17.8 us
  blocking collectives: 750 us -> 0 us
  Pallas kernels: 0 us -> 448 us
  matrix products: 279 us -> 113 us
  starting transfers between devices: 144 us -> 5.61 us
  local copies, waits for them, and re-layouts: 191 us -> 65.4 us
    all_gather x12 -> x0, waiting for transfers between devices: 815 us -> none  [the longest x1 195 us: body(): lax.all_gather(w_down, 'group', axis=1, tiled=True)]
    unnamed x4 -> x0, blocking collectives: 681 us -> none
    pallas_call x0 -> x6, Pallas kernels: none -> 448 us  [the longest x1 169 us: sum_gradients(): pl.pallas_call(functools.partial(sum_kernel, count), out_shape=[jax.Shape...]
    unnamed x56 -> x0, waiting for transfers between devices: 187 us -> none
    dot_general x54 -> x18, matrix products: 279 us -> 113 us  [the longest x14 94.1 us: plain(): return jnp.dot(left, right, preferred_element_type=jnp.float32)]
    unnamed x407 -> x127, local copies, waits for them, and re-layouts: 143 us -> 11 us
    unnamed x41 -> x0, starting transfers between devices: 120 us -> none
    all_gather x4 -> x0, blocking collectives: 69.1 us -> none  [the longest x1 29.4 us: body(): lax.all_gather(vectors, 'group', axis=2, tiled=True)]
  transfers between devices with their start and end apart: 57 -> 2, of which waited for: 18 -> 2; matrix products, arithmetic and copies ran while one was open for 23% -> 1% of each run, Pallas kernels for 0% -> 0%
where the time goes in v1:
time: 677 us; the launch traced here: 671 us
  Pallas kernels  448 us (66%)
  matrix products  113 us (17%)
  local copies, waits for them, and re-layouts  65.4 us (10%)
  other arithmetic  19.7 us (3%)
  waiting for transfers between devices  17.8 us (3%)
    pallas_call x1, Pallas kernels, sum_gradients(): pl.pallas_call(functools.partial(sum_kernel, count), out_shape=[jax.Shape...  169 us
    pallas_call x1, Pallas kernels, gather_weights(): pl.pallas_call(functools.partial(gather_kernel, count), out_shape=[jax.Sh...  129 us
    dot_general x14, matrix products, plain(): return jnp.dot(left, right, preferred_element_type=jnp.float32)  94.1 us
    pallas_call x2, Pallas kernels, attend(): pl.pallas_call(attend_kernel, out_shape=[jax.ShapeDtypeStruct((count, mic...  77.2 us
    pallas_call x2, Pallas kernels, attend_back(): pl.pallas_call(attend_back_kernel, out_shape=[jax.ShapeDtypeStruct(held.s...  73 us
    dot_general x4, matrix products, over_rows(): lax.dot_general(left, right, (((0,), (0,)), ((), ())), preferred_element_...  18.4 us
    ppermute x1, waiting for transfers between devices, body(): arrived = lax.ppermute(last_grad.astype(jnp.bfloat16), 'pipe', [(1, 0)])  15.4 us
    convert_element_type x1, local copies, waits for them, and re-layouts, outer(): return over_rows(left, right).astype(jnp.bfloat16)  14.1 us
  transfers between devices with their start and end apart: 2, of which 2 were waited for; matrix products, arithmetic and copies ran while one was open for 1% of the time, Pallas kernels for 0%

profile of v1, /device:TPU:1, one launch (start us, length us, event | category | flops | bytes accessed | tf_op | source)
XLA Modules:
  0.0 671.5 jit_solution(12676067300076853971)
XLA Ops:
  0.6 0.7 reduce.4
  1.5 1.4 maximum_bitcast_fusion.5.refs_0_
  2.9 128.8 %gather_weights.1 = (bf16[8,2,8,136]{3,2,1,0:T(8,128)(2,1)}, bf16[8,17,8,3264]{3,2,1,0:T(8,128)(2,1)}, bf16[8,17,8,1088]{3,2,1,0:T(8,128)(2,1)}, bf16[8,17,8,435...) custom-call(bf16[2,8,136]{2,1,0:T(8,128)(2,1)} %maximum_bitcast_fusion.5.refs_0_, bf16[17,8,3264]{2,1,0:T(8,128)(2,1)} %bitcast.306, ...), custom_call_target="tpu_custom_call" | custom-call | tf_op jit(solution)/shard_map/gather_weights/pallas_call | solution.py:165
  131.7 0.8 convert_bitcast_fusion
  134.1 6.5 fusion
  140.7 4.9 copy.65
  145.6 0.8 slice_convert_fusion
  149.2 40.2 %attend.2 = (bf16[8,2,128,128]{3,2,1,0:T(8,128)(2,1)S(1)}, bf16[2,128,128]{2,1,0:T(8,128)(2,1)S(1)}, bf16[8,2,3,128,128]{4,3,2,1,0:T(8,128)(2,1)}, bf16[8,2,128,128]{3,2,1,0:T(8,128)(2,1)}) custom-call(s32[2]{0:T(128)S(1)} %fusion.42.lengths, bf16[8,2,3,128,128]{4,3,2,1,0:T(8,128)(2,1)S(1)} %pad_maximum_fusion.pack, bf16[2,128,128]{2,1,0:T(8,128)(2,1)S(1)} %bitcast.259, ...), custom_call_target="tpu_custom_call" | custom-call | tf_op jit(solution)/shard_map/attend/pallas_call | solution.py:558
  190.2 3.0 fusion.74
  193.4 14.1 %fusion.18 = bf16[256,1088]{0,1:T(8,128)(2,1)} fusion(f32[256,1088]{0,1:T(8,128)S(1)} %get-tuple-element.140, bf16[4352,1088]{1,0:T(8,128)(2,1)} %bitcast.325, bf16[1088,4352]{1,0:T(8,128)(2,1)} %bitcast.266, f32[4352]{0:T(1024)S(1)} %reshape.504, f32[1088]{0:T(1024)S(1)} %add.240, f32[1088]{0:T(1024)S(1)} %add.232, f32[1088]{0:T(1024)S(1)} %mul.366, ...), kind=kOutput, calls=%fused_computation.44 | convolution fusion | flops 4861984768 | bytes 20643584 | tf_op jit(solution)/shard_map/dot_general | solution.py:435
  207.5 4.3 collective-permute-start
  211.9 5.6 copy.63
  217.6 1.1 copy.64
  218.8 2.4 collective-permute-done
  221.7 6.9 %fusion.1 = bf16[256,3264]{0,1:T(8,128)(2,1)S(1)} fusion(bf16[1088,3264]{1,0:T(8,128)(2,1)} %bitcast.330, f32[3264]{0:T(1024)S(1)} %concatenate.41, f32[256,1088]{0,1:T(8,128)S(1)} %get-tuple-element.101, f32[1088]{0:T(1024)S(1)} %add.222, f32[1088]{0:T(1024)S(1)} %mul.360, f32[256]{0:T(256)S(1)} %fusion.43, f32[256]{0:T(256)S(1)} %broadcast_multiply_fusion.1), kind=kOutput, calls=%fused_computation.12 | convolution fusion | flops 1821294592 | bytes 9911552 | tf_op jit(solution)/shard_map/dot_general | solution.py:435
  231.1 37.0 %attend.3 = (bf16[8,2,128,128]{3,2,1,0:T(8,128)(2,1)S(1)}, bf16[2,128,128]{2,1,0:T(8,128)(2,1)S(1)}, bf16[8,2,3,128,128]{4,3,2,1,0:T(8,128)(2,1)S(1)}, bf16[8,2,128,128]{3,2,1,0:T(8,128)(2,1)S(1)}) custom-call(s32[2]{0:T(128)S(1)} %fusion.42.lengths, bf16[8,2,3,128,128]{4,3,2,1,0:T(8,128)(2,1)S(1)} %pad_maximum_fusion.1.pack, ...), custom_call_target="tpu_custom_call" | custom-call | tf_op jit(solution)/shard_map/attend/pallas_call | solution.py:558
  268.7 0.7 copy-done.4
  269.4 1.2 fusion.75
  270.9 9.2 %convolution_add_fusion = f32[256,4352]{1,0:T(8,128)} fusion(bf16[1088,4352]{1,0:T(8,128)(2,1)} %bitcast.267, f32[4352]{0:T(1024)S(1)} %reshape.504, f32[256,1088]{0,1:T(8,128)S(1)} %get-tuple-element.142, f32[256]{0:T(256)S(1)} %fusion.44, f32[256]{0:T(256)S(1)} %broadcast_multiply_fusion, f32[1088]{0:T(1024)S(1)} %add.232, f32[1088]{0:T(1024)S(1)} %mul.366), kind=kOutput, calls=%fused_computation.5 | convolution fusion | flops 2426814464 | bytes 15068672 | tf_op jit(solution)/shard_map/dot_general | solution.py:435
  280.0 12.8 %multiply_reduce_fusion.5 = (f32[256]{0:T(256)S(1)}, f32[256,1088]{0,1:T(8,128)}) fusion(f32[256,1088]{0,1:T(8,128)S(1)} %get-tuple-element.142, f32[256]{0:T(256)S(1)} %broadcast_multiply_fusion, f32[1088]{0:T(1024)S(1)} %mul.366, bf16[1088,4352]{1,0:T(8,128)(2,1)} %bitcast.268, f32[256,4352]{1,0:T(8,128)} %convolution_add_fusion, ...), kind=kOutput, calls=%fused_computation.74 | convolution fusion | flops 4872011776 | bytes 26188032 | tf_op jit(solution)/shard_map/dot_general | solution.py:435
  293.4 1.6 fusion.65
  295.1 3.0 convolution_convert_fusion.5
  298.2 0.8 copy-done.30
  299.9 37.1 %attend_back.2 = (bf16[8,2,3,128,128]{4,3,2,1,0:T(8,128)(2,1)S(1)}, bf16[2,128,128]{2,1,0:T(8,128)(2,1)S(1)}, bf16[2,128,128]{2,1,0:T(8,128)(2,1)S(1)}) custom-call(s32[2]{0:T(128)S(1)} %fusion.42.lengths, bf16[8,2,3,128,128]{4,3,2,1,0:T(8,128)(2,1)S(1)} %get-tuple-element.38.held, bf16[8,2,128,128]{3,2,1,0:T(8,128)(2,1)S(1)} %get-tuple-element.39.held_last, ...), custom_call_target="tpu_custom_call" | custom-call | tf_op jit(solution)/shard_map/attend_back/pallas_call | solution.py:704
  337.5 0.9 copy.155
  339.2 1.2 copy_bitcast_fusion.3
  340.4 4.0 concatenate.46
  344.5 5.6 multiply_reduce_fusion.4
  350.5 0.9 copy-done.8
  351.8 1.2 add_convert_fusion.3
  353.0 1.3 collective-permute-start.1
  354.4 15.4 %collective-permute-done.1 = bf16[256,1088]{0,1:T(8,128)(2,1)S(1)} collective-permute-done((bf16[256,1088]{0,1:T(8,128)(2,1)}, bf16[256,1088]{0,1:T(8,128)(2,1)S(1)}, u32[]{:S(2)}, u32[]{:S(2)}) %collective-permute-start.1) | collective-permute-done | bytes 557088 | tf_op jit(solution)/shard_map/ppermute | solution.py:895
  369.8 1.5 convert_reduce_fusion.2
  371.3 7.8 %convert_reduce_fusion = (f32[4352]{0:T(1024)S(1)}, bf16[256,4352]{1,0:T(8,128)(2,1)S(1)}) fusion(f32[256,4352]{1,0:T(8,128)} %convolution_add_fusion, bf16[256,1088]{0,1:T(8,128)(2,1)S(1)} %get-tuple-element.89, bf16[4352,1088]{1,0:T(8,128)(2,1)} %bitcast.327), kind=kOutput, calls=%fused_computation.25 | convolution fusion | flops 2448813824 | bytes 16729088 | tf_op jit(solution)/shard_map/dot_general | solution.py:435
  379.2 6.5 fusion.62
  387.0 0.7 convert_reduce_fusion.3
  387.6 1.1 copy-done.12
  388.8 0.9 convolution_convert_fusion.4
  390.4 5.4 convolution_convert_fusion
  395.8 5.5 convolution_convert_fusion.1
  402.3 35.9 %attend_back.3 = (bf16[8,2,3,128,128]{4,3,2,1,0:T(8,128)(2,1)S(1)}, bf16[2,128,128]{2,1,0:T(8,128)(2,1)S(1)}, bf16[2,128,128]{2,1,0:T(8,128)(2,1)S(1)}) custom-call(s32[2]{0:T(128)S(1)} %fusion.42.lengths, bf16[8,2,3,128,128]{4,3,2,1,0:T(8,128)(2,1)S(1)} %get-tuple-element.38.held, bf16[8,2,128,128]{3,2,1,0:T(8,128)(2,1)S(1)} %get-tuple-element.39.held_last, ...), custom_call_target="tpu_custom_call" | custom-call | tf_op jit(solution)/shard_map/attend_back/pallas_call | solution.py:704
  439.8 2.1 concatenate.47
  442.0 5.9 fusion.63
  447.9 5.1 convolution_convert_fusion.2
  453.3 0.8 copy-done.15
  454.4 2.4 convolution_convert_fusion.3
  456.8 14.1 %copy.97 = bf16[4352,1088]{1,0:T(8,128)(2,1)} copy(bf16[4352,1088]{0,1:T(8,128)(2,1)} %convolution_convert_fusion) | data formatting | bytes 18939904 | tf_op jit(solution)/shard_map/convert_element_type | solution.py:864
  472.5 0.8 maximum_bitcast_fusion.4.refs_3_
  473.3 168.9 %sum_gradients.1 = (bf16[4,17,8,1088]{3,2,1,0:T(8,128)(2,1)}, bf16[4,5,8,4352]{3,2,1,0:T(8,128)(2,1)}, bf16[4,5,8,3264]{3,2,1,0:T(8,128)(2,1)}, f32[4,1,8,136]{3,2,1,0:T(8,128)}, bf16[4,5,8,1088]{3,2,1,0:T(8,128)(2,1)}) custom-call(bf16[8,68,8,1088]{3,2,1,0:T(8,128)(2,1)} %bitcast.265, bf16[8,17,8,4352]{3,2,1,0:T(8,128)(2,1)} %bitcast.263, ...), custom_call_target="tpu_custom_call" | custom-call | tf_op jit(solution)/shard_map/sum_gradients/pallas_call | solution.py:389
  642.3 1.8 slice_bitcast_fusion.14
  644.1 2.0 slice_bitcast_fusion.17
  646.1 0.7 slice_bitcast_fusion.21
  646.9 1.1 copy-done.2
  648.4 10.6 %add_select_fusion = f32[256,1088]{0,1:T(8,128)} fusion(f32[256,1088]{0,1:T(8,128)S(1)} %copy-done.17, f32[256]{0:T(256)S(1)} %negate_multiply_fusion, f32[1088]{0:T(1024)S(1)} %copy-done.52, f32[256,1088]{0,1:T(8,128)S(1)} %copy-done.2, bf16[4352,1088]{1,0:T(8,128)(2,1)} %bitcast.328, pred[]{:T(512)S(6)} %eq.16, f32[256]{0:T(256)S(1)} %multiply_multiply_fusion.3, ...), kind=kOutput, calls=%fused_computation.66 | convolution fusion | flops 2437398528 | bytes 19509760 | tf_op jit(solution)/shard_map/dot_general | solution.py:435
  659.0 1.8 reshape.493
  660.9 1.1 copy.98
  661.9 0.6 copy-done.21
  662.7 1.4 slice_bitcast_fusion.22
  664.1 0.7 slice.317
  664.8 0.7 reshape.501
  665.5 1.4 fusion.26
  666.9 0.9 fusion.40
  667.8 1.6 fusion.25
  669.4 1.7 fusion.24
  (241 shorter events, 20.0 us)
Async XLA Ops:
  2.9 129.9 %copy-start.13 = (bf16[2,1,128,1088]{2,3,1,0:T(8,128)(2,1)S(1)}, bf16[2,1,128,1088]{2,3,1,0:T(8,128)(2,1)}, u32[]{:S(2)}) copy-start(bf16[2,1,128,1088]{2,3,1,0:T(8,128)(2,1)} %param.10) | copy-start | bytes 1671172
  132.7 89.0 %copy-start.39 = (f32[1088]{0:T(1024)}, f32[1088]{0:T(1024)S(1)}, u32[]{:S(2)}) copy-start(f32[1088]{0:T(1024)S(1)} %add.222) | copy-start | bytes 13060
  132.8 88.9 %copy-start.35 = (f32[1088]{0:T(1024)}, f32[1088]{0:T(1024)S(1)}, u32[]{:S(2)}) copy-start(f32[1088]{0:T(1024)S(1)} %mul.360) | copy-start | bytes 13060
  147.8 0.9 copy-start.56
  147.8 0.9 copy-start.57
  190.1 3.3 copy-start.51
  190.2 80.6 %copy-start.37 = (f32[1088]{0:T(1024)}, f32[1088]{0:T(1024)S(1)}, u32[]{:S(2)}) copy-start(f32[1088]{0:T(1024)S(1)} %add.232) | copy-start | bytes 13060
  193.4 18.6 %copy-start.20 = (bf16[2,1,128,1088]{2,3,1,0:T(8,128)(2,1)S(1)}, bf16[2,1,128,1088]{2,3,1,0:T(8,128)(2,1)}, u32[]{:S(2)}) copy-start(bf16[2,1,128,1088]{2,3,1,0:T(8,128)(2,1)} %param.11) | copy-start | bytes 1671172
  207.5 13.7 %collective-permute-start = (bf16[256,1088]{0,1:T(8,128)(2,1)}, bf16[256,1088]{0,1:T(8,128)(2,1)S(1)}, u32[]{:S(2)}, u32[]{:S(2)}) collective-permute-start(bf16[256,1088]{0,1:T(8,128)(2,1)} %fusion.18), channel_id=1, source_target_pairs={{0,64},{1,65},{2,66},{3,67},{4,68},{5,69},{6,70},{7,71},{8,72},{9,... | collective-permute-start | bytes 1671176 | tf_op jit(solution)/shard_map/ppermute | solution.py:892
  218.8 76.3 %copy-start.47 = (f32[256]{0:T(256)}, f32[256]{0:T(256)S(1)}, u32[]{:S(2)}) copy-start(f32[256]{0:T(256)S(1)} %compare_convert_fusion.1) | copy-start | bytes 3076
  221.4 7.2 %copy-start.3 = (f32[256,1088]{0,1:T(8,128)}, f32[256,1088]{0,1:T(8,128)S(1)}, u32[]{:S(2)}) copy-start(f32[256,1088]{0,1:T(8,128)S(1)} %get-tuple-element.101) | copy-start | bytes 3342340
  221.5 7.2 %copy-start.43 = (f32[256]{0:T(256)}, f32[256]{0:T(256)S(1)}, u32[]{:S(2)}) copy-start(f32[256]{0:T(256)S(1)} %broadcast_multiply_fusion.1) | copy-start | bytes 3076
  221.7 7.0 %copy-start.49 = (f32[256]{0:T(256)}, f32[256]{0:T(256)S(1)}, u32[]{:S(2)}) copy-start(f32[256]{0:T(256)S(1)} %multiply_reduce_fusion.7) | copy-start | bytes 3076
  221.7 7.0 %copy-start.45 = (f32[256]{0:T(256)}, f32[256]{0:T(256)S(1)}, u32[]{:S(2)}) copy-start(f32[256]{0:T(256)S(1)} %fusion.43) | copy-start | bytes 3076
  231.1 37.6 %copy-start.11 = (bf16[8,17,8,1088]{3,2,1,0:T(8,128)(2,1)S(1)}, bf16[8,17,8,1088]{3,2,1,0:T(8,128)(2,1)}, u32[]{:S(2)}) copy-start(bf16[8,17,8,1088]{3,2,1,0:T(8,128)(2,1)} %get-tuple-element.34) | copy-start | bytes 7102468
  268.1 1.3 copy-start.4
  268.7 1.9 copy-start.14
  270.6 22.8 %copy-start = (f32[256,1088]{0,1:T(8,128)}, f32[256,1088]{0,1:T(8,128)S(1)}, u32[]{:S(2)}) copy-start(f32[256,1088]{0,1:T(8,128)S(1)} %get-tuple-element.142) | copy-start | bytes 3342340
  270.8 22.5 %copy-start.41 = (f32[256]{0:T(256)}, f32[256]{0:T(256)S(1)}, u32[]{:S(2)}) copy-start(f32[256]{0:T(256)S(1)} %fusion.44) | copy-start | bytes 3076
  293.4 1.7 copy-start.7
  295.0 3.1 copy-start.18
  295.0 3.1 copy-start.54
  298.1 0.8 copy-start.30
  298.9 0.8 slice-start.3
  340.4 4.0 copy-start.5
  344.5 5.7 copy-start.50
  344.5 5.7 copy-start.44
  344.5 5.7 copy-start.46
  350.2 1.3 copy-start.8
  350.2 1.6 copy-start.19
  350.2 1.6 copy-start.48
  350.2 1.6 copy-start.55
  353.0 16.8 %collective-permute-start.1 = (bf16[256,1088]{0,1:T(8,128)(2,1)}, bf16[256,1088]{0,1:T(8,128)(2,1)S(1)}, u32[]{:S(2)}, u32[]{:S(2)}) collective-permute-start(bf16[256,1088]{0,1:T(8,128)(2,1)} %add_convert_fusion.3), channel_id=1, source_target_pairs={{64,0},{65,1},{66,2},{67,3},{68,4},{69,5},{70,6},{71,7},{72,8},{73... | collective-permute-start | bytes 1671176 | tf_op jit(solution)/shard_map/ppermute | solution.py:895
  371.3 7.8 %copy-start.1 = (f32[256,1088]{0,1:T(8,128)S(1)}, f32[256,1088]{0,1:T(8,128)}, u32[]{:S(2)}) copy-start(f32[256,1088]{0,1:T(8,128)} %copy-done) | copy-start | bytes 3342340
  379.1 6.5 copy-start.53
  379.2 6.5 copy-start.42
  385.7 1.3 copy-start.9
  387.0 1.8 copy-start.12
  387.0 3.4 slice-start
  387.6 2.1 copy-start.16
  388.8 1.6 slice-start.1
  389.7 6.1 copy-start.29
  390.4 5.4 copy-start.38
  401.3 0.8 slice-start.2
  439.8 2.2 copy-start.6
  439.8 2.1 copy-start.36
  442.0 5.9 copy-start.10
  442.0 5.9 copy-start.40
  447.8 23.2 %copy-start.22 = (f32[256,1088]{0,1:T(8,128)}, f32[256,1088]{0,1:T(8,128)S(1)}, u32[]{:S(2)}) copy-start(f32[256,1088]{0,1:T(8,128)S(1)} %get-tuple-element.148) | copy-start | bytes 3342340
  453.0 1.0 copy-start.15
  453.0 1.4 copy-start.17
  642.3 3.8 copy-start.34
  642.3 4.5 copy-start.25
  646.8 1.2 copy-start.2
  646.8 1.6 copy-start.23
  646.8 1.6 copy-start.52
  660.9 1.7 copy-start.21
  662.6 2.9 copy-start.24
  662.6 2.9 copy-start.26
  662.6 2.9 copy-start.27
  662.6 2.9 copy-start.28
  665.5 1.4 copy-start.31
  665.5 1.4 copy-start.32
  665.5 1.4 copy-start.33

commit v2 on v1

--- a/solution.py
+++ b/solution.py
@@ -37,141 +37,214 @@
     return (member // 2, member % 2, replica // 2, replica % 2)
 
 
-def gather_kernel(count, *refs):
+class Links:
+    def __init__(self, send, recv):
+        self.send, self.recv, self.used = send, recv, 0
+
+    def channel(self, device):
+        self.used += 1
+        return Channel(self.send.at[self.used - 1], self.recv.at[self.used - 1], device)
+
+
+class Channel:
+    def __init__(self, send, recv, device):
+        self.send_sem, self.recv_sem, self.device = send, recv, device
+
+    def copy(self, src, dst):
+        return remote(src, dst, self.send_sem, self.recv_sem, self.device)
+
+    def send(self, src, dst):
+        self.copy(src, dst).start()
+
+    def sent(self, src):
+        self.copy(src, src).wait_send()
+
+    def came(self, dst):
+        self.copy(dst, dst).wait_recv()
+
+
+def near_devices():
+    z, x, y, c = place()
+    return {
+        "above": {"group": 2 * ((z + 1) % RING) + x},
+        "below": {"group": 2 * ((z + 3) % RING) + x},
+        "partner": {"group": 2 * z + 1 - x},
+        "sibling": {"rep": 2 * y + 1 - c},
+        "next": {"rep": 2 * ((y + 1) % RING) + c},
+        "last": {"rep": 2 * ((y + 3) % RING) + c},
+    }
+
+
+def gather_job(links, shard, full, first, size, spread):
+    z, x, y, c = place()
+    near = near_devices()
+    xc = (x + c) % 2
+    me = 2 * z + x
+    base, above, below, across = (2 * ((z + k) % RING) + xc for k in (0, 1, 3, 2))
+    piece = size // RING if spread else size
+    low = piece - piece // 2
+    finals = []
+
+    def region(slot, owner, part=""):
+        start = first + owner * piece if spread else first
+        if part == "low":
+            return full.at[slot, pl.ds(start, low)]
+        if part == "high":
+            return full.at[slot, pl.ds(start + low, piece - low)]
+        return full.at[slot, pl.ds(start, piece)]
+
+    def on_core(core, action):
+        pl.when(c == core)(action)
+
+    def always(action):
+        action()
+
+    def relay(channel, ref, run):
+        run(lambda: channel.send(ref, ref))
+        finals.append(lambda: run(lambda: channel.sent(ref)))
+
+    def hand(slot, owner, run, part=""):
+        channel = links.channel(near["sibling"])
+        relay(channel, region(slot, owner, part), run)
+        other = region(slot + 1 - 2 * xc, owner, part)
+        get = (lambda action: on_core(0, action)) if run is not always else always
+        finals.append(lambda: get(lambda: channel.came(other)))
+
+    across_x = links.channel(near["partner"])
+    up, down = links.channel(near["above"]), links.channel(near["below"])
+    far_up, far_down = links.channel(near["above"]), links.channel(near["below"])
+    own = shard.at[pl.ds(first + y * piece if spread else first, piece)]
+    second = lambda action: on_core(1, action)
+
+    def first_core():
+        up.send(own, region(base, y))
+        down.send(own, region(base, y))
+
+    on_core(0, first_core)
+    on_core(1, lambda: across_x.send(own, region(me, y)))
+    finals.append(lambda: on_core(1, lambda: across_x.sent(own)))
+    finals.append(lambda: up.sent(own))
+    finals.append(lambda: down.sent(own))
+    yield
+
+    rings = []
+
+    def pass_on(slot, run):
+        if spread:
+            forth, back = links.channel(near["next"]), links.channel(near["last"])
+            relay(forth, region(slot, y), run)
+            relay(back, region(slot, y), run)
+            rings.append((slot, run, forth, back))
+        hand(slot, y, run)
+
+    def second_core():
+        across_x.came(region(base, y))
+        up.send(region(base, y), region(base, y))
+        down.send(region(base, y), region(base, y))
+
+    on_core(1, second_core)
+    pass_on(base, second)
+    yield
+
+    up.came(region(below, y))
+    relay(far_up, region(below, y, "low"), always)
+    pass_on(below, always)
+    down.came(region(above, y))
+    if piece > low:
+        relay(far_down, region(above, y, "high"), always)
+    pass_on(above, always)
+    yield
+
+    far_up.came(region(across, y, "low"))
+    if piece > low:
+        far_down.came(region(across, y, "high"))
+    pass_on(across, always)
+    yield
+
+    if spread:
+        ends = []
+        for slot, run, forth, back in rings:
+            far_forth, far_back = links.channel(near["next"]), links.channel(near["last"])
+            behind, ahead = (y + 3) % RING, (y + 1) % RING
+            run(lambda: forth.came(region(slot, behind)))
+            relay(far_forth, region(slot, behind, "low"), run)
+            hand(slot, behind, run)
+            run(lambda: back.came(region(slot, ahead)))
+            if piece > low:
+                relay(far_back, region(slot, ahead, "high"), run)
+            hand(slot, ahead, run)
+            ends.append((slot, run, far_forth, far_back))
+        yield
+        for slot, run, far_forth, far_back in ends:
+            far = (y + 2) % RING
+            run(lambda: far_forth.came(region(slot, far, "low")))
+            if piece > low:
+                run(lambda: far_back.came(region(slot, far, "high")))
+            hand(slot, far, run)
+        yield
+    for action in finals:
+        action()
+
+
+class Pump:
+    def __init__(self, jobs):
+        self.jobs = list(jobs)
+
+    def __call__(self):
+        alive = []
+        for job in self.jobs:
+            try:
+                next(job)
+                alive.append(job)
+            except StopIteration:
+                pass
+        self.jobs = alive
+
+    def drain(self):
+        while self.jobs:
+            self()
+
+
+MAX_LINKS = 160
+
+
+def gather_jobs(links, local, plan, ins, outs):
+    member = lax.axis_index("group")
+
+    def own(i):
+        copy = pltpu.make_async_copy(ins[i], outs[i].at[member], local.at[i])
+        copy.start()
+        yield
+        copy.wait()
+
+    jobs = [gather_job(links, ins[i], outs[i], *rest) for i, *rest in plan]
+    return Pump(jobs + [own(i) for i in range(len(ins))])
+
+
+def gather_kernel(plan, count, *refs):
     ins, outs = refs[:count], refs[count : 2 * count]
     send, recv, local = refs[2 * count :]
-    z, x, y, c = place()
-    me = 2 * z + x
-    xc = (x + c) % 2
-    zp, zm, zo = (z + 1) % RING, (z + 3) % RING, (z + 2) % RING
-    base, above, below, across = 2 * z + xc, 2 * zp + xc, 2 * zm + xc, 2 * zo + xc
-    to_above = {"group": 2 * zp + x}
-    to_below = {"group": 2 * zm + x}
-    sibling = {"rep": 2 * y + 1 - c}
-    partner = {"group": 2 * z + 1 - x}
-    greet([to_above, to_below, sibling, partner])
-
-    def part(array, slot, kind):
-        half = ins[array].shape[0] // 2
-        ref = outs[array].at[slot]
-        if kind == "low":
-            return ref.at[pl.ds(0, half)]
-        if kind == "high":
-            return ref.at[pl.ds(half, ins[array].shape[0] - half)]
-        return ref
-
-    def across_x(i):
-        return remote(ins[i], part(i, me, ""), send.at[i, 0], recv.at[i, 0], partner)
-
-    def first_up(i):
-        src = part(i, base, "")
-        return remote(src, part(i, base, ""), send.at[i, 1], recv.at[i, 1], to_above)
-
-    def first_down(i):
-        src = part(i, base, "")
-        return remote(src, part(i, base, ""), send.at[i, 2], recv.at[i, 2], to_below)
-
-    def second_up(i):
-        src = part(i, below, "low")
-        return remote(src, src, send.at[i, 3], recv.at[i, 3], to_above)
-
-    def second_down(i):
-        src = part(i, above, "high")
-        return remote(src, src, send.at[i, 4], recv.at[i, 4], to_below)
-
-    def hand(i, slot, kind, sem):
-        src = part(i, slot, kind)
-        return remote(src, src, send.at[i, sem], recv.at[i, sem], sibling)
-
-    def own(i):
-        return pltpu.make_async_copy(ins[i], part(i, me, ""), local.at[i])
-
-    def own_up(i):
-        return remote(ins[i], part(i, me, ""), send.at[i, 1], recv.at[i, 1], to_above)
-
-    def own_down(i):
-        return remote(ins[i], part(i, me, ""), send.at[i, 2], recv.at[i, 2], to_below)
-
-    arrays = range(count)
-
-    @pl.when(c == 0)
-    def _():
-        for i in arrays:
-            own_up(i).start()
-            own_down(i).start()
-
-    @pl.when(c == 1)
-    def _():
-        for i in arrays:
-            across_x(i).start()
-
-    for i in arrays:
-        own(i).start()
-
-    @pl.when(c == 1)
-    def _():
-        for i in arrays:
-            remote(ins[i], part(i, base, ""), send.at[i, 0], recv.at[i, 0], partner).wait_recv()
-            first_up(i).start()
-            first_down(i).start()
-            hand(i, base, "", 5).start()
-
-    for i in arrays:
-        remote(ins[i], part(i, below, ""), send.at[i, 1], recv.at[i, 1], to_above).wait_recv()
-        second_up(i).start()
-        hand(i, below, "", 6).start()
-        remote(ins[i], part(i, above, ""), send.at[i, 2], recv.at[i, 2], to_below).wait_recv()
-        second_down(i).start()
-        hand(i, above, "", 7).start()
-    for i in arrays:
-        src = part(i, across, "low")
-        remote(src, src, send.at[i, 3], recv.at[i, 3], to_above).wait_recv()
-        hand(i, across, "low", 8).start()
-        src = part(i, across, "high")
-        remote(src, src, send.at[i, 4], recv.at[i, 4], to_below).wait_recv()
-        hand(i, across, "high", 9).start()
-
-    @pl.when(c == 0)
-    def _():
-        for i in arrays:
-            hand(i, 2 * z + 1 - xc, "", 5).wait_recv()
-            own_up(i).wait_send()
-            own_down(i).wait_send()
-
-    @pl.when(c == 1)
-    def _():
-        for i in arrays:
-            across_x(i).wait_send()
-            first_up(i).wait_send()
-            first_down(i).wait_send()
-            hand(i, base, "", 5).wait_send()
-
-    for i in arrays:
-        hand(i, 2 * zm + 1 - xc, "", 6).wait_recv()
-        hand(i, 2 * zp + 1 - xc, "", 7).wait_recv()
-        hand(i, 2 * zo + 1 - xc, "low", 8).wait_recv()
-        hand(i, 2 * zo + 1 - xc, "high", 9).wait_recv()
-        second_up(i).wait_send()
-        second_down(i).wait_send()
-        hand(i, below, "", 6).wait_send()
-        hand(i, above, "", 7).wait_send()
-        hand(i, across, "low", 8).wait_send()
-        hand(i, across, "high", 9).wait_send()
-        own(i).wait()
-
-
-def gather_weights(shards):
+    greet(list(near_devices().values()))
+    gather_jobs(Links(send, recv), local, plan, ins, outs).drain()
+
+
+def gathered_shapes(shards):
+    return [jax.ShapeDtypeStruct((8,) + s.shape, s.dtype) for s in shards]
+
+
+def gather_sems(count):
+    dma = pltpu.SemaphoreType.DMA
+    return [dma((MAX_LINKS,)), dma((MAX_LINKS,)), dma((count,))]
+
+
+def gather_weights(shards, plan):
     count = len(shards)
     return pl.pallas_call(
-        functools.partial(gather_kernel, count),
-        out_shape=[jax.ShapeDtypeStruct((8,) + s.shape, s.dtype) for s in shards],
+        functools.partial(gather_kernel, plan, count),
+        out_shape=gathered_shapes(shards),
         in_specs=[pl.BlockSpec(memory_space=pl.ANY)] * count,
         out_specs=[pl.BlockSpec(memory_space=pl.ANY)] * count,
-        scratch_shapes=[
-            pltpu.SemaphoreType.DMA((count, 10)),
-            pltpu.SemaphoreType.DMA((count, 10)),
-            pltpu.SemaphoreType.DMA((count,)),
-        ],
+        scratch_shapes=gather_sems(count),
         compiler_params=pltpu.CompilerParams(collective_id=0, has_side_effects=True),
         name="gather_weights",
     )(*shards)
@@ -196,19 +269,19 @@
 PER_ARRAY = 9
 
 
-def sum_kernel(count, *refs):
-    ins, outs = refs[:count], refs[count : 2 * count]
-    buffers = refs[2 * count : 2 * count + PER_ARRAY * count]
-    send, recv, local = refs[2 * count + PER_ARRAY * count :]
+def sum_devices():
+    z, x, y, c = place()
+    near = near_devices()
+    partner = {"group": 2 * z + 1 - x, "rep": 2 * y + 1 - c}
+    others = [{"rep": 2 * ((y + j) % RING) + c} for j in range(1, RING)]
+    return (near["above"], near["below"], near["sibling"], partner, others)
+
+
+def sum_job(ins, outs, buffers, send, recv, local):
+    count = len(ins)
     z, x, y, c = place()
     xc = (x + c) % 2
-    zp, zm = (z + 1) % RING, (z + 3) % RING
-    to_above = {"group": 2 * zp + x}
-    to_below = {"group": 2 * zm + x}
-    sibling = {"rep": 2 * y + 1 - c}
-    partner = {"group": 2 * z + 1 - x, "rep": 2 * y + 1 - c}
-    others = [{"rep": 2 * ((y + j) % RING) + c} for j in range(1, RING)]
-    greet([to_above, to_below, sibling, partner] + others)
+    to_above, to_below, sibling, partner, others = sum_devices()
 
     def parts(i):
         return buffers[PER_ARRAY * i : PER_ARRAY * (i + 1)]
@@ -268,6 +341,7 @@
         for k in (2, 1, 3, 0):
             swap(i, k).start()
             load(i, k).start()
+    yield
 
     def step_cores(i):
         blocks, half, _ = sizes(i)
@@ -350,6 +424,7 @@
             at = tick - i
             if 0 <= at < len(steps):
                 steps[at](i)
+        yield
     for i in range(count):
         for k in range(RING):
             swap(i, k).wait_send()
@@ -368,8 +443,16 @@
             hand(i).wait_send()
 
 
-def sum_gradients(grads):
-    count = len(grads)
+def sum_kernel(count, *refs):
+    above, below, sibling, partner, others = sum_devices()
+    greet([above, below, sibling, partner] + others)
+    split = (2 + PER_ARRAY) * count
+    Pump(
+        [sum_job(refs[:count], refs[count : 2 * count], refs[2 * count : split], *refs[split:])]
+    ).drain()
+
+
+def sum_scratch(grads):
     scratch = []
     for grad in grads:
         _, blocks, rows, width = grad.shape
@@ -386,20 +469,24 @@
             (piece,),
         ):
             scratch.append(pltpu.VMEM(lead + (rows, width), grad.dtype))
+    dma = pltpu.SemaphoreType.DMA
+    return scratch + [dma((len(grads), 16)), dma((len(grads), 16)), dma((len(grads), 5))]
+
+
+def sum_shapes(grads):
+    return [
+        jax.ShapeDtypeStruct((RING, piece_rows(g.shape[1])) + g.shape[2:], g.dtype) for g in grads
+    ]
+
+
+def sum_gradients(grads):
+    count = len(grads)
     return pl.pallas_call(
         functools.partial(sum_kernel, count),
-        out_shape=[
-            jax.ShapeDtypeStruct((RING, piece_rows(g.shape[1])) + g.shape[2:], g.dtype)
-            for g in grads
-        ],
+        out_shape=sum_shapes(grads),
         in_specs=[pl.BlockSpec(memory_space=pl.ANY)] * count,
         out_specs=[pl.BlockSpec(memory_space=pl.ANY)] * count,
-        scratch_shapes=scratch
-        + [
-            pltpu.SemaphoreType.DMA((count, 16)),
-            pltpu.SemaphoreType.DMA((count, 16)),
-            pltpu.SemaphoreType.DMA((count, 5)),
-        ],
+        scratch_shapes=sum_scratch(grads),
         compiler_params=pltpu.CompilerParams(
             collective_id=1, has_side_effects=True, vmem_limit_bytes=60 * 1024 * 1024
         ),
@@ -451,13 +538,23 @@
     return (member, ahead, behind)
 
 
-def attend_kernel(
-    lengths, pack, last_kv, last_q, mixed, last_mixed, kept, kept_last,
-    held, held_last, staged, send, recv, send_last, recv_last, send_back, recv_back, local,
-):
+def attend_kernel(plan, shards, *refs):
+    lengths, pack, last_kv, last_q = refs[:4]
+    ins, refs = refs[4 : 4 + shards], refs[4 + shards :]
+    mixed, last_mixed, kept, kept_last = refs[:4]
+    outs, refs = refs[4 : 4 + shards], refs[4 + shards :]
+    held, held_last, staged = refs[:3]
+    send, recv, send_last, recv_last, send_back, recv_back, local = refs[3:10]
     count, micros, _, rows, lanes = pack.shape
     member, ahead, behind = peers(count)
-    greet([{"group": peer} for peer in ahead])
+    devices = [{"group": peer} for peer in ahead]
+    pump = Pump([])
+    if shards:
+        near = near_devices()
+        devices = devices + [near[name] for name in ("sibling", "next", "last")]
+    greet(devices)
+    if shards:
+        pump = gather_jobs(Links(refs[10], refs[11]), refs[12], plan, ins, outs)
 
     def out(m, j):
         return remote(
@@ -504,8 +601,10 @@
             out_last(m, j).start()
         for copy in own(m):
             copy.start()
-
-    def micro(m, carry):
+    pump()
+    pump()
+
+    def micro(m):
         for copy in own(m):
             copy.wait()
         for j in peer_range:
@@ -532,14 +631,16 @@
         for j in peer_range:
             back(m, j).start()
         own_back(m).start()
+        pump()
         both = held_last[:, m].reshape(count * rows, lanes)
         probs = soft_columns(both, last_q[m], member * rows, length).astype(jnp.bfloat16)
         last_mixed[m] = over_rows(both, probs).T.astype(jnp.bfloat16)
-        return carry
-
-    lax.fori_loop(0, micros, micro, 0)
+
+    for m in range(micros):
+        micro(m)
     for copy in keep():
         copy.start()
+    pump.drain()
     for m in range(micros):
         own_back(m).wait()
         for j in peer_range:
@@ -550,43 +651,58 @@
         copy.wait()
 
 
-def attend(lengths, pack, last_kv, last_q):
+def attend(lengths, pack, last_kv, last_q, shards=(), plan=()):
     count, micros, _, rows, lanes = pack.shape
     bf16 = jnp.bfloat16
     vmem, hbm = pl.BlockSpec(memory_space=pltpu.VMEM), pl.BlockSpec(memory_space=pl.ANY)
     dma = pltpu.SemaphoreType.DMA
     return pl.pallas_call(
-        attend_kernel,
+        functools.partial(attend_kernel, plan, len(shards)),
         out_shape=[
             jax.ShapeDtypeStruct((count, micros, rows, lanes), bf16),
             jax.ShapeDtypeStruct((micros, rows, lanes), bf16),
             jax.ShapeDtypeStruct(pack.shape, bf16),
             jax.ShapeDtypeStruct((count, micros, rows, lanes), bf16),
-        ],
-        in_specs=[pl.BlockSpec(memory_space=pltpu.SMEM), hbm, vmem, vmem],
-        out_specs=[hbm, vmem, hbm, hbm],
+        ]
+        + gathered_shapes(shards),
+        in_specs=[pl.BlockSpec(memory_space=pltpu.SMEM), hbm, vmem, vmem] + [hbm] * len(shards),
+        out_specs=[hbm, vmem, hbm, hbm] + [hbm] * len(shards),
         scratch_shapes=[
             pltpu.VMEM(pack.shape, bf16),
             pltpu.VMEM((count, micros, rows, lanes), bf16),
             pltpu.VMEM((count, micros, rows, lanes), bf16),
         ]
         + [dma((micros, count - 1))] * 6
-        + [dma((micros, 4))],
+        + [dma((micros, 4))]
+        + (gather_sems(len(shards)) if shards else []),
         compiler_params=pltpu.CompilerParams(
-            collective_id=2, has_side_effects=True, vmem_limit_bytes=48 * 1024 * 1024
+            collective_id=2 + 2 * min(1, len(shards)),
+            has_side_effects=True,
+            vmem_limit_bytes=48 * 1024 * 1024,
         ),
-        name="attend",
-    )(lengths, pack, last_kv, last_q)
-
-
-def attend_back_kernel(
-    lengths, held, held_last, last_q, grad_pack, last_grad, grads, last_key_grad, last_query_grad,
-    came, staged, staged_last, parts_last, key_total, value_total,
-    send, recv, send_back, recv_back, send_last, recv_last, local,
-):
+        name="attend_gather" if shards else "attend",
+    )(lengths, pack, last_kv, last_q, *shards)
+
+
+def attend_back_kernel(extra, *refs):
+    lengths, held, held_last, last_q, grad_pack, last_grad = refs[:6]
+    ins, refs = refs[6 : 6 + extra], refs[6 + extra :]
+    grads, last_key_grad, last_query_grad = refs[:3]
+    outs, refs = refs[3 : 3 + extra], refs[3 + extra :]
+    came, staged, staged_last, parts_last, key_total, value_total = refs[:6]
+    send, recv, send_back, recv_back, send_last, recv_last, local = refs[6:13]
     count, micros, _, rows, lanes = held.shape
     member, ahead, behind = peers(count)
-    greet([{"group": peer} for peer in ahead])
+    devices = [{"group": peer} for peer in ahead]
+    pump = Pump([])
+    if extra:
+        _, _, sibling, partner, others = sum_devices()
+        devices = devices + [sibling, partner] + others
+    greet(devices)
+    if extra:
+        split = 13 + PER_ARRAY * extra
+        pump = Pump([sum_job(ins, outs, refs[13:split], *refs[split:])])
+    pump()
     scale = HEAD ** (-0.5)
 
     def out(m, j):
@@ -633,7 +749,7 @@
             out(m, j).start()
         own(m).start()
 
-    def micro(m, carry):
+    def micro(m):
         length = lengths[m]
         both = held_last[:, m].reshape(count * rows, lanes)
         probs = soft_columns(both, last_q[m], member * rows, length)
@@ -647,6 +763,7 @@
         staged_last[:, m] = both_grad.astype(jnp.bfloat16).reshape(count, rows, lanes)
         for j in peer_range:
             back_last(m, j).start()
+        pump()
         own(m).wait()
         for j in peer_range:
             out(m, j).wait_recv()
@@ -680,9 +797,11 @@
             back(m, j).start()
         for copy in own_back(m):
             copy.start()
-        return carry
-
-    lax.fori_loop(0, micros, micro, 0)
+        pump()
+
+    for m in range(micros):
+        micro(m)
+    pump.drain()
     for m in range(micros):
         for copy in own_back(m):
             copy.wait()
@@ -696,20 +815,22 @@
             back(m, j).wait()
 
 
-def attend_back(lengths, held, held_last, last_q, grad_pack, last_grad):
+def attend_back(lengths, held, held_last, last_q, grad_pack, last_grad, sums=()):
     count, micros, _, rows, lanes = held.shape
     bf16 = jnp.bfloat16
     vmem, hbm = pl.BlockSpec(memory_space=pltpu.VMEM), pl.BlockSpec(memory_space=pl.ANY)
     dma = pltpu.SemaphoreType.DMA
     return pl.pallas_call(
-        attend_back_kernel,
+        functools.partial(attend_back_kernel, len(sums)),
         out_shape=[
             jax.ShapeDtypeStruct(held.shape, bf16),
             jax.ShapeDtypeStruct((micros, rows, lanes), bf16),
             jax.ShapeDtypeStruct((micros, rows, lanes), bf16),
-        ],
-        in_specs=[pl.BlockSpec(memory_space=pltpu.SMEM), vmem, vmem, vmem, hbm, vmem],
-        out_specs=[hbm, vmem, vmem],
+        ]
+        + sum_shapes(sums),
+        in_specs=[pl.BlockSpec(memory_space=pltpu.SMEM), vmem, vmem, vmem, hbm, vmem]
+        + [hbm] * len(sums),
+        out_specs=[hbm, vmem, vmem] + [hbm] * len(sums),
         scratch_shapes=[
             pltpu.VMEM((count, micros, rows, lanes), bf16),
             pltpu.VMEM(held.shape, bf16),
@@ -719,12 +840,15 @@
             pltpu.VMEM((count * rows, lanes), jnp.float32),
         ]
         + [dma((micros, count - 1))] * 6
-        + [dma((micros, 3))],
+        + [dma((micros, 3))]
+        + (sum_scratch(sums) if sums else []),
         compiler_params=pltpu.CompilerParams(
-            collective_id=3, has_side_effects=True, vmem_limit_bytes=48 * 1024 * 1024
+            collective_id=3 + 2 * min(1, len(sums)),
+            has_side_effects=True,
+            vmem_limit_bytes=58 * 1024 * 1024 if sums else 48 * 1024 * 1024,
         ),
-        name="attend_back",
-    )(lengths, held, held_last, last_q, grad_pack, last_grad)
+        name="attend_back_sum" if sums else "attend_back",
+    )(lengths, held, held_last, last_q, grad_pack, last_grad, *sums)
 
 
 def norm_rows(inputs, gain_row, bias_row):
@@ -782,27 +906,22 @@
         ],
         0,
     )
-    full = gather_weights(
-        [
-            in_blocks(small),
-            in_blocks(w_qkv[0]),
-            in_blocks(w_proj[0]),
-            in_blocks(w_up[0]),
-            in_blocks(w_down[0]),
-        ]
+    small_full, qkv_full = gather_weights(
+        [in_blocks(small), in_blocks(w_qkv[0])],
+        ((0, 0, 2, False), (1, 0, 9, False), (1, 9, 8, True)),
     )
-    vector_rows = full[0][:, 0].transpose(1, 0, 2).reshape(8, width).astype(jnp.float32)
-    up_bias = full[0][:, 1, :bias_rows].reshape(-1).astype(jnp.float32)
-    qkv_weight, proj_weight, up_weight, down_weight = (
-        array.reshape(-1, array.shape[-1]) for array in full[1:]
-    )
+    vector_rows = small_full[:, 0].transpose(1, 0, 2).reshape(8, width).astype(jnp.float32)
+    up_bias = small_full[:, 1, :bias_rows].reshape(-1).astype(jnp.float32)
+    qkv_weight = qkv_full.reshape(width, -1)
+    later = [in_blocks(w_proj[0]), in_blocks(w_up[0]), in_blocks(w_down[0])]
+    later_plan = ((0, 0, 17, False), (1, 0, 16, True), (2, 0, 68, True), (1, 16, 1, False))
     qkv_bias = jnp.concatenate([vector_rows[2], jnp.zeros_like(vector_rows[2]), vector_rows[3]])
 
     def pad_last(matrix, before):
         block = matrix.reshape(micros, rows, HEAD)
         return jnp.pad(block, ((0, 0), (0, 0), (before, LANES - HEAD - before)))
 
-    def forward(inputs):
+    def forward(inputs, weights):
         normed = norm_rows(inputs, vector_rows[0], vector_rows[1]).astype(jnp.bfloat16)
         qkv = (plain(normed, qkv_weight) + qkv_bias).astype(jnp.bfloat16)
         thirds = [qkv[:, i * width : (i + 1) * width] for i in range(3)]
@@ -811,7 +930,14 @@
             micros, rows, LANES
         )
         last_q = pad_last(thirds[0][:, wide:], 0)
-        mixed, last_mixed, held, held_last = attend(lengths, pack, last_kv, last_q)
+        if weights is None:
+            mixed, last_mixed, held, held_last, *full = attend(
+                lengths, pack, last_kv, last_q, later, later_plan
+            )
+            weights = [array.reshape(-1, width if i != 1 else 4 * width) for i, array in enumerate(full)]
+        else:
+            mixed, last_mixed, held, held_last = attend(lengths, pack, last_kv, last_q)
+        proj_weight, up_weight, down_weight = weights
         attn_mixed = jnp.concatenate(
             [by_rows(mixed), last_mixed[:, :, HEAD:].reshape(micros * rows, HEAD)], 1
         )
@@ -820,9 +946,15 @@
         pre_act = plain(normed_two, up_weight) + up_bias
         activated = gelu_tanh(pre_act).astype(jnp.bfloat16)
         output = hidden + plain(activated, down_weight) + vector_rows[7]
-        return (output, (inputs, held, held_last, last_q, attn_mixed, hidden, pre_act, activated))
-
-    def backward(grad_output, saved):
+        return (output, weights, (inputs, held, held_last, last_q, attn_mixed, hidden, pre_act, activated))
+
+    def outer(left, right):
+        return over_rows(left, right).astype(jnp.bfloat16)
+
+    def shards(matrix):
+        return matrix.reshape(count, -1, 8, matrix.shape[-1])
+
+    def backward(grad_output, saved, final):
         inputs, held, held_last, last_q, attn_mixed, hidden, pre_act, activated = saved
         grad_two = grad_output.astype(jnp.bfloat16)
         grad_act = plain(grad_two, down_weight.T)
@@ -832,13 +964,20 @@
         grad_hidden = grad_output + from_norm
         grad_one = grad_hidden.astype(jnp.bfloat16)
         grad_mixed = plain(grad_one, proj_weight.T).astype(jnp.bfloat16)
-        grads, last_key_grad, last_query_grad = attend_back(
+        first_grads = ()
+        if final:
+            first_grads = (
+                shards(outer(activated, grad_two)),
+                shards(outer(normed_two.astype(jnp.bfloat16), grad_pre)),
+            )
+        grads, last_key_grad, last_query_grad, *first_sums = attend_back(
             lengths,
             held,
             held_last,
             last_q,
             by_heads(grad_mixed[:, :wide], micros, rows, count),
             pad_last(grad_mixed[:, wide:], HEAD),
+            first_grads,
         )
 
         def last(block, first):
@@ -860,9 +999,6 @@
         grad_in = grad_hidden + from_norm
 
         def weight_grads():
-            def outer(left, right):
-                return over_rows(left, right).astype(jnp.bfloat16)
-
             sums = jnp.sum(grad_qkv.astype(jnp.float32), 0)
             rows_of_vectors = jnp.stack(
                 [
@@ -879,8 +1015,8 @@
             return (
                 outer(normed.astype(jnp.bfloat16), grad_qkv),
                 outer(attn_mixed, grad_one),
-                outer(normed_two.astype(jnp.bfloat16), grad_pre),
-                outer(activated, grad_two),
+                first_sums[1],
+                first_sums[0],
                 rows_of_vectors,
                 jnp.sum(grad_pre.astype(jnp.float32), 0),
             )
@@ -888,18 +1024,18 @@
         return (grad_in, weight_grads)
 
     first_in = block_input[:, 0].reshape(micros * rows, width).astype(jnp.float32)
-    first_out, _ = forward(first_in)
+    first_out, weights, _ = forward(first_in, None)
+    proj_weight, up_weight, down_weight = weights
     arrived = lax.ppermute(first_out.astype(jnp.bfloat16), "pipe", [(0, 1)])
-    output, saved = forward(jnp.where(section == 0, first_in, arrived.astype(jnp.float32)))
-    last_grad, _ = backward(cotangent, saved)
+    output, _, saved = forward(
+        jnp.where(section == 0, first_in, arrived.astype(jnp.float32)), weights
+    )
+    last_grad, _ = backward(cotangent, saved, False)
     arrived = lax.ppermute(last_grad.astype(jnp.bfloat16), "pipe", [(1, 0)])
     grad_in, weight_grads = backward(
-        jnp.where(section == 1, cotangent, arrived.astype(jnp.float32)), saved
+        jnp.where(section == 1, cotangent, arrived.astype(jnp.float32)), saved, True
     )
-    grad_qkv, grad_proj, grad_up, grad_down, grad_vectors, grad_bias = weight_grads()
-
-    def shards(matrix):
-        return matrix.reshape(count, -1, 8, matrix.shape[-1])
+    grad_qkv, grad_proj, sum_up, sum_down, grad_vectors, grad_bias = weight_grads()
 
     small_grads = jnp.concatenate(
         [
@@ -909,16 +1045,14 @@
         ],
         1,
     ).reshape(count, RING, 8, width // count)
-    sums = sum_gradients(
-        [shards(grad_down), shards(grad_up), shards(grad_qkv), small_grads, shards(grad_proj)]
+    sum_qkv, small_sum, sum_proj = sum_gradients(
+        [shards(grad_qkv), small_grads, shards(grad_proj)]
     )
     totals = [
-        assemble(total, grad.shape[0] // count // 8)
-        for total, grad in zip(
-            (sums[2], sums[4], sums[1], sums[0]), (grad_qkv, grad_proj, grad_up, grad_down)
-        )
+        assemble(total, blocks)
+        for total, blocks in ((sum_qkv, 17), (sum_proj, 17), (sum_up, 17), (sum_down, 68))
     ]
-    small_total = sums[3].reshape(RING * 8, -1)
+    small_total = small_sum.reshape(RING * 8, -1)
     edges = jnp.where(section == 0, grad_in, output).reshape(1, micros, 1, rows, width)
     return (
         edges,

time: 677 us -> 722 us (1.066)
  Pallas kernels: 448 us -> 474 us
  local copies, waits for them, and re-layouts: 65.4 us -> 77.5 us
    pallas_call x6, Pallas kernels: 448 us -> 474 us  [the longest x2 187 us: attend_back(): pl.pallas_call(functools.partial(attend_back_kernel, len(sums)), out_shap...]
    convert_element_type x1, local copies, waits for them, and re-layouts: 5.57 us -> 14.1 us  [body(): out_grad[:, 0].astype(jnp.float32) * valid]
  transfers between devices with their start and end apart: 2 -> 2, of which waited for: 2 -> 1; matrix products, arithmetic and copies ran while one was open for 1% -> 2% of each run, Pallas kernels for 0% -> 0%
where the time goes in v2:
time: 722 us; the launch traced here: 713 us
  Pallas kernels  474 us (66%)
  matrix products  115 us (16%)
  local copies, waits for them, and re-layouts  77.5 us (11%)
  other arithmetic  23.8 us (3%)
  waiting for transfers between devices  13.8 us (2%)
    pallas_call x2, Pallas kernels, attend_back(): pl.pallas_call(functools.partial(attend_back_kernel, len(sums)), out_shap...  187 us
    pallas_call x2, Pallas kernels, attend(): pl.pallas_call(functools.partial(attend_kernel, plan, len(shards)), out_s...  148 us
    dot_general x14, matrix products, plain(): return jnp.dot(left, right, preferred_element_type=jnp.float32)  96.7 us
    pallas_call x1, Pallas kernels, sum_gradients(): pl.pallas_call(functools.partial(sum_kernel, count), out_shape=sum_shapes...  81.1 us
    pallas_call x1, Pallas kernels, gather_weights(): pl.pallas_call(functools.partial(gather_kernel, plan, count), out_shape=g...  57.5 us
    dot_general x4, matrix products, over_rows(): lax.dot_general(left, right, (((0,), (0,)), ((), ())), preferred_element_...  18.4 us
  transfers between devices with their start and end apart: 2, of which 1 were waited for; matrix products, arithmetic and copies ran while one was open for 2% of the time, Pallas kernels for 0%

profile of v2, /device:TPU:1, one launch (start us, length us, event | category | flops | bytes accessed | tf_op | source)
XLA Modules:
  0.0 712.8 jit_solution(8035555248051250626)
XLA Ops:
  0.6 0.8 reduce.4
  1.6 1.4 maximum_bitcast_fusion.5.refs_0_
  2.9 57.5 %gather_weights.1 = (bf16[8,2,8,136]{3,2,1,0:T(8,128)(2,1)}, bf16[8,17,8,3264]{3,2,1,0:T(8,128)(2,1)}) custom-call(bf16[2,8,136]{2,1,0:T(8,128)(2,1)} %maximum_bitcast_fusion.5.refs_0_, bf16[17,8,3264]{2,1,0:T(8,128)(2,1)} %bitcast.306), custom_call_target="tpu_custom_call" | custom-call | tf_op jit(solution)/shard_map/gather_weights/pallas_call | solution.py:242
  60.5 0.8 convert_bitcast_fusion
  62.9 6.5 fusion
  69.5 4.6 copy.74
  74.2 0.8 slice_convert_fusion
  77.5 1.3 pad_maximum_fusion.refs_1_
  79.8 110.6 %attend_gather.1 = (bf16[8,2,128,128]{3,2,1,0:T(8,128)(2,1)S(1)}, bf16[2,128,128]{2,1,0:T(8,128)(2,1)S(1)}, bf16[8,2,3,128,128]{4,3,2,1,0:T(8,128)(2,1)}, bf16[8...) custom-call(s32[2]{0:T(128)S(1)} %fusion.42.refs_0_, ...), custom_call_target="tpu_custom_call" | custom-call | tf_op jit(solution)/shard_map/attend_gather/pallas_call | solution.py:659
  191.2 3.0 fusion.74
  194.4 14.1 %fusion.18 = bf16[256,1088]{0,1:T(8,128)(2,1)} fusion(f32[256,1088]{0,1:T(8,128)S(1)} %get-tuple-element.140, bf16[4352,1088]{1,0:T(8,128)(2,1)} %bitcast.325, bf16[1088,4352]{1,0:T(8,128)(2,1)} %bitcast.267, f32[4352]{0:T(1024)S(1)} %reshape.504, f32[1088]{0:T(1024)S(1)} %add.240, f32[1088]{0:T(1024)S(1)} %add.232, f32[1088]{0:T(1024)S(1)} %mul.366, ...), kind=kOutput, calls=%fused_computation.44 | convolution fusion | flops 4861984768 | bytes 20643584 | tf_op jit(solution)/shard_map/dot_general | solution.py:522
  208.5 4.6 collective-permute-start
  213.1 14.1 %copy.63 = f32[2,1,128,1088]{2,0,3,1:T(2,128)} copy(bf16[2,1,128,1088]{2,3,1,0:T(8,128)(2,1)S(1)} %copy-done.26) | data formatting | bytes 1671168 | tf_op jit(solution)/shard_map/convert_element_type | solution.py:898
  227.3 1.1 copy.64
  228.9 7.0 fusion.1
  238.3 37.6 %attend.1 = (bf16[8,2,128,128]{3,2,1,0:T(8,128)(2,1)S(1)}, bf16[2,128,128]{2,1,0:T(8,128)(2,1)S(1)}, bf16[8,2,3,128,128]{4,3,2,1,0:T(8,128)(2,1)S(1)}, bf16[8,2,128,128]{3,2,1,0:T(8,128)(2,1)S(1)}) custom-call(s32[2]{0:T(128)S(1)} %fusion.42.refs_0_, bf16[8,2,3,128,128]{4,3,2,1,0:T(8,128)(2,1)S(1)} %pad_maximum_fusion.1.refs_1_, ...), custom_call_target="tpu_custom_call" | custom-call | tf_op jit(solution)/shard_map/attend/pallas_call | solution.py:659
  276.5 1.5 copy-done.10
  278.0 1.2 fusion.75
  279.5 9.2 %convolution_add_fusion = f32[256,4352]{1,0:T(8,128)} fusion(bf16[1088,4352]{1,0:T(8,128)(2,1)} %bitcast.268, f32[4352]{0:T(1024)S(1)} %reshape.504, f32[256,1088]{0,1:T(8,128)S(1)} %get-tuple-element.142, f32[256]{0:T(256)S(1)} %fusion.44, f32[256]{0:T(256)S(1)} %broadcast_multiply_fusion, f32[1088]{0:T(1024)S(1)} %add.232, f32[1088]{0:T(1024)S(1)} %mul.366), kind=kOutput, calls=%fused_computation.5 | convolution fusion | flops 2426814464 | bytes 15068672 | tf_op jit(solution)/shard_map/dot_general | solution.py:522
  288.7 12.9 %multiply_reduce_fusion.5 = (f32[256]{0:T(256)S(1)}, f32[256,1088]{0,1:T(8,128)}) fusion(f32[256,1088]{0,1:T(8,128)S(1)} %get-tuple-element.142, f32[256]{0:T(256)S(1)} %broadcast_multiply_fusion, f32[1088]{0:T(1024)S(1)} %mul.366, bf16[1088,4352]{1,0:T(8,128)(2,1)} %bitcast.269, f32[256,4352]{1,0:T(8,128)} %convolution_add_fusion, ...), kind=kOutput, calls=%fused_computation.74 | convolution fusion | flops 4872011776 | bytes 26188032 | tf_op jit(solution)/shard_map/dot_general | solution.py:522
  302.3 1.6 fusion.65
  304.0 3.0 convolution_convert_fusion.5
  307.1 0.8 copy-done.38
  308.8 37.1 %attend_back.1 = (bf16[8,2,3,128,128]{4,3,2,1,0:T(8,128)(2,1)S(1)}, bf16[2,128,128]{2,1,0:T(8,128)(2,1)S(1)}, bf16[2,128,128]{2,1,0:T(8,128)(2,1)S(1)}) custom-call(s32[2]{0:T(128)S(1)} %fusion.42.refs_0_, bf16[8,2,3,128,128]{4,3,2,1,0:T(8,128)(2,1)S(1)} %get-tuple-element.38.refs_1_, bf16[8,2,128,128]{3,2,1,0:T(8,128)(2,1)S(1)} %get-tuple-element.39.refs_2_, ...), custom_call_target="tpu_custom_call" | custom-call | tf_op jit(solution)/shard_map/attend_back/pallas_call | solution.py:823
  347.6 2.1 concatenate.46
  349.7 5.7 multiply_reduce_fusion.4
  356.3 0.9 copy-done.13
  357.6 1.2 add_convert_fusion.3
  358.8 1.3 collective-permute-start.1
  360.8 13.8 %collective-permute-done.1 = bf16[256,1088]{0,1:T(8,128)(2,1)S(1)} collective-permute-done((bf16[256,1088]{0,1:T(8,128)(2,1)}, bf16[256,1088]{0,1:T(8,128)(2,1)S(1)}, u32[]{:S(2)}, u32[]{:S(2)}) %collective-permute-start.1) | collective-permute-done | bytes 557088 | tf_op jit(solution)/shard_map/ppermute | solution.py:1034
  374.6 0.8 convert_reduce_fusion.2
  375.4 8.8 %convert_reduce_fusion = (f32[4352]{0:T(1024)}, bf16[256,4352]{1,0:T(8,128)(2,1)S(1)}) fusion(f32[256,4352]{1,0:T(8,128)} %convolution_add_fusion, bf16[256,1088]{0,1:T(8,128)(2,1)S(1)} %get-tuple-element.89, bf16[4352,1088]{1,0:T(8,128)(2,1)} %bitcast.327), kind=kOutput, calls=%fused_computation.25 | convolution fusion | flops 2448813824 | bytes 16729088 | tf_op jit(solution)/shard_map/dot_general | solution.py:522
  384.2 7.1 fusion.62
  391.3 1.2 multiply_reduce_fusion
  392.5 1.2 convert_reduce_fusion.3
  394.3 0.9 convolution_convert_fusion.4
  396.0 5.3 convolution_convert_fusion
  401.3 5.5 convolution_convert_fusion.1
  406.9 1.1 copy.92
  408.1 0.7 pad.17.refs_5_
  408.9 13.9 %copy.94 = bf16[4352,1088]{1,0:T(8,128)(2,1)} copy(bf16[4352,1088]{0,1:T(8,128)(2,1)} %convolution_convert_fusion) | data formatting | bytes 18939904 | tf_op jit(solution)/shard_map/convert_element_type | solution.py:952
  422.8 150.4 %attend_back_sum.1 = (bf16[8,2,3,128,128]{4,3,2,1,0:T(8,128)(2,1)}, bf16[2,128,128]{2,1,0:T(8,128)(2,1)}, bf16[2,128,128]{2,1,0:T(8,128)(2,1)}, bf16[4,17,8,1088]{3,2,1,0:T(8,128)(2,1)}, bf16[4,5,8,4352]{3,2,1,0:T(8,128)(2,1)}) custom-call(s32[2]{0:T(128)} %copy-done.6, bf16[8,2,3,128,128]{4,3,2,1,0:T(8,128)(2,1)} %copy-done, ...), custom_call_target="tpu_custom_call" | custom-call | tf_op jit(solution)/shard_map/attend_back_sum/pallas_call | solution.py:823
  573.2 1.5 slice_bitcast_fusion
  576.5 0.9 copy.152
  577.4 3.9 concatenate.47
  581.3 6.8 fusion.63
  588.1 5.2 convolution_convert_fusion.2
  593.5 0.8 copy-done.19
  594.6 2.4 convolution_convert_fusion.3
  597.3 2.4 multiply_reduce_fusion.1
  600.6 0.8 maximum_bitcast_fusion.4.refs_1_
  601.4 81.1 %sum_gradients.1 = (bf16[4,5,8,3264]{3,2,1,0:T(8,128)(2,1)}, f32[4,1,8,136]{3,2,1,0:T(8,128)}, bf16[4,5,8,1088]{3,2,1,0:T(8,128)(2,1)}) custom-call(bf16[8,17,8,3264]{3,2,1,0:T(8,128)(2,1)} %bitcast.265, f32[8,4,8,136]{3,2,1,0:T(8,128)} %maximum_bitcast_fusion.4.refs_1_, bf16[8,17,8,1088]{3,2,1,0:T(8,128)(2,1)} %bitcast.275), custom_call_target="tpu_custom_call" | custom-call | tf_op jit(solution)/shard_map/sum_gradients/pallas_call | solution.py:484
  682.6 1.8 slice_bitcast_fusion.14
  684.4 1.9 slice_bitcast_fusion.17
  687.7 0.8 slice_bitcast_fusion.6
  688.5 0.9 slice_bitcast_fusion.13
  689.4 10.6 %add_select_fusion = f32[256,1088]{0,1:T(8,128)} fusion(f32[256,1088]{0,1:T(8,128)S(1)} %copy-done.21, f32[256]{0:T(256)S(1)} %negate_multiply_fusion, f32[1088]{0:T(1024)S(1)} %copy-done.72, f32[256,1088]{0,1:T(8,128)S(1)} %copy-done.8, bf16[4352,1088]{1,0:T(8,128)(2,1)} %bitcast.328, pred[]{:T(512)S(6)} %eq.16, f32[256]{0:T(256)S(1)} %copy-done.75, ...), kind=kOutput, calls=%fused_computation.66 | convolution fusion | flops 2437398528 | bytes 19509760 | tf_op jit(solution)/shard_map/dot_general | solution.py:522
  700.1 1.8 reshape.495
  701.9 1.1 copy.98
  703.7 1.4 slice_bitcast_fusion.22
  706.5 1.4 fusion.26
  707.9 0.9 fusion.40
  709.3 1.6 fusion.25
  710.9 1.7 fusion.24
  (293 shorter events, 23.8 us)
Async XLA Ops:
  0.6 61.0 %copy-start.17 = (bf16[2,1,128,1088]{2,3,1,0:T(8,128)(2,1)S(1)}, bf16[2,1,128,1088]{2,3,1,0:T(8,128)(2,1)}, u32[]{:S(2)}) copy-start(bf16[2,1,128,1088]{2,3,1,0:T(8,128)(2,1)} %param.10) | copy-start | bytes 1671172
  61.5 167.4 %copy-start.49 = (f32[1088]{0:T(1024)}, f32[1088]{0:T(1024)S(1)}, u32[]{:S(2)}) copy-start(f32[1088]{0:T(1024)S(1)} %add.222) | copy-start | bytes 13060
  61.6 535.6 %copy-start.45 = (f32[1088]{0:T(1024)}, f32[1088]{0:T(1024)S(1)}, u32[]{:S(2)}) copy-start(f32[1088]{0:T(1024)S(1)} %mul.360) | copy-start | bytes 13060
  77.5 231.3 %copy-start.6 = (s32[2]{0:T(128)}, s32[2]{0:T(128)S(1)}, u32[]{:S(2)}) copy-start(s32[2]{0:T(128)S(1)} %fusion.42.refs_0_) | copy-start | bytes 28
  77.5 1.7 copy-start.2
  77.5 2.2 copy-start.3
  77.5 2.2 copy-start.5
  191.1 3.3 copy-start.71
  191.2 88.4 %copy-start.47 = (f32[1088]{0:T(1024)}, f32[1088]{0:T(1024)S(1)}, u32[]{:S(2)}) copy-start(f32[1088]{0:T(1024)S(1)} %add.232) | copy-start | bytes 13060
  194.3 18.8 %copy-start.26 = (bf16[2,1,128,1088]{2,3,1,0:T(8,128)(2,1)S(1)}, bf16[2,1,128,1088]{2,3,1,0:T(8,128)(2,1)}, u32[]{:S(2)}) copy-start(bf16[2,1,128,1088]{2,3,1,0:T(8,128)(2,1)} %param.11) | copy-start | bytes 1671172
  208.5 20.0 %collective-permute-start = (bf16[256,1088]{0,1:T(8,128)(2,1)}, bf16[256,1088]{0,1:T(8,128)(2,1)S(1)}, u32[]{:S(2)}, u32[]{:S(2)}) collective-permute-start(bf16[256,1088]{0,1:T(8,128)(2,1)} %fusion.18), channel_id=1, source_target_pairs={{0,64},{1,65},{2,66},{3,67},{4,68},{5,69},{6,70},{7,71},{8,72},{9,... | collective-permute-start | bytes 1671176 | tf_op jit(solution)/shard_map/ppermute | solution.py:1029
  228.4 75.5 %copy-start.67 = (f32[256]{0:T(256)}, f32[256]{0:T(256)S(1)}, u32[]{:S(2)}) copy-start(f32[256]{0:T(256)S(1)} %compare_convert_fusion.1) | copy-start | bytes 3076
  228.7 7.2 %copy-start.9 = (f32[256,1088]{0,1:T(8,128)}, f32[256,1088]{0,1:T(8,128)S(1)}, u32[]{:S(2)}) copy-start(f32[256,1088]{0,1:T(8,128)S(1)} %get-tuple-element.101) | copy-start | bytes 3342340
  228.7 7.2 %copy-start.56 = (f32[256]{0:T(256)}, f32[256]{0:T(256)S(1)}, u32[]{:S(2)}) copy-start(f32[256]{0:T(256)S(1)} %broadcast_multiply_fusion.1) | copy-start | bytes 3076
  228.9 7.0 copy-start.69
  228.9 7.0 copy-start.60
  238.1 70.7 %copy-start.4 = (bf16[2,128,128]{2,1,0:T(8,128)(2,1)}, bf16[2,128,128]{2,1,0:T(8,128)(2,1)S(1)}, u32[]{:S(2)}) copy-start(bf16[2,128,128]{2,1,0:T(8,128)(2,1)S(1)} %pad.15.refs_3_) | copy-start | bytes 196612
  238.3 38.2 %copy-start.15 = (bf16[8,17,8,1088]{3,2,1,0:T(8,128)(2,1)S(1)}, bf16[8,17,8,1088]{3,2,1,0:T(8,128)(2,1)}, u32[]{:S(2)}) copy-start(bf16[8,17,8,1088]{3,2,1,0:T(8,128)(2,1)} %get-tuple-element.34) | copy-start | bytes 7102468
  275.9 32.9 %copy-start = (bf16[8,2,3,128,128]{4,3,2,1,0:T(8,128)(2,1)}, bf16[8,2,3,128,128]{4,3,2,1,0:T(8,128)(2,1)S(1)}, u32[]{:S(2)}) copy-start(bf16[8,2,3,128,128]{4,3,2,1,0:T(8,128)(2,1)S(1)} %get-tuple-element.38.refs_1_) | copy-start | bytes 4718596
  275.9 32.9 %copy-start.1 = (bf16[8,2,128,128]{3,2,1,0:T(8,128)(2,1)}, bf16[8,2,128,128]{3,2,1,0:T(8,128)(2,1)S(1)}, u32[]{:S(2)}) copy-start(bf16[8,2,128,128]{3,2,1,0:T(8,128)(2,1)S(1)} %get-tuple-element.39.refs_2_) | copy-start | bytes 1572868
  275.9 2.1 copy-start.10
  276.5 2.8 copy-start.18
  279.3 23.0 %copy-start.7 = (f32[256,1088]{0,1:T(8,128)}, f32[256,1088]{0,1:T(8,128)S(1)}, u32[]{:S(2)}) copy-start(f32[256,1088]{0,1:T(8,128)S(1)} %get-tuple-element.142) | copy-start | bytes 3342340
  279.3 23.0 %copy-start.51 = (f32[256]{0:T(256)}, f32[256]{0:T(256)S(1)}, u32[]{:S(2)}) copy-start(f32[256]{0:T(256)S(1)} %broadcast_multiply_fusion) | copy-start | bytes 3076
  279.5 22.7 %copy-start.53 = (f32[256]{0:T(256)}, f32[256]{0:T(256)S(1)}, u32[]{:S(2)}) copy-start(f32[256]{0:T(256)S(1)} %fusion.44) | copy-start | bytes 3076
  303.9 3.1 copy-start.22
  303.9 3.1 copy-start.79
  347.5 2.2 copy-start.11
  347.6 2.1 copy-start.57
  349.7 5.7 copy-start.70
  349.7 6.3 copy-start.58
  349.7 6.3 copy-start.61
  358.8 15.8 %collective-permute-start.1 = (bf16[256,1088]{0,1:T(8,128)(2,1)}, bf16[256,1088]{0,1:T(8,128)(2,1)S(1)}, u32[]{:S(2)}, u32[]{:S(2)}) collective-permute-start(bf16[256,1088]{0,1:T(8,128)(2,1)} %add_convert_fusion.3), channel_id=1, source_target_pairs={{64,0},{65,1},{66,2},{67,3},{68,4},{69,5},{70,6},{71,7},{72,8},{73... | collective-permute-start | bytes 1671176 | tf_op jit(solution)/shard_map/ppermute | solution.py:1034
  375.4 8.8 %copy-start.8 = (f32[256,1088]{0,1:T(8,128)S(1)}, f32[256,1088]{0,1:T(8,128)}, u32[]{:S(2)}) copy-start(f32[256,1088]{0,1:T(8,128)} %copy-done.7) | copy-start | bytes 3342340
  375.4 8.8 %copy-start.52 = (f32[256]{0:T(256)S(1)}, f32[256]{0:T(256)}, u32[]{:S(2)}) copy-start(f32[256]{0:T(256)} %copy-done.51) | copy-start | bytes 3076
  384.2 7.1 copy-start.78
  384.2 7.1 copy-start.54
  392.5 1.7 copy-start.16
  392.5 3.4 slice-start
  395.2 6.1 copy-start.37
  396.0 5.3 copy-start.48
  581.3 6.8 copy-start.14
  581.3 6.8 copy-start.50
  594.6 2.5 copy-start.66
  594.6 2.6 copy-start.77
  597.2 2.5 copy-start.74
  597.2 2.8 copy-start.65
  597.2 2.9 copy-start.64
  597.3 3.0 copy-start.73
  597.3 3.1 copy-start.63
  597.3 3.3 copy-start.81
  682.6 3.8 copy-start.43
  682.6 5.1 copy-start.34
  687.6 1.7 copy-start.76
  687.6 1.8 copy-start.29
  687.6 1.8 copy-start.46
  687.7 1.8 copy-start.59
  687.7 1.8 copy-start.62
  687.7 1.8 copy-start.72
  687.7 1.8 copy-start.75
  703.6 2.9 copy-start.33
  703.6 2.9 copy-start.35
  703.6 2.9 copy-start.36
  706.5 2.3 copy-start.32
  (26 other events, 32.9 us)

commit v3 on v1

--- a/solution.py
+++ b/solution.py
@@ -435,6 +435,20 @@
     return jnp.dot(left, right, preferred_element_type=jnp.float32)
 
 
+def half_selector(first):
+    rows = lax.broadcasted_iota(jnp.int32, (HEAD, LANES), 0)
+    lanes = lax.broadcasted_iota(jnp.int32, (HEAD, LANES), 1)
+    return (rows + first == lanes).astype(jnp.bfloat16)
+
+
+def widen(matrix, first):
+    return plain(matrix, half_selector(first)).astype(jnp.bfloat16)
+
+
+def narrow(matrix, first):
+    return over_lanes(matrix, half_selector(first)).astype(jnp.bfloat16)
+
+
 def soft_columns(key_rows, queries, first_query, length):
     scores = over_lanes(key_rows, queries) * HEAD ** (-0.5)
     key_pos = lax.broadcasted_iota(jnp.int32, scores.shape, 0)
@@ -447,16 +461,61 @@
 def peers(count):
     member = lax.axis_index("group")
     ahead = [(member + j) % count for j in range(1, count)]
-    behind = [(member + count - j) % count for j in range(1, count)]
-    return (member, ahead, behind)
-
-
-def attend_kernel(
-    lengths, pack, last_kv, last_q, mixed, last_mixed, kept, kept_last,
-    held, held_last, staged, send, recv, send_last, recv_last, send_back, recv_back, local,
+    return (member, ahead)
+
+
+def normalize(inputs):
+    average = jnp.mean(inputs, -1, keepdims=True)
+    centered = inputs - average
+    variance = jnp.mean(centered * centered, -1, keepdims=True)
+    scale = lax.rsqrt(variance + EPSILON)
+    return (centered * scale, scale)
+
+
+def norm_back(unit, scale, gain, grad):
+    scaled = grad * gain
+    pulled = scaled - jnp.mean(scaled, -1, keepdims=True)
+    pulled = pulled - unit * jnp.mean(scaled * unit, -1, keepdims=True)
+    return (
+        pulled * scale,
+        jnp.sum(grad * unit, 0, keepdims=True),
+        jnp.sum(grad, 0, keepdims=True),
+    )
+
+
+GELU_IN, GELU_CUBE = 0.7978845608028654, 0.044715
+
+
+def gelu_parts(value):
+    square = value * value
+    bent = jnp.tanh(GELU_IN * value * (1.0 + GELU_CUBE * square))
+    half = 0.5 * (1.0 + bent)
+    slope = half + 0.5 * value * (1.0 - bent * bent) * GELU_IN * (1.0 + 3.0 * GELU_CUBE * square)
+    return (value * half, slope)
+
+
+def column_chunks(width, most):
+    return [(first, min(most, width - first)) for first in range(0, width, most)]
+
+
+FORWARD_WEIGHTS = ("q", "k", "v", "proj", "up", "down")
+
+
+def forward_kernel(
+    lengths, inputs, vectors, up_bias, wq, wk, wv, wproj, wup, wdown,
+    output, hidden_out, pre_act, attn_mixed, last_q, kept, kept_last,
+    vq, vk, vv, vproj, vup, vdown, pack, last_kv, held, held_last, staged, mixed,
+    send, recv, send_last, recv_last, send_back, recv_back, local, loaded,
 ):
     count, micros, _, rows, lanes = pack.shape
-    member, ahead, behind = peers(count)
+    member, ahead = peers(count)
+    wide = count * lanes
+    sources, places = (wq, wk, wv, wproj, wup, wdown), (vq, vk, vv, vproj, vup, vdown)
+    loads = [
+        pltpu.make_async_copy(sources[i], places[i], loaded.at[i]) for i in range(len(sources))
+    ]
+    for load in loads:
+        load.start()
     greet([{"group": peer} for peer in ahead])
 
     def out(m, j):
@@ -498,6 +557,24 @@
         )
 
     peer_range = range(count - 1)
+    unit, _ = normalize(inputs[...])
+    normed = (unit * vectors[0:1] + vectors[1:2]).astype(jnp.bfloat16)
+    lasts = []
+    for third, (weight, bias) in enumerate(((vq, 2), (vk, None), (vv, 3))):
+        loads[third].wait()
+        product = plain(normed, weight[...])
+        if bias is not None:
+            product = product + vectors[bias : bias + 1]
+        product = product.astype(jnp.bfloat16)
+        for d in range(count):
+            for m in range(micros):
+                pack[d, m, third] = product[m * rows : (m + 1) * rows, d * lanes : (d + 1) * lanes]
+        lasts.append(product[:, wide:])
+    wide_q = widen(lasts[0], 0)
+    both_last = widen(lasts[1], 0) + widen(lasts[2], HEAD)
+    for m in range(micros):
+        last_q[m] = wide_q[m * rows : (m + 1) * rows]
+        last_kv[m] = both_last[m * rows : (m + 1) * rows]
     for m in range(micros):
         for j in peer_range:
             out(m, j).start()
@@ -505,89 +582,140 @@
         for copy in own(m):
             copy.start()
 
-    def micro(m, carry):
+    def micro(m):
         for copy in own(m):
             copy.wait()
         for j in peer_range:
             out(m, j).wait_recv()
             out_last(m, j).wait_recv()
         length = lengths[m]
-        wide = 2
-        for block in range(count // wide):
-            reach = wide * (block + 1)
-            queries = held[wide * block : reach, m, 0].reshape(wide * rows, lanes)
+        span = 2
+        for block in range(count // span):
+            reach = span * (block + 1)
+            queries = held[span * block : reach, m, 0].reshape(span * rows, lanes)
             key_rows = held[0:reach, m, 1].reshape(reach * rows, lanes)
             values = held[0:reach, m, 2].reshape(reach * rows, lanes)
 
             def head_step(head, total):
                 probs = soft_columns(
-                    key_rows, one_head(queries, head), wide * block * rows, length
+                    key_rows, one_head(queries, head), span * block * rows, length
                 ).astype(jnp.bfloat16)
                 return total + over_rows(one_head(values, head), probs)
 
-            total = lax.fori_loop(0, 2, head_step, jnp.zeros((lanes, wide * rows), jnp.float32))
-            staged[wide * block : reach, m] = (
-                total.T.astype(jnp.bfloat16).reshape(wide, rows, lanes)
+            total = lax.fori_loop(0, 2, head_step, jnp.zeros((lanes, span * rows), jnp.float32))
+            staged[span * block : reach, m] = (
+                total.T.astype(jnp.bfloat16).reshape(span, rows, lanes)
             )
         for j in peer_range:
             back(m, j).start()
         own_back(m).start()
         both = held_last[:, m].reshape(count * rows, lanes)
         probs = soft_columns(both, last_q[m], member * rows, length).astype(jnp.bfloat16)
-        last_mixed[m] = over_rows(both, probs).T.astype(jnp.bfloat16)
-        return carry
-
-    lax.fori_loop(0, micros, micro, 0)
+        last_out = over_rows(both, probs).T.astype(jnp.bfloat16)
+        attn_mixed[m * rows : (m + 1) * rows, wide:] = narrow(last_out, HEAD)
+
+    for m in range(micros):
+        micro(m)
     for copy in keep():
         copy.start()
     for m in range(micros):
         own_back(m).wait()
         for j in peer_range:
+            back(m, j).wait_recv()
+        for d in range(count):
+            attn_mixed[m * rows : (m + 1) * rows, d * lanes : (d + 1) * lanes] = mixed[d, m]
+    loads[3].wait()
+    hidden = inputs[...] + plain(attn_mixed[...], vproj[...]) + vectors[4:5]
+    hidden_out[...] = hidden
+    unit, _ = normalize(hidden)
+    normed = (unit * vectors[5:6] + vectors[6:7]).astype(jnp.bfloat16)
+    output[...] = hidden + vectors[7:8]
+    loads[4].wait()
+    for first, size in column_chunks(pre_act.shape[1], 1152):
+        columns = slice(first, first + size)
+        value = plain(normed, vup[:, columns]) + up_bias[:, columns]
+        pre_act[:, columns] = value
+        activated, _ = gelu_parts(value)
+        if first == 0:
+            loads[5].wait()
+        output[...] += plain(activated.astype(jnp.bfloat16), vdown[columns, :])
+    for m in range(micros):
+        for j in peer_range:
             out(m, j).wait_send()
             out_last(m, j).wait_send()
-            back(m, j).wait()
+            back(m, j).wait_send()
     for copy in keep():
         copy.wait()
 
 
-def attend(lengths, pack, last_kv, last_q):
-    count, micros, _, rows, lanes = pack.shape
-    bf16 = jnp.bfloat16
+def forward_layer(lengths, inputs, vectors, up_bias, weights, count, micros):
+    total, width = inputs.shape
+    rows, lanes = total // micros, LANES
+    hidden = weights[4].shape[1]
+    bf16, f32 = jnp.bfloat16, jnp.float32
     vmem, hbm = pl.BlockSpec(memory_space=pltpu.VMEM), pl.BlockSpec(memory_space=pl.ANY)
     dma = pltpu.SemaphoreType.DMA
+    pack, blocks = (count, micros, 3, rows, lanes), (count, micros, rows, lanes)
     return pl.pallas_call(
-        attend_kernel,
+        forward_kernel,
         out_shape=[
-            jax.ShapeDtypeStruct((count, micros, rows, lanes), bf16),
+            jax.ShapeDtypeStruct((total, width), f32),
+            jax.ShapeDtypeStruct((total, width), f32),
+            jax.ShapeDtypeStruct((total, hidden), f32),
+            jax.ShapeDtypeStruct((total, width), bf16),
             jax.ShapeDtypeStruct((micros, rows, lanes), bf16),
-            jax.ShapeDtypeStruct(pack.shape, bf16),
-            jax.ShapeDtypeStruct((count, micros, rows, lanes), bf16),
+            jax.ShapeDtypeStruct(pack, bf16),
+            jax.ShapeDtypeStruct(blocks, bf16),
         ],
-        in_specs=[pl.BlockSpec(memory_space=pltpu.SMEM), hbm, vmem, vmem],
-        out_specs=[hbm, vmem, hbm, hbm],
-        scratch_shapes=[
-            pltpu.VMEM(pack.shape, bf16),
-            pltpu.VMEM((count, micros, rows, lanes), bf16),
-            pltpu.VMEM((count, micros, rows, lanes), bf16),
+        in_specs=[pl.BlockSpec(memory_space=pltpu.SMEM)] + [vmem] * 3 + [hbm] * 6,
+        out_specs=[vmem] * 5 + [hbm] * 2,
+        scratch_shapes=[pltpu.VMEM(w.shape, bf16) for w in weights]
+        + [
+            pltpu.VMEM(pack, bf16),
+            pltpu.VMEM((micros, rows, lanes), bf16),
+            pltpu.VMEM(pack, bf16),
+            pltpu.VMEM(blocks, bf16),
+            pltpu.VMEM(blocks, bf16),
+            pltpu.VMEM(blocks, bf16),
         ]
         + [dma((micros, count - 1))] * 6
-        + [dma((micros, 4))],
+        + [dma((micros, 4)), dma((6,))],
         compiler_params=pltpu.CompilerParams(
-            collective_id=2, has_side_effects=True, vmem_limit_bytes=48 * 1024 * 1024
+            collective_id=2, has_side_effects=True, vmem_limit_bytes=60 * 1024 * 1024
         ),
-        name="attend",
-    )(lengths, pack, last_kv, last_q)
-
-
-def attend_back_kernel(
-    lengths, held, held_last, last_q, grad_pack, last_grad, grads, last_key_grad, last_query_grad,
-    came, staged, staged_last, parts_last, key_total, value_total,
-    send, recv, send_back, recv_back, send_last, recv_last, local,
+        name="forward_layer",
+    )(lengths, inputs, vectors, up_bias, *weights)
+
+
+def backward_kernel(
+    lengths, grad_output, inputs, hidden, vectors, pre_act, held, held_last, last_q,
+    wq, wk, wv, wproj, wup, wdown,
+    grad_in, grad_q, grad_k, grad_v, grad_one, grad_pre, activated, normed_one, normed_two,
+    vector_grads, bias_grads,
+    vproj, vup, vdown, vqkv, grad_norm, grad_pack, last_grad, came, staged, staged_last, grads, parts_last,
+    key_total, value_total, last_query_grad,
+    send, recv, send_back, recv_back, send_last, recv_last, local, loaded,
 ):
     count, micros, _, rows, lanes = held.shape
-    member, ahead, behind = peers(count)
+    member, ahead = peers(count)
+    wide = count * lanes
+    scale = HEAD ** (-0.5)
+    loads = [
+        pltpu.make_async_copy(source, target, loaded.at[i])
+        for i, (source, target) in enumerate(
+            (
+                (wdown, vdown),
+                (wup, vup),
+                (wproj, vproj),
+                (wq, vqkv.at[0]),
+                (wk, vqkv.at[1]),
+                (wv, vqkv.at[2]),
+            )
+        )
+    ]
+    for load in loads:
+        load.start()
     greet([{"group": peer} for peer in ahead])
-    scale = HEAD ** (-0.5)
 
     def out(m, j):
         return remote(
@@ -627,42 +755,81 @@
             ),
         )
 
+    def column_sum(matrix):
+        return jnp.sum(matrix.astype(jnp.float32), 0, keepdims=True)
+
     peer_range = range(count - 1)
+    grad_two = grad_output[...].astype(jnp.bfloat16)
+    vector_grads[7:8] = column_sum(grad_two)
+    loads[0].wait()
+    for first, size in column_chunks(pre_act.shape[1], 1152):
+        columns = slice(first, first + size)
+        value, slope = gelu_parts(pre_act[:, columns])
+        activated[:, columns] = value.astype(jnp.bfloat16)
+        part = (slope * over_lanes(grad_two, vdown[columns, :])).astype(jnp.bfloat16)
+        grad_pre[:, columns] = part
+        bias_grads[:, columns] = column_sum(part)
+        if first == 0:
+            loads[1].wait()
+            grad_norm[...] = over_lanes(part, vup[:, columns])
+        else:
+            grad_norm[...] += over_lanes(part, vup[:, columns])
+    unit, deviation = normalize(hidden[...])
+    normed_two[...] = (unit * vectors[5:6] + vectors[6:7]).astype(jnp.bfloat16)
+    from_norm, gain_sum, bias_sum = norm_back(unit, deviation, vectors[5:6], grad_norm[...])
+    vector_grads[5:6] = gain_sum
+    vector_grads[6:7] = bias_sum
+    grad_hidden = grad_output[...] + from_norm
+    grad_norm[...] = grad_hidden
+    one = grad_hidden.astype(jnp.bfloat16)
+    grad_one[...] = one
+    vector_grads[4:5] = column_sum(one)
+    loads[2].wait()
+    grad_mixed = over_lanes(one, vproj[...]).astype(jnp.bfloat16)
     for m in range(micros):
+        for d in range(count):
+            grad_pack[d, m] = grad_mixed[m * rows : (m + 1) * rows, d * lanes : (d + 1) * lanes]
         for j in peer_range:
             out(m, j).start()
         own(m).start()
-
-    def micro(m, carry):
+    wide_last = widen(grad_mixed[:, wide:], HEAD)
+    for m in range(micros):
+        last_grad[m] = wide_last[m * rows : (m + 1) * rows]
+
+    def last_head(m):
         length = lengths[m]
         both = held_last[:, m].reshape(count * rows, lanes)
         probs = soft_columns(both, last_q[m], member * rows, length)
         grad_probs = over_lanes(both, last_grad[m])
         inner = jnp.sum(probs * grad_probs, 0, keepdims=True)
         grad_scores = (probs * (grad_probs - inner)).astype(jnp.bfloat16)
-        last_query_grad[m] = (scale * over_rows(both, grad_scores)).T.astype(jnp.bfloat16)
+        query_grad = (scale * over_rows(both, grad_scores)).T.astype(jnp.bfloat16)
+        grad_q[m * rows : (m + 1) * rows, wide:] = narrow(query_grad, 0)
         both_grad = scale * plain(grad_scores, last_q[m]) + plain(
             probs.astype(jnp.bfloat16), last_grad[m]
         )
         staged_last[:, m] = both_grad.astype(jnp.bfloat16).reshape(count, rows, lanes)
         for j in peer_range:
             back_last(m, j).start()
+
+    def micro(m):
+        length = lengths[m]
         own(m).wait()
         for j in peer_range:
             out(m, j).wait_recv()
         key_total[...] = jnp.zeros_like(key_total)
         value_total[...] = jnp.zeros_like(value_total)
-        wide = 2
-        for block in range(count // wide):
-            reach = wide * (block + 1)
-            queries = held[wide * block : reach, m, 0].reshape(wide * rows, lanes)
-            grad_out = came[wide * block : reach, m].reshape(wide * rows, lanes)
+        span = 2
+        for block in range(count // span):
+            reach = span * (block + 1)
+            queries = held[span * block : reach, m, 0].reshape(span * rows, lanes)
+            grad_out = came[span * block : reach, m].reshape(span * rows, lanes)
             key_rows = held[0:reach, m, 1].reshape(reach * rows, lanes)
             values = held[0:reach, m, 2].reshape(reach * rows, lanes)
 
             def head_step(head, total):
                 head_queries, head_grad = one_head(queries, head), one_head(grad_out, head)
-                probs = soft_columns(key_rows, head_queries, wide * block * rows, length)
+                probs = soft_columns(key_rows, head_queries, span * block * rows, length)
                 grad_probs = over_lanes(values, head_grad)
                 inner = jnp.sum(probs * grad_probs, 0, keepdims=True)
                 grad_scores = (probs * (grad_probs - inner)).astype(jnp.bfloat16)
@@ -670,9 +837,9 @@
                 key_total[0 : reach * rows] += plain(grad_scores, head_queries)
                 return total + over_rows(one_head(key_rows, head), grad_scores)
 
-            total = lax.fori_loop(0, 2, head_step, jnp.zeros((lanes, wide * rows), jnp.float32))
-            staged[wide * block : reach, m, 0] = (
-                (scale * total).T.astype(jnp.bfloat16).reshape(wide, rows, lanes)
+            total = lax.fori_loop(0, 2, head_step, jnp.zeros((lanes, span * rows), jnp.float32))
+            staged[span * block : reach, m, 0] = (
+                (scale * total).T.astype(jnp.bfloat16).reshape(span, rows, lanes)
             )
         staged[:, m, 1] = (scale * key_total[...]).astype(jnp.bfloat16).reshape(count, rows, lanes)
         staged[:, m, 2] = value_total[...].astype(jnp.bfloat16).reshape(count, rows, lanes)
@@ -680,71 +847,130 @@
             back(m, j).start()
         for copy in own_back(m):
             copy.start()
-        return carry
-
-    lax.fori_loop(0, micros, micro, 0)
+
     for m in range(micros):
+        last_head(m)
+    for m in range(micros):
+        micro(m)
+    unit, deviation = normalize(inputs[...])
+    normed_one[...] = (unit * vectors[0:1] + vectors[1:2]).astype(jnp.bfloat16)
+    for m in range(micros):
+        here = slice(m * rows, (m + 1) * rows)
         for copy in own_back(m):
             copy.wait()
         for j in peer_range:
             back_last(m, j).wait_recv()
-        last_key_grad[m] = jnp.sum(parts_last[:, m].astype(jnp.float32), 0).astype(jnp.bfloat16)
+            back(m, j).wait_recv()
+        last = jnp.sum(parts_last[:, m].astype(jnp.float32), 0).astype(jnp.bfloat16)
+        grad_k[here, wide:] = narrow(last, 0)
+        grad_v[here, wide:] = narrow(last, HEAD)
+        for third, target in enumerate((grad_q, grad_k, grad_v)):
+            for d in range(count):
+                target[here, d * lanes : (d + 1) * lanes] = grads[d, m, third]
+    vector_grads[2:3] = column_sum(grad_q[...])
+    vector_grads[3:4] = column_sum(grad_v[...])
+    for i in (3, 4, 5):
+        loads[i].wait()
+    pulled = over_lanes(grad_q[...], vqkv[0])
+    pulled += over_lanes(grad_k[...], vqkv[1])
+    pulled += over_lanes(grad_v[...], vqkv[2])
+    from_norm, gain_sum, bias_sum = norm_back(unit, deviation, vectors[0:1], pulled)
+    vector_grads[0:1] = gain_sum
+    vector_grads[1:2] = bias_sum
+    grad_in[...] = grad_norm[...] + from_norm
     for m in range(micros):
         for j in peer_range:
             out(m, j).wait_send()
             back_last(m, j).wait_send()
-            back(m, j).wait()
-
-
-def attend_back(lengths, held, held_last, last_q, grad_pack, last_grad):
+            back(m, j).wait_send()
+
+
+def backward_layer(lengths, grad_output, saved, vectors, weights):
+    inputs, hidden, pre_act, held, held_last, last_q = saved
     count, micros, _, rows, lanes = held.shape
-    bf16 = jnp.bfloat16
+    total, width = inputs.shape
+    bf16, f32 = jnp.bfloat16, jnp.float32
     vmem, hbm = pl.BlockSpec(memory_space=pltpu.VMEM), pl.BlockSpec(memory_space=pl.ANY)
     dma = pltpu.SemaphoreType.DMA
+    narrow_out, wide_out = (total, width), pre_act.shape
+    blocks, pack = (count, micros, rows, lanes), (count, micros, 3, rows, lanes)
     return pl.pallas_call(
-        attend_back_kernel,
+        backward_kernel,
         out_shape=[
-            jax.ShapeDtypeStruct(held.shape, bf16),
-            jax.ShapeDtypeStruct((micros, rows, lanes), bf16),
-            jax.ShapeDtypeStruct((micros, rows, lanes), bf16),
+            jax.ShapeDtypeStruct(shape, dtype)
+            for shape, dtype in (
+                (narrow_out, f32),
+                (narrow_out, bf16),
+                (narrow_out, bf16),
+                (narrow_out, bf16),
+                (narrow_out, bf16),
+                (wide_out, bf16),
+                (wide_out, bf16),
+                (narrow_out, bf16),
+                (narrow_out, bf16),
+                ((8, width), f32),
+                ((1, pre_act.shape[1]), f32),
+            )
         ],
-        in_specs=[pl.BlockSpec(memory_space=pltpu.SMEM), vmem, vmem, vmem, hbm, vmem],
-        out_specs=[hbm, vmem, vmem],
+        in_specs=[pl.BlockSpec(memory_space=pltpu.SMEM)] + [vmem] * 8 + [hbm] * 6,
+        out_specs=[vmem] * 11,
         scratch_shapes=[
-            pltpu.VMEM((count, micros, rows, lanes), bf16),
-            pltpu.VMEM(held.shape, bf16),
-            pltpu.VMEM((count, micros, rows, lanes), bf16),
-            pltpu.VMEM((count, micros, rows, lanes), bf16),
-            pltpu.VMEM((count * rows, lanes), jnp.float32),
-            pltpu.VMEM((count * rows, lanes), jnp.float32),
+            pltpu.VMEM(weights[3].shape, bf16),
+            pltpu.VMEM(weights[4].shape, bf16),
+            pltpu.VMEM(weights[5].shape, bf16),
+            pltpu.VMEM((3,) + weights[0].shape, bf16),
+            pltpu.VMEM(narrow_out, f32),
+            pltpu.VMEM(blocks, bf16),
+            pltpu.VMEM((micros, rows, lanes), bf16),
+            pltpu.VMEM(blocks, bf16),
+            pltpu.VMEM(pack, bf16),
+            pltpu.VMEM(blocks, bf16),
+            pltpu.VMEM(pack, bf16),
+            pltpu.VMEM(blocks, bf16),
+            pltpu.VMEM((count * rows, lanes), f32),
+            pltpu.VMEM((count * rows, lanes), f32),
+            pltpu.VMEM((micros, rows, lanes), bf16),
         ]
         + [dma((micros, count - 1))] * 6
-        + [dma((micros, 3))],
+        + [dma((micros, 3)), dma((6,))],
         compiler_params=pltpu.CompilerParams(
-            collective_id=3, has_side_effects=True, vmem_limit_bytes=48 * 1024 * 1024
+            collective_id=3, has_side_effects=True, vmem_limit_bytes=62 * 1024 * 1024
         ),
-        name="attend_back",
-    )(lengths, held, held_last, last_q, grad_pack, last_grad)
-
-
-def norm_rows(inputs, gain_row, bias_row):
-    average = jnp.mean(inputs, -1, keepdims=True)
-    centered = inputs - average
-    variance = jnp.mean(centered * centered, -1, keepdims=True)
-    return centered * lax.rsqrt(variance + EPSILON) * gain_row + bias_row
-
-
-def gelu_tanh(inputs):
-    return jax.nn.gelu(inputs, approximate=True)
-
-
-def by_heads(matrix, micros, rows, count):
-    return matrix.reshape(micros, rows, count, LANES).transpose(2, 0, 1, 3)
-
-
-def by_rows(blocks):
-    count, micros, rows, lanes = blocks.shape
-    return blocks.transpose(1, 2, 0, 3).reshape(micros * rows, count * lanes)
+        name="backward_layer",
+    )(lengths, grad_output, inputs, hidden, vectors, pre_act, held, held_last, last_q, *weights)
+
+
+def outer_kernel(left, right, out):
+    out[...] = over_rows(left[...], right[...]).astype(out.dtype)
+
+
+def outer(left, right):
+    rows, height = left.shape
+    width = right.shape[1]
+    tile = 256
+    if height > width:
+        grid = pl.cdiv(height, tile)
+        specs = [
+            pl.BlockSpec((rows, tile), lambda i: (0, i)),
+            pl.BlockSpec((rows, width), lambda i: (0, 0)),
+        ]
+        out_spec = pl.BlockSpec((tile, width), lambda i: (i, 0))
+    else:
+        grid = pl.cdiv(width, tile)
+        specs = [
+            pl.BlockSpec((rows, height), lambda i: (0, 0)),
+            pl.BlockSpec((rows, tile), lambda i: (0, i)),
+        ]
+        out_spec = pl.BlockSpec((height, tile), lambda i: (0, i))
+    return pl.pallas_call(
+        outer_kernel,
+        grid=(grid,),
+        out_shape=jax.ShapeDtypeStruct((height, width), jnp.bfloat16),
+        in_specs=specs,
+        out_specs=out_spec,
+        compiler_params=pltpu.CompilerParams(vmem_limit_bytes=32 * 1024 * 1024),
+        name="outer",
+    )(left, right)
 
 
 def in_blocks(matrix):
@@ -760,7 +986,6 @@
     rep_count = lax.axis_size("rep")
     count = lax.axis_size("group")
     micros, rows, width = block_input.shape[0], block_input.shape[2], block_input.shape[3]
-    wide = count * LANES
     slot_ids = jnp.arange(seq_lengths.shape[0], dtype=jnp.int32)
     slot_len = jnp.sum(
         seq_lengths[:, None] * (slot_of_seq[:, None] == slot_ids[None, :]).astype(jnp.int32), axis=0
@@ -782,121 +1007,30 @@
         ],
         0,
     )
-    full = gather_weights(
-        [
-            in_blocks(small),
-            in_blocks(w_qkv[0]),
-            in_blocks(w_proj[0]),
-            in_blocks(w_up[0]),
-            in_blocks(w_down[0]),
-        ]
+    thirds = [w_qkv[0][:, i * width : (i + 1) * width] for i in range(3)]
+    small_full, *full = gather_weights(
+        [in_blocks(array) for array in (small, *thirds, w_proj[0], w_up[0], w_down[0])]
     )
-    vector_rows = full[0][:, 0].transpose(1, 0, 2).reshape(8, width).astype(jnp.float32)
-    up_bias = full[0][:, 1, :bias_rows].reshape(-1).astype(jnp.float32)
-    qkv_weight, proj_weight, up_weight, down_weight = (
-        array.reshape(-1, array.shape[-1]) for array in full[1:]
-    )
-    qkv_bias = jnp.concatenate([vector_rows[2], jnp.zeros_like(vector_rows[2]), vector_rows[3]])
-
-    def pad_last(matrix, before):
-        block = matrix.reshape(micros, rows, HEAD)
-        return jnp.pad(block, ((0, 0), (0, 0), (before, LANES - HEAD - before)))
+    vector_rows = small_full[:, 0].transpose(1, 0, 2).reshape(8, width).astype(jnp.float32)
+    up_bias = small_full[:, 1, :bias_rows].reshape(1, -1).astype(jnp.float32)
+    weights = [array.reshape(-1, array.shape[-1]) for array in full]
 
     def forward(inputs):
-        normed = norm_rows(inputs, vector_rows[0], vector_rows[1]).astype(jnp.bfloat16)
-        qkv = (plain(normed, qkv_weight) + qkv_bias).astype(jnp.bfloat16)
-        thirds = [qkv[:, i * width : (i + 1) * width] for i in range(3)]
-        pack = jnp.stack([by_heads(t[:, :wide], micros, rows, count) for t in thirds], 2)
-        last_kv = jnp.concatenate([thirds[1][:, wide:], thirds[2][:, wide:]], 1).reshape(
-            micros, rows, LANES
-        )
-        last_q = pad_last(thirds[0][:, wide:], 0)
-        mixed, last_mixed, held, held_last = attend(lengths, pack, last_kv, last_q)
-        attn_mixed = jnp.concatenate(
-            [by_rows(mixed), last_mixed[:, :, HEAD:].reshape(micros * rows, HEAD)], 1
-        )
-        hidden = inputs + plain(attn_mixed, proj_weight) + vector_rows[4]
-        normed_two = norm_rows(hidden, vector_rows[5], vector_rows[6]).astype(jnp.bfloat16)
-        pre_act = plain(normed_two, up_weight) + up_bias
-        activated = gelu_tanh(pre_act).astype(jnp.bfloat16)
-        output = hidden + plain(activated, down_weight) + vector_rows[7]
-        return (output, (inputs, held, held_last, last_q, attn_mixed, hidden, pre_act, activated))
-
-    def backward(grad_output, saved):
-        inputs, held, held_last, last_q, attn_mixed, hidden, pre_act, activated = saved
-        grad_two = grad_output.astype(jnp.bfloat16)
-        grad_act = plain(grad_two, down_weight.T)
-        grad_pre = jax.vjp(gelu_tanh, pre_act)[1](grad_act)[0].astype(jnp.bfloat16)
-        normed_two, pull_two = jax.vjp(norm_rows, hidden, vector_rows[5], vector_rows[6])
-        from_norm, gain_two, shift_two = pull_two(plain(grad_pre, up_weight.T))
-        grad_hidden = grad_output + from_norm
-        grad_one = grad_hidden.astype(jnp.bfloat16)
-        grad_mixed = plain(grad_one, proj_weight.T).astype(jnp.bfloat16)
-        grads, last_key_grad, last_query_grad = attend_back(
-            lengths,
-            held,
-            held_last,
-            last_q,
-            by_heads(grad_mixed[:, :wide], micros, rows, count),
-            pad_last(grad_mixed[:, wide:], HEAD),
-        )
-
-        def last(block, first):
-            return block[:, :, first : first + HEAD].reshape(micros * rows, HEAD)
-
-        grad_qkv = jnp.concatenate(
-            [
-                by_rows(grads[:, :, 0]),
-                last(last_query_grad, 0),
-                by_rows(grads[:, :, 1]),
-                last(last_key_grad, 0),
-                by_rows(grads[:, :, 2]),
-                last(last_key_grad, HEAD),
-            ],
-            1,
-        )
-        normed, pull = jax.vjp(norm_rows, inputs, vector_rows[0], vector_rows[1])
-        from_norm, gain, shift = pull(plain(grad_qkv, qkv_weight.T))
-        grad_in = grad_hidden + from_norm
-
-        def weight_grads():
-            def outer(left, right):
-                return over_rows(left, right).astype(jnp.bfloat16)
-
-            sums = jnp.sum(grad_qkv.astype(jnp.float32), 0)
-            rows_of_vectors = jnp.stack(
-                [
-                    gain,
-                    shift,
-                    sums[:width],
-                    sums[2 * width :],
-                    jnp.sum(grad_one.astype(jnp.float32), 0),
-                    gain_two,
-                    shift_two,
-                    jnp.sum(grad_two.astype(jnp.float32), 0),
-                ]
-            )
-            return (
-                outer(normed.astype(jnp.bfloat16), grad_qkv),
-                outer(attn_mixed, grad_one),
-                outer(normed_two.astype(jnp.bfloat16), grad_pre),
-                outer(activated, grad_two),
-                rows_of_vectors,
-                jnp.sum(grad_pre.astype(jnp.float32), 0),
-            )
-
-        return (grad_in, weight_grads)
+        return forward_layer(lengths, inputs, vector_rows, up_bias, weights, count, micros)
 
     first_in = block_input[:, 0].reshape(micros * rows, width).astype(jnp.float32)
-    first_out, _ = forward(first_in)
+    first_out = forward(first_in)[0]
     arrived = lax.ppermute(first_out.astype(jnp.bfloat16), "pipe", [(0, 1)])
-    output, saved = forward(jnp.where(section == 0, first_in, arrived.astype(jnp.float32)))
-    last_grad, _ = backward(cotangent, saved)
+    inputs = jnp.where(section == 0, first_in, arrived.astype(jnp.float32))
+    output, hidden, pre_act, attn_mixed, last_q, held, held_last = forward(inputs)
+    saved = (inputs, hidden, pre_act, held, held_last, last_q)
+    last_grad = backward_layer(lengths, cotangent, saved, vector_rows, weights)[0]
     arrived = lax.ppermute(last_grad.astype(jnp.bfloat16), "pipe", [(1, 0)])
-    grad_in, weight_grads = backward(
-        jnp.where(section == 1, cotangent, arrived.astype(jnp.float32)), saved
-    )
-    grad_qkv, grad_proj, grad_up, grad_down, grad_vectors, grad_bias = weight_grads()
+    grad_output = jnp.where(section == 1, cotangent, arrived.astype(jnp.float32))
+    (
+        grad_in, grad_q, grad_k, grad_v, grad_one, grad_pre, activated, normed_one, normed_two,
+        grad_vectors, grad_bias,
+    ) = backward_layer(lengths, grad_output, saved, vector_rows, weights)
 
     def shards(matrix):
         return matrix.reshape(count, -1, 8, matrix.shape[-1])
@@ -909,23 +1043,27 @@
         ],
         1,
     ).reshape(count, RING, 8, width // count)
-    sums = sum_gradients(
-        [shards(grad_down), shards(grad_up), shards(grad_qkv), small_grads, shards(grad_proj)]
+    grads = [
+        shards(outer(activated, grad_output.astype(jnp.bfloat16))),
+        shards(outer(normed_two, grad_pre)),
+        shards(outer(normed_one, grad_q)),
+        shards(outer(normed_one, grad_k)),
+        shards(outer(normed_one, grad_v)),
+        shards(outer(attn_mixed, grad_one)),
+        small_grads,
+    ]
+    sums = sum_gradients(grads)
+    down, up, grad_q, grad_k, grad_v, proj = (
+        assemble(total, grad.shape[1]) for total, grad in zip(sums[:6], grads)
     )
-    totals = [
-        assemble(total, grad.shape[0] // count // 8)
-        for total, grad in zip(
-            (sums[2], sums[4], sums[1], sums[0]), (grad_qkv, grad_proj, grad_up, grad_down)
-        )
-    ]
-    small_total = sums[3].reshape(RING * 8, -1)
+    small_total = sums[6].reshape(RING * 8, -1)
     edges = jnp.where(section == 0, grad_in, output).reshape(1, micros, 1, rows, width)
     return (
         edges,
-        totals[0][None],
-        totals[1][None],
-        totals[2][None],
-        totals[3][None],
+        jnp.concatenate([grad_q, grad_k, grad_v], 1)[None],
+        proj[None],
+        up[None],
+        down[None],
         small_total[None, :8],
         small_total[8 : 8 + bias_rows].reshape(1, -1),
     )

time: 677 us -> 639 us (0.944)
  matrix products: 113 us -> 0 us
  Pallas kernels: 448 us -> 547 us
  local copies, waits for them, and re-layouts: 65.4 us -> 33.7 us
    dot_general x18 -> x0, matrix products: 113 us -> none  [the longest x14 94.1 us: plain(): return jnp.dot(left, right, preferred_element_type=jnp.float32)]
    pallas_call x4 -> x10, Pallas kernels: 150 us -> 249 us  [the longest x2 115 us: forward_layer(): pl.pallas_call(forward_kernel, out_shape=[jax.ShapeDtypeStruct((total, wi...]
    convert_element_type x4 -> x5, local copies, waits for them, and re-layouts: 15.6 us -> 1.91 us  [the longest x2 0.73 us: body(): small_full[:, 0].transpose(1, 0, 2).reshape(8, width).astype(jnp.float32)]
    unnamed x127 -> x69, local copies, waits for them, and re-layouts: 11 us -> 17.6 us
  transfers between devices with their start and end apart: 2 -> 2, of which waited for: 2 -> 2; matrix products, arithmetic and copies ran while one was open for 1% -> 0% of each run, Pallas kernels for 0% -> 0%
where the time goes in v3:
time: 639 us; the launch traced here: 631 us
  Pallas kernels  547 us (86%)
  local copies, waits for them, and re-layouts  33.7 us (5%)
  waiting for transfers between devices  24.4 us (4%)
  other arithmetic  17.9 us (3%)
  starting transfers between devices  6.61 us (1%)
    pallas_call x1, Pallas kernels, sum_gradients(): pl.pallas_call(functools.partial(sum_kernel, count), out_shape=[jax.Shape...  168 us
    pallas_call x1, Pallas kernels, gather_weights(): pl.pallas_call(functools.partial(gather_kernel, count), out_shape=[jax.Sh...  130 us
    pallas_call x2, Pallas kernels, forward_layer(): pl.pallas_call(forward_kernel, out_shape=[jax.ShapeDtypeStruct((total, wi...  115 us
    pallas_call x2, Pallas kernels, backward_layer(): pl.pallas_call(backward_kernel, out_shape=[jax.ShapeDtypeStruct(shape, dt...  112 us
    pallas_call x6, Pallas kernels, outer(): pl.pallas_call(outer_kernel, grid=(grid,), out_shape=jax.ShapeDtypeStruct...  21.9 us
    ppermute x1, waiting for transfers between devices, body(): arrived = lax.ppermute(last_grad.astype(jnp.bfloat16), 'pipe', [(1, 0)])  17.6 us
    unnamed x69, local copies, waits for them, and re-layouts  17.6 us
  transfers between devices with their start and end apart: 2, of which 2 were waited for; matrix products, arithmetic and copies ran while one was open for 0% of the time, Pallas kernels for 0%

profile of v3, /device:TPU:1, one launch (start us, length us, event | category | flops | bytes accessed | tf_op | source)
XLA Modules:
  0.0 630.8 jit_solution(2568908052730749604)
XLA Ops:
  0.7 2.2 slice_bitcast_fusion.1
  2.9 0.1 reshape_squeeze.14
  3.0 0.1 pad.29.clone
  3.1 0.7 maximum_bitcast_fusion.7.refs_0_
  3.8 130.3 %gather_weights.1 = (bf16[8,2,8,136]{3,2,1,0:T(8,128)(2,1)}, bf16[8,17,8,1088]{3,2,1,0:T(8,128)(2,1)}, bf16[8,17,8,1088]{3,2,1,0:T(8,128)(2,1)}, bf16[8,17,8,108...) custom-call(bf16[2,8,136]{2,1,0:T(8,128)(2,1)} %maximum_bitcast_fusi, ...), custom_call_target="tpu_custom_call" | custom-call | tf_op jit(solution)/shard_map/gather_weights/pallas_call | solution.py:165
  134.1 0.8 convert_bitcast_fusion
  134.9 0.8 slice_convert_fusion
  135.7 0.7 reshape.218.vectors
  136.4 0.7 reshape.219.up_bias
  137.1 1.3 copy.32
  138.4 0.1 select_reduce_fusion
  138.5 0.7 fusion.3.lengths
  139.2 56.1 %forward_layer.2 = (f32[256,1088]{1,0:T(8,128)}, f32[256,1088]{1,0:T(8,128)}, f32[256,4352]{1,0:T(8,128)}, bf16[256,1088]{1,0:T(8,128)(2,1)}, bf16[2,128,128]{2,...) custom-call(s32[2]{0:T(128)} %fusion.3.lengths, f32[256,1088]{1,0:T(8,128)} %bitcast.150, ...), custom_call_target="tpu_custom_call" | custom-call | tf_op jit(solution)/shard_map/forward_layer/pallas_call | solution.py:659
  195.2 1.4 convert_element_type.115
  196.6 0.2 copy.34
  196.9 5.1 collective-permute-start
  202.1 0.2 copy.31
  202.4 1.2 bitcast_multiply_fusion.grad_output
  203.5 6.8 %collective-permute-done = bf16[256,1088]{0,1:T(8,128)(2,1)} collective-permute-done((bf16[256,1088]{0,1:T(8,128)(2,1)S(1)}, bf16[256,1088]{0,1:T(8,128)(2,1)}, u32[]{:S(2)}, u32[]{:S(2)}) %collective-permute-start) | collective-permute-done | bytes 557088 | tf_op jit(solution)/shard_map/ppermute | solution.py:1023
  210.3 1.3 copy.35
  211.7 1.1 convert_select_fusion.1.inputs
  212.8 59.3 %forward_layer.3 = (f32[256,1088]{1,0:T(8,128)}, f32[256,1088]{1,0:T(8,128)}, f32[256,4352]{1,0:T(8,128)}, bf16[256,1088]{1,0:T(8,128)(2,1)}, bf16[2,128,128]{2,...) custom-call(s32[2]{0:T(128)} %fusion.3.lengths, ...), custom_call_target="tpu_custom_call" | custom-call | tf_op jit(solution)/shard_map/forward_layer/pallas_call | solution.py:659
  272.1 54.5 %backward_layer.2 = (f32[256,1088]{1,0:T(8,128)}, bf16[256,1088]{1,0:T(8,128)(2,1)}, bf16[256,1088]{1,0:T(8,128)(2,1)}, bf16[256,1088]{1,0:T(8,128)(2,1)}, bf16[...) custom-call(s32[2]{0:T(128)} %fusion.3.lengths, ...), custom_call_target="tpu_custom_call" | custom-call | tf_op jit(solution)/shard_map/backward_layer/pallas_call | solution.py:897
  326.7 1.3 convert_element_type.117
  328.0 0.2 copy.36
  328.2 1.5 collective-permute-start.1
  329.8 17.6 %collective-permute-done.1 = bf16[256,1088]{0,1:T(8,128)(2,1)S(1)} collective-permute-done((bf16[256,1088]{0,1:T(8,128)(2,1)S(1)}, bf16[256,1088]{0,1:T(8,128)(2,1)S(1)}, u32[]{:S(2)}, u32[]{:S(2)}) %collective-permute-start.1) | collective-permute-done | bytes 557088 | tf_op jit(solution)/shard_map/ppermute | solution.py:1028
  347.4 0.3 copy.37
  347.7 1.2 fusion.4
  348.9 57.0 %backward_layer.3 = (f32[256,1088]{1,0:T(8,128)}, bf16[256,1088]{1,0:T(8,128)(2,1)}, bf16[256,1088]{1,0:T(8,128)(2,1)}, bf16[256,1088]{1,0:T(8,128)(2,1)}, bf16[...) custom-call(s32[2]{0:T(128)} %fusion.3.lengths, ...), custom_call_target="tpu_custom_call" | custom-call | tf_op jit(solution)/shard_map/backward_layer/pallas_call | solution.py:897
  405.9 0.9 reshape.211
  406.8 0.8 reduce.1
  407.6 0.1 reshape.212
  407.7 1.1 copy-done.6
  408.8 1.1 copy-done.14
  409.9 2.2 outer.10
  412.1 1.5 copy-done.2
  413.6 2.2 outer.9
  415.8 1.5 copy-done.3
  417.3 2.2 outer.8
  419.5 1.4 copy-done.4
  421.0 2.2 outer.11
  423.2 1.5 copy-done.5
  424.8 6.4 %outer.7 = bf16[1088,4352]{1,0:T(8,128)(2,1)S(1)} custom-call(bf16[256,1088]{1,0:T(8,128)(2,1)S(1)} %copy-done.9, bf16[256,4352]{1,0:T(8,128)(2,1)S(1)} %copy-done.8), custom_call_target="tpu_custom_call" | custom-call | tf_op jit(solution)/shard_map/outer/pallas_call | solution.py:965
  431.2 3.6 copy-done.1
  434.8 6.6 %outer.6 = bf16[4352,1088]{1,0:T(8,128)(2,1)S(1)} custom-call(bf16[256,4352]{1,0:T(8,128)(2,1)S(1)} %copy-done.7, bf16[256,1088]{1,0:T(8,128)(2,1)S(1)} %get-tuple-element.96.right), custom_call_target="tpu_custom_call" | custom-call | tf_op jit(solution)/shard_map/outer/pallas_call | solution.py:965
  441.4 3.8 copy-done
  445.3 0.8 maximum_bitcast_fusion.6.refs_6_
  446.0 167.5 %sum_gradients.1 = (bf16[4,17,8,1088]{3,2,1,0:T(8,128)(2,1)}, bf16[4,5,8,4352]{3,2,1,0:T(8,128)(2,1)}, bf16[4,5,8,1088]{3,2,1,0:T(8,128)(2,1)}, bf16[4,5,8,1088]...) custom-call(bf16[8,68,8,1088]{3,2,1,0:T(8,128)(2,1)} %bitcast.120, ...), custom_call_target="tpu_custom_call" | custom-call | tf_op jit(solution)/shard_map/sum_gradients/pallas_call | solution.py:389
  613.6 2.1 slice_bitcast_fusion.10
  615.7 1.1 slice_bitcast_fusion
  616.8 0.7 slice_bitcast_fusion.17
  617.6 0.6 copy-done.16
  618.2 0.1 slice_bitcast_fusion.7
  618.4 0.9 concatenate.33
  619.4 1.3 bitcast_convert_fusion
  620.7 1.3 slice_bitcast_fusion.27
  622.0 0.7 slice.128
  622.7 0.7 reshape.215
  623.4 1.4 broadcast_select_fusion
  624.8 1.4 copy.39
  626.2 1.7 fusion
  627.9 1.6 fusion.1
  629.5 0.9 fusion.2
  (75 shorter events, 0.6 us)
Async XLA Ops:
  0.6 2.3 copy-start.31
  0.6 2.4 copy-start.30
  3.8 133.3 %copy-start.20 = (bf16[2,1,128,1088]{2,3,1,0:T(8,128)(2,1)S(1)}, bf16[2,1,128,1088]{2,3,1,0:T(8,128)(2,1)}, u32[]{:S(2)}) copy-start(bf16[2,1,128,1088]{2,3,1,0:T(8,128)(2,1)} %param.10) | copy-start | bytes 1671172
  134.1 4.3 copy-start.32
  134.1 4.3 copy-start.33
  195.2 6.8 %copy-start.29 = (s32[2]{0:T(128)S(1)}, s32[2]{0:T(128)}, u32[]{:S(2)}) copy-start(s32[2]{0:T(128)} %fusion.3.lengths) | copy-start | bytes 28
  195.2 6.9 %copy-start.21 = (bf16[2,1,128,1088]{2,3,1,0:T(8,128)(2,1)S(1)}, bf16[2,1,128,1088]{2,3,1,0:T(8,128)(2,1)}, u32[]{:S(2)}) copy-start(bf16[2,1,128,1088]{2,3,1,0:T(8,128)(2,1)} %param.11) | copy-start | bytes 1671172
  196.9 13.5 %collective-permute-start = (bf16[256,1088]{0,1:T(8,128)(2,1)S(1)}, bf16[256,1088]{0,1:T(8,128)(2,1)}, u32[]{:S(2)}, u32[]{:S(2)}) collective-permute-start(bf16[256,1088]{0,1:T(8,128)(2,1)S(1)} %copy.34), channel_id=1, source_target_pairs={{0,64},{1,65},{2,66},{3,67},{4,68},{5,69},{6,70},{7,71},{8,72},{9,... | collective-permute-start | bytes 1671176 | tf_op jit(solution)/shard_map/ppermute | solution.py:1023
  202.4 9.3 %copy-start.15 = (f32[2,1,128,1088]{3,2,0,1:T(8,128)S(1)}, f32[2,1,128,1088]{3,2,0,1:T(8,128)}, u32[]{:S(2)}) copy-start(f32[2,1,128,1088]{3,2,0,1:T(8,128)} %copy.32) | copy-start | bytes 3342340
  328.2 19.1 %collective-permute-start.1 = (bf16[256,1088]{0,1:T(8,128)(2,1)S(1)}, bf16[256,1088]{0,1:T(8,128)(2,1)S(1)}, u32[]{:S(2)}, u32[]{:S(2)}) collective-permute-start(bf16[256,1088]{0,1:T(8,128)(2,1)S(1)} %copy.36), channel_id=1, source_target_pairs={{64,0},{65,1},{66,2},{67,3},{68,4},{69,5},{70,6},{71,7},{72,8},{73... | collective-permute-start | bytes 1671176 | tf_op jit(solution)/shard_map/ppermute | solution.py:1028
  407.7 1.1 copy-start.6
  408.8 1.1 copy-start.14
  409.9 3.7 copy-start.13
  412.1 1.5 copy-start.2
  413.6 3.7 copy-start.12
  415.8 1.5 copy-start.3
  417.3 3.7 copy-start.10
  417.3 3.7 copy-start.11
  419.5 1.5 copy-start.4
  421.0 3.8 copy-start.8
  421.0 3.8 copy-start.9
  423.2 1.6 copy-start.5
  424.8 10.1 %copy-start.7 = (bf16[256,4352]{1,0:T(8,128)(2,1)S(1)}, bf16[256,4352]{1,0:T(8,128)(2,1)}, u32[]{:S(2)}) copy-start(bf16[256,4352]{1,0:T(8,128)(2,1)} %get-tuple-element.57.left) | copy-start | bytes 6684676
  431.2 3.6 copy-start.1
  441.4 3.8 copy-start
  613.6 3.2 copy-start.27
  613.6 3.2 copy-start.28
  615.7 1.8 copy-start.25
  615.7 1.8 copy-start.26
  616.8 1.4 copy-start.16
  626.1 1.7 copy-start.17
  626.1 1.7 copy-start.18
  626.2 1.7 copy-start.19
  627.8 1.6 copy-start.22
  627.8 1.6 copy-start.23
  627.9 1.6 copy-start.24

commit v4 on v3

--- a/solution.py
+++ b/solution.py
@@ -37,141 +37,195 @@
     return (member // 2, member % 2, replica // 2, replica % 2)
 
 
-def gather_kernel(count, *refs):
+class Links:
+    def __init__(self, send, recv):
+        self.send, self.recv, self.used = send, recv, 0
+
+    def channel(self, device):
+        self.used += 1
+        return Channel(self.send.at[self.used - 1], self.recv.at[self.used - 1], device)
+
+
+class Channel:
+    def __init__(self, send, recv, device):
+        self.send_sem, self.recv_sem, self.device = send, recv, device
+
+    def copy(self, src, dst):
+        return remote(src, dst, self.send_sem, self.recv_sem, self.device)
+
+    def send(self, src, dst):
+        self.copy(src, dst).start()
+
+    def sent(self, src):
+        self.copy(src, src).wait_send()
+
+    def came(self, dst):
+        self.copy(dst, dst).wait_recv()
+
+
+def near_devices():
+    z, x, y, c = place()
+    return {
+        "above": {"group": 2 * ((z + 1) % RING) + x},
+        "below": {"group": 2 * ((z + 3) % RING) + x},
+        "partner": {"group": 2 * z + 1 - x},
+        "sibling": {"rep": 2 * y + 1 - c},
+        "next": {"rep": 2 * ((y + 1) % RING) + c},
+        "last": {"rep": 2 * ((y + 3) % RING) + c},
+    }
+
+
+def gather_job(links, shard, full, first, size, spread):
+    z, x, y, c = place()
+    near = near_devices()
+    xc = (x + c) % 2
+    me = 2 * z + x
+    base, above, below, across = (2 * ((z + k) % RING) + xc for k in (0, 1, 3, 2))
+    piece = size // RING if spread else size
+    low = piece - piece // 2
+    finals = []
+
+    def region(slot, owner, part=""):
+        start = first + owner * piece if spread else first
+        if part == "low":
+            return full.at[slot, pl.ds(start, low)]
+        if part == "high":
+            return full.at[slot, pl.ds(start + low, piece - low)]
+        return full.at[slot, pl.ds(start, piece)]
+
+    def on_core(core, action):
+        pl.when(c == core)(action)
+
+    def always(action):
+        action()
+
+    def relay(channel, ref, run):
+        run(lambda: channel.send(ref, ref))
+        finals.append(lambda: run(lambda: channel.sent(ref)))
+
+    def hand(slot, owner, run, part=""):
+        channel = links.channel(near["sibling"])
+        relay(channel, region(slot, owner, part), run)
+        other = region(slot + 1 - 2 * xc, owner, part)
+        get = (lambda action: on_core(0, action)) if run is not always else always
+        finals.append(lambda: get(lambda: channel.came(other)))
+
+    across_x = links.channel(near["partner"])
+    up, down = links.channel(near["above"]), links.channel(near["below"])
+    far_up, far_down = links.channel(near["above"]), links.channel(near["below"])
+    own = shard.at[pl.ds(first + y * piece if spread else first, piece)]
+    second = lambda action: on_core(1, action)
+
+    def first_core():
+        up.send(own, region(base, y))
+        down.send(own, region(base, y))
+
+    if spread:
+        on_core(0, first_core)
+    on_core(1, lambda: across_x.send(own, region(me, y)))
+    finals.append(lambda: on_core(1, lambda: across_x.sent(own)))
+    finals.append(lambda: up.sent(own))
+    finals.append(lambda: down.sent(own))
+    yield
+
+    rings = []
+
+    def pass_on(slot, run):
+        if spread:
+            forth, back = links.channel(near["next"]), links.channel(near["last"])
+            relay(forth, region(slot, y), run)
+            relay(back, region(slot, y), run)
+            rings.append((slot, run, forth, back))
+        hand(slot, y, run)
+
+    def second_core():
+        across_x.came(region(base, y))
+        up.send(region(base, y), region(base, y))
+        down.send(region(base, y), region(base, y))
+
+    if not spread:
+        on_core(0, first_core)
+    on_core(1, second_core)
+    pass_on(base, second)
+    yield
+
+    up.came(region(below, y))
+    relay(far_up, region(below, y, "low"), always)
+    pass_on(below, always)
+    down.came(region(above, y))
+    if piece > low:
+        relay(far_down, region(above, y, "high"), always)
+    pass_on(above, always)
+    yield
+
+    far_up.came(region(across, y, "low"))
+    if piece > low:
+        far_down.came(region(across, y, "high"))
+    pass_on(across, always)
+    yield
+
+    if spread:
+        ends = []
+        for slot, run, forth, back in rings:
+            far_forth, far_back = links.channel(near["next"]), links.channel(near["last"])
+            behind, ahead = (y + 3) % RING, (y + 1) % RING
+            run(lambda: forth.came(region(slot, behind)))
+            relay(far_forth, region(slot, behind, "low"), run)
+            hand(slot, behind, run)
+            run(lambda: back.came(region(slot, ahead)))
+            if piece > low:
+                relay(far_back, region(slot, ahead, "high"), run)
+            hand(slot, ahead, run)
+            ends.append((slot, run, far_forth, far_back))
+        yield
+        for slot, run, far_forth, far_back in ends:
+            far = (y + 2) % RING
+            run(lambda: far_forth.came(region(slot, far, "low")))
+            if piece > low:
+                run(lambda: far_back.came(region(slot, far, "high")))
+            hand(slot, far, run)
+        yield
+    for action in finals:
+        action()
+
+
+MAX_LINKS = 160
+
+
+ORDER = "SPSSSPSPSP"
+
+
+def gather_kernel(plan, count, *refs):
     ins, outs = refs[:count], refs[count : 2 * count]
-    send, recv, local = refs[2 * count :]
-    z, x, y, c = place()
-    me = 2 * z + x
-    xc = (x + c) % 2
-    zp, zm, zo = (z + 1) % RING, (z + 3) % RING, (z + 2) % RING
-    base, above, below, across = 2 * z + xc, 2 * zp + xc, 2 * zm + xc, 2 * zo + xc
-    to_above = {"group": 2 * zp + x}
-    to_below = {"group": 2 * zm + x}
-    sibling = {"rep": 2 * y + 1 - c}
-    partner = {"group": 2 * z + 1 - x}
-    greet([to_above, to_below, sibling, partner])
-
-    def part(array, slot, kind):
-        half = ins[array].shape[0] // 2
-        ref = outs[array].at[slot]
-        if kind == "low":
-            return ref.at[pl.ds(0, half)]
-        if kind == "high":
-            return ref.at[pl.ds(half, ins[array].shape[0] - half)]
-        return ref
-
-    def across_x(i):
-        return remote(ins[i], part(i, me, ""), send.at[i, 0], recv.at[i, 0], partner)
-
-    def first_up(i):
-        src = part(i, base, "")
-        return remote(src, part(i, base, ""), send.at[i, 1], recv.at[i, 1], to_above)
-
-    def first_down(i):
-        src = part(i, base, "")
-        return remote(src, part(i, base, ""), send.at[i, 2], recv.at[i, 2], to_below)
-
-    def second_up(i):
-        src = part(i, below, "low")
-        return remote(src, src, send.at[i, 3], recv.at[i, 3], to_above)
-
-    def second_down(i):
-        src = part(i, above, "high")
-        return remote(src, src, send.at[i, 4], recv.at[i, 4], to_below)
-
-    def hand(i, slot, kind, sem):
-        src = part(i, slot, kind)
-        return remote(src, src, send.at[i, sem], recv.at[i, sem], sibling)
-
-    def own(i):
-        return pltpu.make_async_copy(ins[i], part(i, me, ""), local.at[i])
-
-    def own_up(i):
-        return remote(ins[i], part(i, me, ""), send.at[i, 1], recv.at[i, 1], to_above)
-
-    def own_down(i):
-        return remote(ins[i], part(i, me, ""), send.at[i, 2], recv.at[i, 2], to_below)
-
-    arrays = range(count)
-
-    @pl.when(c == 0)
-    def _():
-        for i in arrays:
-            own_up(i).start()
-            own_down(i).start()
-
-    @pl.when(c == 1)
-    def _():
-        for i in arrays:
-            across_x(i).start()
-
-    for i in arrays:
-        own(i).start()
-
-    @pl.when(c == 1)
-    def _():
-        for i in arrays:
-            remote(ins[i], part(i, base, ""), send.at[i, 0], recv.at[i, 0], partner).wait_recv()
-            first_up(i).start()
-            first_down(i).start()
-            hand(i, base, "", 5).start()
-
-    for i in arrays:
-        remote(ins[i], part(i, below, ""), send.at[i, 1], recv.at[i, 1], to_above).wait_recv()
-        second_up(i).start()
-        hand(i, below, "", 6).start()
-        remote(ins[i], part(i, above, ""), send.at[i, 2], recv.at[i, 2], to_below).wait_recv()
-        second_down(i).start()
-        hand(i, above, "", 7).start()
-    for i in arrays:
-        src = part(i, across, "low")
-        remote(src, src, send.at[i, 3], recv.at[i, 3], to_above).wait_recv()
-        hand(i, across, "low", 8).start()
-        src = part(i, across, "high")
-        remote(src, src, send.at[i, 4], recv.at[i, 4], to_below).wait_recv()
-        hand(i, across, "high", 9).start()
-
-    @pl.when(c == 0)
-    def _():
-        for i in arrays:
-            hand(i, 2 * z + 1 - xc, "", 5).wait_recv()
-            own_up(i).wait_send()
-            own_down(i).wait_send()
-
-    @pl.when(c == 1)
-    def _():
-        for i in arrays:
-            across_x(i).wait_send()
-            first_up(i).wait_send()
-            first_down(i).wait_send()
-            hand(i, base, "", 5).wait_send()
-
-    for i in arrays:
-        hand(i, 2 * zm + 1 - xc, "", 6).wait_recv()
-        hand(i, 2 * zp + 1 - xc, "", 7).wait_recv()
-        hand(i, 2 * zo + 1 - xc, "low", 8).wait_recv()
-        hand(i, 2 * zo + 1 - xc, "high", 9).wait_recv()
-        second_up(i).wait_send()
-        second_down(i).wait_send()
-        hand(i, below, "", 6).wait_send()
-        hand(i, above, "", 7).wait_send()
-        hand(i, across, "low", 8).wait_send()
-        hand(i, across, "high", 9).wait_send()
-        own(i).wait()
-
-
-def gather_weights(shards):
+    links = Links(*refs[2 * count :])
+    member = lax.axis_index("group")
+    greet(list(near_devices().values()))
+    spread = [gather_job(links, ins[i], outs[i], *rest) for i, *rest in plan if rest[-1]]
+    whole = [gather_job(links, ins[i], outs[i], *rest) for i, *rest in plan if not rest[-1]]
+    owns = [links.channel(near_devices()["sibling"]) for _ in range(count)]
+    for step, which in enumerate(ORDER):
+        for job in spread if which == "S" else whole:
+            next(job)
+        if step == 1:
+            for i in range(count):
+                owns[i].send(ins[i], outs[i].at[member])
+    for job in spread + whole:
+        for _ in job:
+            pass
+    for i in range(count):
+        owns[i].came(outs[i].at[member])
+        owns[i].sent(ins[i])
+
+
+def gather_weights(shards, plan):
     count = len(shards)
+    dma = pltpu.SemaphoreType.DMA
     return pl.pallas_call(
-        functools.partial(gather_kernel, count),
+        functools.partial(gather_kernel, plan, count),
         out_shape=[jax.ShapeDtypeStruct((8,) + s.shape, s.dtype) for s in shards],
         in_specs=[pl.BlockSpec(memory_space=pl.ANY)] * count,
         out_specs=[pl.BlockSpec(memory_space=pl.ANY)] * count,
-        scratch_shapes=[
-            pltpu.SemaphoreType.DMA((count, 10)),
-            pltpu.SemaphoreType.DMA((count, 10)),
-            pltpu.SemaphoreType.DMA((count,)),
-        ],
+        scratch_shapes=[dma((MAX_LINKS,)), dma((MAX_LINKS,))],
         compiler_params=pltpu.CompilerParams(collective_id=0, has_side_effects=True),
         name="gather_weights",
     )(*shards)
@@ -193,218 +247,301 @@
     lax.fori_loop(0, count, step, 0)
 
 
-PER_ARRAY = 9
-
-
-def sum_kernel(count, *refs):
-    ins, outs = refs[:count], refs[count : 2 * count]
-    buffers = refs[2 * count : 2 * count + PER_ARRAY * count]
-    send, recv, local = refs[2 * count + PER_ARRAY * count :]
+TILE = 256
+
+
+def product_into(left, right, whole, stage, sems):
+    def copy(tile, first, size):
+        src = stage.at[tile % 2, pl.ds(0, size // 8)]
+        return pltpu.make_async_copy(src, whole.at[pl.ds(first // 8, size // 8)], sems.at[tile % 2])
+
+    tiles = [(t, *chunk) for t, chunk in enumerate(column_chunks(left.shape[1], TILE))]
+    for t, first, size in tiles:
+        if t >= 2:
+            copy(*tiles[t - 2]).wait()
+        for column, width in column_chunks(right.shape[1], 1152):
+            tile = over_rows(left[:, first : first + size], right[:, column : column + width])
+            stage[t % 2, 0 : size // 8, :, column : column + width] = tile.reshape(
+                size // 8, 8, width
+            ).astype(stage.dtype)
+        copy(t, first, size).start()
+    for tile in tiles[-2:]:
+        copy(*tile).wait()
+
+
+def sum_job(links, fill, whole, blocks, spread, total, stage, loads, buffers, out, kept):
     z, x, y, c = place()
+    near = near_devices()
     xc = (x + c) % 2
-    zp, zm = (z + 1) % RING, (z + 3) % RING
-    to_above = {"group": 2 * zp + x}
-    to_below = {"group": 2 * zm + x}
-    sibling = {"rep": 2 * y + 1 - c}
-    partner = {"group": 2 * z + 1 - x, "rep": 2 * y + 1 - c}
+    cross_core = {"group": 2 * z + 1 - x, "rep": 2 * y + 1 - c}
     others = [{"rep": 2 * ((y + j) % RING) + c} for j in range(1, RING)]
-    greet([to_above, to_below, sibling, partner] + others)
-
-    def parts(i):
-        return buffers[PER_ARRAY * i : PER_ARRAY * (i + 1)]
-
-    def swap(i, k):
-        own, came = ins[i].at[2 * ((z + k) % RING) + 1 - xc], parts(i)[1].at[k]
-        return remote(own, came, send.at[i, k], recv.at[i, k], sibling)
-
-    def load(i, k):
-        return pltpu.make_async_copy(
-            ins[i].at[2 * ((z + k) % RING) + xc], parts(i)[0].at[k], local.at[i, k]
+    far_low, far_high, from_below, from_above, cross = buffers[:5]
+    size = blocks // RING if spread else blocks
+    first = y * size if spread else 0
+    low = size // 2
+    order = (2, 1, 3, 0)
+    finals = []
+
+    def on_core(core, action):
+        def run():
+            action()
+
+        pl.when(c == core)(run)
+
+    def launch(device, src, dst):
+        channel = links.channel(device)
+        channel.send(src, dst)
+        finals.append(lambda: channel.sent(src))
+        return channel
+
+    def shard(k, column):
+        return whole.at[pl.ds((2 * ((z + k) % RING) + column) * blocks, blocks)]
+
+    def rows(k, start, count):
+        return total.at[k, pl.ds(start, count)]
+
+    fill()
+    swaps = [launch(near["sibling"], shard(k, 1 - xc), total.at[k]) for k in order]
+    yield
+
+    def load(n):
+        return pltpu.make_async_copy(shard(order[n], xc), stage.at[n % 2], loads.at[n % 2])
+
+    def send_far():
+        up = launch(near["above"], rows(2, first, low), far_low)
+        down = launch(near["below"], rows(2, first + low, size - low), far_high)
+        return (up, down)
+
+    load(0).start()
+    load(1).start()
+    for n, k in enumerate(order):
+        load(n).wait()
+        swaps[n].came(total.at[k])
+        add_blocks(blocks, total.at[k], [stage.at[n % 2]])
+        if n + 2 < RING:
+            load(n + 2).start()
+        if k == 2 and not spread:
+            far = send_far()
+    if spread:
+        ring_low, ring_high, from_last, from_next = buffers[5:9]
+        ahead, behind, opposite = ((y + j) % RING * size for j in (1, 3, 2))
+
+        def quarter(start, count):
+            return total.at[:, pl.ds(start, count)]
+
+        forth = launch(near["next"], quarter(opposite, low), ring_low)
+        back = launch(near["last"], quarter(opposite + low, size - low), ring_high)
+        yield
+        forth.came(ring_low)
+        for k in range(RING):
+            add_blocks(low, rows(k, ahead, low), [ring_low.at[k]])
+        forth = launch(near["next"], quarter(ahead, size), from_last)
+        back.came(ring_high)
+        for k in range(RING):
+            add_blocks(size - low, rows(k, behind + low, size - low), [ring_high.at[k]])
+        back = launch(near["last"], quarter(behind, size), from_next)
+        yield
+        forth.came(from_last)
+        back.came(from_next)
+        for k in order:
+            add_blocks(size, rows(k, first, size), [from_last.at[k], from_next.at[k]])
+            if k == 2:
+                far = send_far()
+    yield
+    far[0].came(far_low)
+    add_blocks(low, rows(1, first, low), [far_low])
+    up = launch(near["above"], rows(1, first, size), from_below)
+    far[1].came(far_high)
+    add_blocks(size - low, rows(3, first + low, size - low), [far_high])
+    down = launch(near["below"], rows(3, first, size), from_above)
+    yield
+    up.came(from_below)
+    down.came(from_above)
+    mine = rows(0, first, size)
+    add_blocks(size, mine, [from_below, from_above])
+    over_x = links.channel(cross_core)
+    on_core(1, lambda: over_x.send(mine, cross))
+    finals.append(lambda: on_core(1, lambda: over_x.sent(mine)))
+    yield
+
+    def take_x():
+        over_x.came(cross)
+        add_blocks(size, mine, [cross])
+
+    on_core(0, take_x)
+    if spread:
+        result = mine
+    else:
+        ring, result = buffers[5:7]
+        piece = result.shape[0]
+        over_y = [links.channel(device) for device in others]
+
+        def part(owner):
+            return total.at[0, pl.ds((owner * blocks) // RING, piece)]
+
+        def send_y():
+            for j in (2, 1, 3):
+                over_y[j - 1].send(part((y + j) % RING), ring.at[j - 1])
+
+        on_core(0, send_y)
+        finals.append(
+            lambda: on_core(0, lambda: [over_y[j].sent(part((y + j + 1) % RING)) for j in range(3)])
         )
-
-    def sizes(i):
-        blocks = ins[i].shape[1]
-        return (blocks, blocks // 2, piece_rows(blocks))
-
-    def far_up(i):
-        blocks, half, _ = sizes(i)
-        src = parts(i)[0].at[2, pl.ds(0, half)]
-        return remote(src, parts(i)[2], send.at[i, 4], recv.at[i, 4], to_above)
-
-    def far_down(i):
-        blocks, half, _ = sizes(i)
-        src = parts(i)[0].at[2, pl.ds(half, blocks - half)]
-        return remote(src, parts(i)[3], send.at[i, 5], recv.at[i, 5], to_below)
-
-    def near_up(i):
-        return remote(parts(i)[0].at[1], parts(i)[4], send.at[i, 6], recv.at[i, 6], to_above)
-
-    def near_down(i):
-        return remote(parts(i)[0].at[3], parts(i)[5], send.at[i, 7], recv.at[i, 7], to_below)
-
-    def over_x(i):
-        return remote(parts(i)[0].at[0], parts(i)[6], send.at[i, 8], recv.at[i, 8], partner)
-
-    def own_piece(i, owner):
-        blocks, _, rows = sizes(i)
-        return parts(i)[0].at[0, pl.ds((owner * blocks) // RING, rows)]
-
-    def over_y(i, j):
-        src = own_piece(i, (y + j) % RING)
-        dst = parts(i)[7].at[j - 1]
-        return remote(src, dst, send.at[i, 8 + j], recv.at[i, 8 + j], others[j - 1])
-
-    def share_y(i, j, slot):
-        dst = outs[i].at[slot]
-        return remote(parts(i)[8], dst, send.at[i, 11 + j], recv.at[i, 11 + j], others[j - 1])
-
-    def keep(i):
-        return pltpu.make_async_copy(parts(i)[8], outs[i].at[y], local.at[i, 4])
-
-    def hand(i):
-        return remote(outs[i], outs[i], send.at[i, 15], recv.at[i, 15], sibling)
-
-    for i in range(count):
-        for k in (2, 1, 3, 0):
-            swap(i, k).start()
-            load(i, k).start()
-
-    def step_cores(i):
-        blocks, half, _ = sizes(i)
-        total, came = parts(i)[0], parts(i)[1]
-        for k in (2, 1, 3, 0):
-            load(i, k).wait()
-            swap(i, k).wait_recv()
-            add_blocks(blocks, total.at[k], [came.at[k]])
-            if k == 2:
-                far_up(i).start()
-                far_down(i).start()
-
-    def step_far(i):
-        blocks, half, _ = sizes(i)
-        total = parts(i)[0]
-        far_up(i).wait_recv()
-        add_blocks(half, total.at[1, pl.ds(0, half)], [parts(i)[2]])
-        near_up(i).start()
-        far_down(i).wait_recv()
-        add_blocks(blocks - half, total.at[3, pl.ds(half, blocks - half)], [parts(i)[3]])
-        near_down(i).start()
-
-    def step_near(i):
-        blocks, half, _ = sizes(i)
-        near_up(i).wait_recv()
-        near_down(i).wait_recv()
-        add_blocks(blocks, parts(i)[0].at[0], [parts(i)[4], parts(i)[5]])
-
-        @pl.when(c == 1)
-        def _():
-            over_x(i).start()
-
-    def step_x(i):
-        blocks, half, _ = sizes(i)
-
-        @pl.when(c == 0)
-        def _():
-            over_x(i).wait_recv()
-            add_blocks(blocks, parts(i)[0].at[0], [parts(i)[6]])
-            for j in (2, 1, 3):
-                over_y(i, j).start()
-
-    def step_y(i):
-        _, _, rows = sizes(i)
-
-        @pl.when(c == 0)
-        def _():
-            for j in (1, 2, 3):
-                over_y(i, j).wait_recv()
-            own, came, result = own_piece(i, y), parts(i)[7], parts(i)[8]
+        yield
+
+        def take_y():
+            for j in range(RING - 1):
+                over_y[j].came(ring.at[j])
+            own = part(y)
 
             def step(b, carry):
-                total = own[b].astype(jnp.float32)
+                value = own[b].astype(jnp.float32)
                 for j in range(RING - 1):
-                    total = total + came[j, b].astype(jnp.float32)
-                result[b] = total.astype(result.dtype)
+                    value = value + ring[j, b].astype(jnp.float32)
+                result[b] = value.astype(result.dtype)
                 return carry
 
-            lax.fori_loop(0, rows, step, 0)
-            for j in (2, 1, 3):
-                share_y(i, j, y).start()
-            keep(i).start()
-
-    def step_hand(i):
-        @pl.when(c == 0)
-        def _():
-            keep(i).wait()
-            for j in (1, 2, 3):
-                share_y(i, j, (y + RING - j) % RING).wait_recv()
-            hand(i).start()
-
-    def step_last(i):
-        @pl.when(c == 1)
-        def _():
-            hand(i).wait_recv()
-
-    steps = [step_cores, step_far, step_near, step_x, step_y, step_hand, step_last]
-    for tick in range(count + len(steps) - 1):
-        for i in range(count):
-            at = tick - i
-            if 0 <= at < len(steps):
-                steps[at](i)
-    for i in range(count):
-        for k in range(RING):
-            swap(i, k).wait_send()
-        for copy in (far_up, far_down, near_up, near_down):
-            copy(i).wait_send()
-
-        @pl.when(c == 1)
-        def _():
-            over_x(i).wait_send()
-
-        @pl.when(c == 0)
-        def _():
-            for j in (1, 2, 3):
-                over_y(i, j).wait_send()
-                share_y(i, j, y).wait_send()
-            hand(i).wait_send()
-
-
-def sum_gradients(grads):
-    count = len(grads)
-    scratch = []
-    for grad in grads:
-        _, blocks, rows, width = grad.shape
-        half, piece = blocks // 2, piece_rows(blocks)
-        for lead in (
-            (RING, blocks),
-            (RING, blocks),
-            (half,),
-            (blocks - half,),
-            (blocks,),
-            (blocks,),
-            (blocks,),
-            (RING - 1, piece),
-            (piece,),
-        ):
-            scratch.append(pltpu.VMEM(lead + (rows, width), grad.dtype))
+            lax.fori_loop(0, piece, step, 0)
+
+        on_core(0, take_y)
+    shares = [links.channel(device) for device in others]
+    keep = pltpu.make_async_copy(result, out.at[y], kept)
+
+    def share():
+        for j in (2, 1, 3):
+            shares[j - 1].send(result, out.at[y])
+        keep.start()
+
+    on_core(0, share)
+    finals.append(lambda: on_core(0, lambda: [channel.sent(result) for channel in shares]))
+    yield
+    hand = links.channel(near["sibling"])
+
+    def pass_on():
+        keep.wait()
+        for j in (1, 2, 3):
+            shares[j - 1].came(out.at[(y + RING - j) % RING])
+        hand.send(out, out)
+
+    on_core(0, pass_on)
+    finals.append(lambda: on_core(0, lambda: hand.sent(out)))
+    yield
+    on_core(1, lambda: hand.came(out))
+    for action in finals:
+        action()
+
+
+SUM_LINKS = 160
+
+
+def sum_kernel(shapes, *refs):
+    operands, refs = refs[: SUM_OPERANDS], refs[SUM_OPERANDS:]
+    count = len(shapes)
+    outs, refs = refs[:count], refs[count:]
+    filled = sum(1 for shape in shapes if shape[1] is not None)
+    wholes, refs = list(refs[:filled]), refs[filled:]
+    send, recv, kept, sems, loads = refs[:5]
+    narrow_fill, wide_fill, narrow_stage, wide_stage, tall_stage, small_stage = refs[5:11]
+    refs = refs[11:]
+    links = Links(send, recv)
+    z, x, y, c = place()
+    near = near_devices()
+    greet(
+        [near["above"], near["below"], near["sibling"]]
+        + [{"group": 2 * z + 1 - x, "rep": 2 * y + 1 - c}]
+        + [{"rep": 2 * ((y + j) % RING) + c} for j in range(1, RING)]
+    )
+    jobs = []
+    for i, (left, right, blocks, spread, offset) in enumerate(shapes):
+        buffers, refs = refs[:10], refs[10:]
+        stage = narrow_stage
+        if right is None:
+            whole, stage, fill = operands[left], small_stage, (lambda: None)
+        else:
+            whole = wholes.pop(0)
+            space = narrow_fill
+            if outs[i].shape[-1] > 2048:
+                space, stage = wide_fill, wide_stage
+            elif spread:
+                stage = tall_stage
+            fill = functools.partial(
+                product_into, operands[left], operands[right], whole, space, sems
+            )
+        job = sum_job(
+            links, fill, whole, blocks, spread, buffers[0], stage, loads, buffers[1:], outs[i], kept.at[i]
+        )
+        jobs.append((offset, job))
+    tick = 0
+    while jobs:
+        alive = []
+        for offset, job in jobs:
+            if offset == tick:
+                next(job)
+        for offset, job in jobs:
+            if offset >= tick:
+                alive.append((offset, job))
+                continue
+            try:
+                next(job)
+                alive.append((offset, job))
+            except StopIteration:
+                pass
+        jobs = alive
+        tick += 1
+
+
+SUM_OPERANDS = 11
+
+
+def sum_gradients(operands, shapes):
+    dma, vmem, hbm = pltpu.SemaphoreType.DMA, pl.BlockSpec(memory_space=pltpu.VMEM), pl.BlockSpec(memory_space=pl.ANY)
+    bf16 = jnp.bfloat16
+    count = len(shapes)
+    outs, wholes, scratch = [], [], []
+    narrow_width = min(operands[right].shape[1] for _, right, *_ in shapes if right is not None)
+    wide_width = max(operands[right].shape[1] for _, right, *_ in shapes if right is not None)
+    for left, right, blocks, spread, _ in shapes:
+        if right is None:
+            width, dtype = operands[left].shape[-1], operands[left].dtype
+        else:
+            width, dtype = operands[right].shape[1], bf16
+            wholes.append(jax.ShapeDtypeStruct((8 * blocks, 8, width), dtype))
+        piece = piece_rows(blocks)
+        outs.append(jax.ShapeDtypeStruct((RING, piece, 8, width), dtype))
+        size = blocks // RING if spread else blocks
+        low = size // 2
+        leads = [(RING, blocks), (low,), (size - low,), (size,), (size,), (size,)]
+        if spread:
+            leads += [(RING, low), (RING, size - low), (RING, size), (RING, size)]
+        else:
+            leads += [(RING - 1, piece), (piece,), (1,), (1,)]
+        scratch += [pltpu.VMEM(lead + (8, width), dtype) for lead in leads]
+    blocks = {spread: b for _, right, b, spread, _ in shapes if right is not None}
+    small_shape = operands[-1].shape
     return pl.pallas_call(
-        functools.partial(sum_kernel, count),
-        out_shape=[
-            jax.ShapeDtypeStruct((RING, piece_rows(g.shape[1])) + g.shape[2:], g.dtype)
-            for g in grads
-        ],
-        in_specs=[pl.BlockSpec(memory_space=pl.ANY)] * count,
-        out_specs=[pl.BlockSpec(memory_space=pl.ANY)] * count,
-        scratch_shapes=scratch
-        + [
-            pltpu.SemaphoreType.DMA((count, 16)),
-            pltpu.SemaphoreType.DMA((count, 16)),
-            pltpu.SemaphoreType.DMA((count, 5)),
-        ],
+        functools.partial(sum_kernel, shapes),
+        out_shape=outs + wholes,
+        in_specs=[vmem] * (len(operands) - 1) + [hbm],
+        out_specs=[hbm] * (count + len(wholes)),
+        scratch_shapes=[
+            dma((SUM_LINKS,)),
+            dma((SUM_LINKS,)),
+            dma((count,)),
+            dma((2,)),
+            dma((2,)),
+            pltpu.VMEM((2, TILE // 8, 8, narrow_width), bf16),
+            pltpu.VMEM((2, TILE // 8, 8, wide_width), bf16),
+            pltpu.VMEM((2, blocks[False], 8, narrow_width), bf16),
+            pltpu.VMEM((2, blocks[False], 8, wide_width), bf16),
+            pltpu.VMEM((2, blocks[True], 8, narrow_width), bf16),
+            pltpu.VMEM((2, small_shape[0] // 8) + small_shape[1:], operands[-1].dtype),
+        ]
+        + scratch,
         compiler_params=pltpu.CompilerParams(
-            collective_id=1, has_side_effects=True, vmem_limit_bytes=60 * 1024 * 1024
+            collective_id=1, has_side_effects=True, vmem_limit_bytes=62 * 1024 * 1024
         ),
         name="sum_gradients",
-    )(*grads)
+    )(*operands)[:count]
 
 
 def assemble(pieces, blocks):
@@ -940,39 +1077,6 @@
     )(lengths, grad_output, inputs, hidden, vectors, pre_act, held, held_last, last_q, *weights)
 
 
-def outer_kernel(left, right, out):
-    out[...] = over_rows(left[...], right[...]).astype(out.dtype)
-
-
-def outer(left, right):
-    rows, height = left.shape
-    width = right.shape[1]
-    tile = 256
-    if height > width:
-        grid = pl.cdiv(height, tile)
-        specs = [
-            pl.BlockSpec((rows, tile), lambda i: (0, i)),
-            pl.BlockSpec((rows, width), lambda i: (0, 0)),
-        ]
-        out_spec = pl.BlockSpec((tile, width), lambda i: (i, 0))
-    else:
-        grid = pl.cdiv(width, tile)
-        specs = [
-            pl.BlockSpec((rows, height), lambda i: (0, 0)),
-            pl.BlockSpec((rows, tile), lambda i: (0, i)),
-        ]
-        out_spec = pl.BlockSpec((height, tile), lambda i: (0, i))
-    return pl.pallas_call(
-        outer_kernel,
-        grid=(grid,),
-        out_shape=jax.ShapeDtypeStruct((height, width), jnp.bfloat16),
-        in_specs=specs,
-        out_specs=out_spec,
-        compiler_params=pltpu.CompilerParams(vmem_limit_bytes=32 * 1024 * 1024),
-        name="outer",
-    )(left, right)
-
-
 def in_blocks(matrix):
     return matrix.reshape(matrix.shape[0] // 8, 8, matrix.shape[1])
 
@@ -1009,7 +1113,17 @@
     )
     thirds = [w_qkv[0][:, i * width : (i + 1) * width] for i in range(3)]
     small_full, *full = gather_weights(
-        [in_blocks(array) for array in (small, *thirds, w_proj[0], w_up[0], w_down[0])]
+        [in_blocks(array) for array in (small, *thirds, w_proj[0], w_up[0], w_down[0])],
+        (
+            (6, 0, 68, True),
+            (5, 0, 16, True),
+            (0, 0, 2, False),
+            (1, 0, 17, False),
+            (2, 0, 17, False),
+            (3, 0, 17, False),
+            (4, 0, 17, False),
+            (5, 16, 1, False),
+        ),
     )
     vector_rows = small_full[:, 0].transpose(1, 0, 2).reshape(8, width).astype(jnp.float32)
     up_bias = small_full[:, 1, :bias_rows].reshape(1, -1).astype(jnp.float32)
@@ -1032,9 +1146,6 @@
         grad_vectors, grad_bias,
     ) = backward_layer(lengths, grad_output, saved, vector_rows, weights)
 
-    def shards(matrix):
-        return matrix.reshape(count, -1, 8, matrix.shape[-1])
-
     small_grads = jnp.concatenate(
         [
             grad_vectors.reshape(8, count, -1).transpose(1, 0, 2),
@@ -1042,19 +1153,26 @@
             jnp.zeros((count, 24 - bias_rows, width // count), jnp.float32),
         ],
         1,
-    ).reshape(count, RING, 8, width // count)
-    grads = [
-        shards(outer(activated, grad_output.astype(jnp.bfloat16))),
-        shards(outer(normed_two, grad_pre)),
-        shards(outer(normed_one, grad_q)),
-        shards(outer(normed_one, grad_k)),
-        shards(outer(normed_one, grad_v)),
-        shards(outer(attn_mixed, grad_one)),
-        small_grads,
-    ]
-    sums = sum_gradients(grads)
-    down, up, grad_q, grad_k, grad_v, proj = (
-        assemble(total, grad.shape[1]) for total, grad in zip(sums[:6], grads)
+    ).reshape(count * RING, 8, width // count)
+    blocks = width // count // 8
+    tall = grad_pre.shape[1] // count // 8
+    sums = sum_gradients(
+        (
+            normed_one, grad_q, grad_k, grad_v, attn_mixed, grad_one, normed_two, grad_pre, activated,
+            grad_output.astype(jnp.bfloat16), small_grads,
+        ),
+        (
+            (0, 1, blocks, False, 0),
+            (8, 9, tall, True, 0),
+            (6, 7, blocks, False, 1),
+            (0, 2, blocks, False, 2),
+            (0, 3, blocks, False, 3),
+            (4, 5, blocks, False, 4),
+            (10, None, RING, False, 5),
+        ),
+    )
+    grad_q, down, up, grad_k, grad_v, proj = (
+        assemble(total, tall if i == 1 else blocks) for i, total in enumerate(sums[:6])
     )
     small_total = sums[6].reshape(RING * 8, -1)
     edges = jnp.where(section == 0, grad_in, output).reshape(1, micros, 1, rows, width)

time: 639 us -> 569 us (0.89)
  Pallas kernels: 547 us -> 494 us
  local copies, waits for them, and re-layouts: 33.7 us -> 18.2 us
    pallas_call x8 -> x2, Pallas kernels: 320 us -> 267 us  [the longest x1 178 us: sum_gradients(): pl.pallas_call(functools.partial(sum_kernel, shapes), out_shape=outs + wh...]
    unnamed x69 -> x39, local copies, waits for them, and re-layouts: 17.6 us -> 2.04 us
where the time goes in v4:
time: 569 us; the launch traced here: 558 us
  Pallas kernels  494 us (87%)
  waiting for transfers between devices  19.2 us (3%)
  local copies, waits for them, and re-layouts  18.2 us (3%)
  other arithmetic  18.1 us (3%)
  starting transfers between devices  7.26 us (1%)
    pallas_call x1, Pallas kernels, sum_gradients(): pl.pallas_call(functools.partial(sum_kernel, shapes), out_shape=outs + wh...  178 us
    pallas_call x2, Pallas kernels, backward_layer(): pl.pallas_call(backward_kernel, out_shape=[jax.ShapeDtypeStruct(shape, dt...  114 us
    pallas_call x2, Pallas kernels, forward_layer(): pl.pallas_call(forward_kernel, out_shape=[jax.ShapeDtypeStruct((total, wi...  113 us
    pallas_call x1, Pallas kernels, gather_weights(): pl.pallas_call(functools.partial(gather_kernel, plan, count), out_shape=[...  88.4 us
    ppermute x1, waiting for transfers between devices, body(): arrived = lax.ppermute(last_grad.astype(jnp.bfloat16), 'pipe', [(1, 0)])  12 us
  transfers between devices with their start and end apart: 2, of which 2 were waited for; matrix products, arithmetic and copies ran while one was open for 0% of the time, Pallas kernels for 0%

profile of v4, /device:TPU:1, one launch (start us, length us, event | category | flops | bytes accessed | tf_op | source)
XLA Modules:
  0.0 557.6 jit_solution(17013041375471392099)
XLA Ops:
  0.6 0.0 copy-start.16
  0.7 2.2 slice_bitcast_fusion.1
  2.9 0.1 reshape_squeeze.14
  3.0 0.1 pad.29.clone
  3.1 0.7 maximum_bitcast_fusion.6.refs_0_
  3.8 88.4 %gather_weights.1 = (bf16[8,2,8,136]{3,2,1,0:T(8,128)(2,1)}, bf16[8,17,8,1088]{3,2,1,0:T(8,128)(2,1)}, bf16[8,17,8,1088]{3,2,1,0:T(8,128)(2,1)}, bf16[8,17,8,108...) custom-call(bf16[2,8,136]{2,1,0:T(8,128)(2,1)} %maximum_bitcast_fusi, ...), custom_call_target="tpu_custom_call" | custom-call | tf_op jit(solution)/shard_map/gather_weights/pallas_call | solution.py:223
  92.2 0.0 copy-start.17
  92.2 0.0 copy-start.18
  92.2 0.8 convert_bitcast_fusion
  93.0 0.8 slice_convert_fusion
  93.7 0.7 reshape.194.vectors
  94.4 0.7 reshape.195.up_bias
  95.2 0.0 copy-done.5
  95.2 1.3 copy.32
  96.5 0.1 select_reduce_fusion
  96.5 0.7 fusion.3.lengths
  97.2 53.7 %forward_layer.2 = (f32[256,1088]{1,0:T(8,128)}, f32[256,1088]{1,0:T(8,128)}, f32[256,4352]{1,0:T(8,128)}, bf16[256,1088]{1,0:T(8,128)(2,1)}, bf16[2,128,128]{2,...) custom-call(s32[2]{0:T(128)} %fusion.3.lengths, f32[256,1088]{1,0:T(8,128)} %bitcast.137, ...), custom_call_target="tpu_custom_call" | custom-call | tf_op jit(solution)/shard_map/forward_layer/pallas_call | solution.py:796
  150.9 0.0 copy-start.14
  150.9 0.0 copy-start.6
  150.9 1.4 convert_element_type.115
  152.3 0.2 copy.34
  152.6 5.8 %collective-permute-start = (bf16[256,1088]{0,1:T(8,128)(2,1)S(1)}, bf16[256,1088]{0,1:T(8,128)(2,1)}, u32[]{:S(2)}, u32[]{:S(2)}) collective-permute-start(bf16[256,1088]{0,1:T(8,128)(2,1)S(1)} %copy.34), channel_id=1, source_target_pairs={{0,64},{1,65},{2,66},{3,67},{4,68},{5,69},{6,70},{7,71},{8,72},{9,... | collective-permute-start | bytes 1671176 | tf_op jit(solution)/shard_map/ppermute | solution.py:1137
  158.4 0.0 copy-done.14
  158.4 0.1 compare_convert_fusion
  158.5 0.0 copy-done.6
  158.5 0.2 copy.31
  158.7 0.0 copy-start
  158.7 1.2 bitcast_multiply_fusion.grad_output
  159.9 7.2 %collective-permute-done = bf16[256,1088]{0,1:T(8,128)(2,1)} collective-permute-done((bf16[256,1088]{0,1:T(8,128)(2,1)S(1)}, bf16[256,1088]{0,1:T(8,128)(2,1)}, u32[]{:S(2)}, u32[]{:S(2)}) %collective-permute-start) | collective-permute-done | bytes 557088 | tf_op jit(solution)/shard_map/ppermute | solution.py:1137
  167.1 1.3 copy.35
  168.4 1.1 convert_select_fusion.1.inputs
  169.6 59.4 %forward_layer.3 = (f32[256,1088]{1,0:T(8,128)}, f32[256,1088]{1,0:T(8,128)}, f32[256,4352]{1,0:T(8,128)}, bf16[256,1088]{1,0:T(8,128)(2,1)}, bf16[2,128,128]{2,...) custom-call(s32[2]{0:T(128)} %fusion.3.lengths, ...), custom_call_target="tpu_custom_call" | custom-call | tf_op jit(solution)/shard_map/forward_layer/pallas_call | solution.py:796
  229.0 54.7 %backward_layer.2 = (f32[256,1088]{1,0:T(8,128)}, bf16[256,1088]{1,0:T(8,128)(2,1)}, bf16[256,1088]{1,0:T(8,128)(2,1)}, bf16[256,1088]{1,0:T(8,128)(2,1)}, bf16[...) custom-call(s32[2]{0:T(128)} %fusion.3.lengths, ...), custom_call_target="tpu_custom_call" | custom-call | tf_op jit(solution)/shard_map/backward_layer/pallas_call | solution.py:1034
  283.7 1.3 convert_element_type.117
  285.0 0.2 copy.36
  285.3 1.5 collective-permute-start.1
  286.8 0.1 pad.26.clone
  286.8 12.0 %collective-permute-done.1 = bf16[256,1088]{0,1:T(8,128)(2,1)S(1)} collective-permute-done((bf16[256,1088]{0,1:T(8,128)(2,1)S(1)}, bf16[256,1088]{0,1:T(8,128)(2,1)S(1)}, u32[]{:S(2)}, u32[]{:S(2)}) %collective-permute-start.1) | collective-permute-done | bytes 557088 | tf_op jit(solution)/shard_map/ppermute | solution.py:1142
  298.9 0.3 copy.37
  299.2 1.4 fusion.4
  300.6 59.0 %backward_layer.3 = (f32[256,1088]{1,0:T(8,128)}, bf16[256,1088]{1,0:T(8,128)(2,1)}, bf16[256,1088]{1,0:T(8,128)(2,1)}, bf16[256,1088]{1,0:T(8,128)(2,1)}, bf16[...) custom-call(s32[2]{0:T(128)} %fusion.3.lengths, ...), custom_call_target="tpu_custom_call" | custom-call | tf_op jit(solution)/shard_map/backward_layer/pallas_call | solution.py:1034
  359.6 0.9 reshape.187
  360.5 0.8 reduce.1
  361.2 0.1 reshape.188
  361.3 0.8 maximum_maximum_fusion
  362.1 178.4 %sum_gradients.1 = (bf16[4,5,8,1088]{3,2,1,0:T(8,128)(2,1)}, bf16[4,17,8,1088]{3,2,1,0:T(8,128)(2,1)}, bf16[4,5,8,4352]{3,2,1,0:T(8,128)(2,1)}, bf16[4,5,8,1088]...) custom-call(bf16[256,1088]{1,0:T(8,128)(2,1)} %get-tuple-element.57., ...), custom_call_target="tpu_custom_call" | custom-call | tf_op jit(solution)/shard_map/sum_gradients/pallas_call | solution.py:521
  540.6 2.1 slice_bitcast_fusion.10
  542.7 1.1 slice_bitcast_fusion
  543.8 0.7 slice_bitcast_fusion.17
  544.6 0.6 copy-done.1
  545.2 0.1 slice_bitcast_fusion.7
  545.5 0.9 concatenate.33
  546.4 1.3 bitcast_convert_fusion
  547.8 1.3 slice_bitcast_fusion.27
  549.1 0.7 slice.128
  549.8 0.7 reshape.191
  550.4 1.4 broadcast_select_fusion
  551.8 1.4 copy.39
  553.2 1.7 fusion
  554.9 0.0 copy-done.2
  554.9 0.0 copy-start.8
  554.9 0.0 copy-start.9
  554.9 1.6 fusion.1
  556.5 0.9 fusion.2
  (39 shorter events, 0.4 us)
Async XLA Ops:
  0.6 2.3 copy-start.16
  0.6 2.4 copy-start.15
  3.8 91.4 %copy-start.5 = (bf16[2,1,128,1088]{2,3,1,0:T(8,128)(2,1)S(1)}, bf16[2,1,128,1088]{2,3,1,0:T(8,128)(2,1)}, u32[]{:S(2)}) copy-start(bf16[2,1,128,1088]{2,3,1,0:T(8,128)(2,1)} %param.10) | copy-start | bytes 1671172
  92.2 4.3 copy-start.17
  92.2 4.3 copy-start.18
  150.9 7.5 %copy-start.14 = (s32[2]{0:T(128)S(1)}, s32[2]{0:T(128)}, u32[]{:S(2)}) copy-start(s32[2]{0:T(128)} %fusion.3.lengths) | copy-start | bytes 28
  150.9 7.5 %copy-start.6 = (bf16[2,1,128,1088]{2,3,1,0:T(8,128)(2,1)S(1)}, bf16[2,1,128,1088]{2,3,1,0:T(8,128)(2,1)}, u32[]{:S(2)}) copy-start(bf16[2,1,128,1088]{2,3,1,0:T(8,128)(2,1)} %param.11) | copy-start | bytes 1671172
  152.6 14.5 %collective-permute-start = (bf16[256,1088]{0,1:T(8,128)(2,1)S(1)}, bf16[256,1088]{0,1:T(8,128)(2,1)}, u32[]{:S(2)}, u32[]{:S(2)}) collective-permute-start(bf16[256,1088]{0,1:T(8,128)(2,1)S(1)} %copy.34), channel_id=1, source_target_pairs={{0,64},{1,65},{2,66},{3,67},{4,68},{5,69},{6,70},{7,71},{8,72},{9,... | collective-permute-start | bytes 1671176 | tf_op jit(solution)/shard_map/ppermute | solution.py:1137
  158.7 9.7 %copy-start = (f32[2,1,128,1088]{3,2,0,1:T(8,128)S(1)}, f32[2,1,128,1088]{3,2,0,1:T(8,128)}, u32[]{:S(2)}) copy-start(f32[2,1,128,1088]{3,2,0,1:T(8,128)} %copy.32) | copy-start | bytes 3342340
  285.3 13.6 %collective-permute-start.1 = (bf16[256,1088]{0,1:T(8,128)(2,1)S(1)}, bf16[256,1088]{0,1:T(8,128)(2,1)S(1)}, u32[]{:S(2)}, u32[]{:S(2)}) collective-permute-start(bf16[256,1088]{0,1:T(8,128)(2,1)S(1)} %copy.36), channel_id=1, source_target_pairs={{64,0},{65,1},{66,2},{67,3},{68,4},{69,5},{70,6},{71,7},{72,8},{73... | collective-permute-start | bytes 1671176 | tf_op jit(solution)/shard_map/ppermute | solution.py:1142
  540.6 3.2 copy-start.12
  540.6 3.2 copy-start.13
  542.7 1.8 copy-start.10
  542.7 1.8 copy-start.11
  543.8 1.4 copy-start.1
  553.2 1.7 copy-start.2
  553.2 1.7 copy-start.3
  553.2 1.7 copy-start.4
  554.9 1.6 copy-start.7
  554.9 1.6 copy-start.8
  554.9 1.6 copy-start.9

commit v5 on v4

--- a/solution.py
+++ b/solution.py
@@ -269,9 +269,10 @@
         copy(*tile).wait()
 
 
-def sum_job(links, fill, whole, blocks, spread, total, stage, loads, buffers, out, kept):
+def sum_job(links, fill, whole, chunk, spread, total, stage, loads, buffers, out, kept):
     z, x, y, c = place()
     near = near_devices()
+    shard_blocks, chunk_first, blocks = chunk
     xc = (x + c) % 2
     cross_core = {"group": 2 * z + 1 - x, "rep": 2 * y + 1 - c}
     others = [{"rep": 2 * ((y + j) % RING) + c} for j in range(1, RING)]
@@ -295,7 +296,8 @@
         return channel
 
     def shard(k, column):
-        return whole.at[pl.ds((2 * ((z + k) % RING) + column) * blocks, blocks)]
+        slot = 2 * ((z + k) % RING) + column
+        return whole.at[pl.ds(slot * shard_blocks + chunk_first, blocks)]
 
     def rows(k, start, count):
         return total.at[k, pl.ds(start, count)]
@@ -305,7 +307,8 @@
     yield
 
     def load(n):
-        return pltpu.make_async_copy(shard(order[n], xc), stage.at[n % 2], loads.at[n % 2])
+        space = stage.at[n % 2, pl.ds(0, blocks)]
+        return pltpu.make_async_copy(shard(order[n], xc), space, loads.at[n % 2])
 
     def send_far():
         up = launch(near["above"], rows(2, first, low), far_low)
@@ -431,15 +434,17 @@
         action()
 
 
-SUM_LINKS = 160
-
-
-def sum_kernel(shapes, *refs):
-    operands, refs = refs[: SUM_OPERANDS], refs[SUM_OPERANDS:]
-    count = len(shapes)
+SUM_LINKS = 200
+SUM_ORDER = "KQDKUQKuQDVKUdDKQuPVQUSudDVPKSQdKUQKQUudDUVuUPSdVuUDVDuPSVudDVPSdDPSdPSdPS"
+SUM_OPERANDS = 11
+
+
+def sum_kernel(arrays, order, *refs):
+    operands, refs = refs[:SUM_OPERANDS], refs[SUM_OPERANDS:]
+    count = len(arrays)
     outs, refs = refs[:count], refs[count:]
-    filled = sum(1 for shape in shapes if shape[1] is not None)
-    wholes, refs = list(refs[:filled]), refs[filled:]
+    pairs = product_pairs(arrays)
+    wholes, refs = dict(zip(pairs, refs)), refs[len(pairs) :]
     send, recv, kept, sems, loads = refs[:5]
     narrow_fill, wide_fill, narrow_stage, wide_stage, tall_stage, small_stage = refs[5:11]
     refs = refs[11:]
@@ -451,61 +456,50 @@
         + [{"group": 2 * z + 1 - x, "rep": 2 * y + 1 - c}]
         + [{"rep": 2 * ((y + j) % RING) + c} for j in range(1, RING)]
     )
-    jobs = []
-    for i, (left, right, blocks, spread, offset) in enumerate(shapes):
+    jobs = {}
+    for i, (name, (left, right, chunk, spread)) in enumerate(arrays.items()):
         buffers, refs = refs[:10], refs[10:]
-        stage = narrow_stage
+        stage, fill = narrow_stage, lambda: None
         if right is None:
-            whole, stage, fill = operands[left], small_stage, (lambda: None)
+            whole, stage = operands[left], small_stage
         else:
-            whole = wholes.pop(0)
-            space = narrow_fill
+            whole, space = wholes[left, right], narrow_fill
             if outs[i].shape[-1] > 2048:
                 space, stage = wide_fill, wide_stage
             elif spread:
                 stage = tall_stage
-            fill = functools.partial(
-                product_into, operands[left], operands[right], whole, space, sems
-            )
-        job = sum_job(
-            links, fill, whole, blocks, spread, buffers[0], stage, loads, buffers[1:], outs[i], kept.at[i]
-        )
-        jobs.append((offset, job))
-    tick = 0
-    while jobs:
-        alive = []
-        for offset, job in jobs:
-            if offset == tick:
-                next(job)
-        for offset, job in jobs:
-            if offset >= tick:
-                alive.append((offset, job))
-                continue
-            try:
-                next(job)
-                alive.append((offset, job))
-            except StopIteration:
-                pass
-        jobs = alive
-        tick += 1
-
-
-SUM_OPERANDS = 11
-
-
-def sum_gradients(operands, shapes):
-    dma, vmem, hbm = pltpu.SemaphoreType.DMA, pl.BlockSpec(memory_space=pltpu.VMEM), pl.BlockSpec(memory_space=pl.ANY)
+            if chunk[1] == 0:
+                fill = functools.partial(
+                    product_into, operands[left], operands[right], whole, space, sems
+                )
+        jobs[name] = sum_job(
+            links, fill, whole, chunk, spread, buffers[0], stage, loads, buffers[1:], outs[i], kept.at[i]
+        )
+    for name in order:
+        next(jobs[name], None)
+    for job in jobs.values():
+        for _ in job:
+            pass
+
+
+def product_pairs(arrays):
+    return list(dict.fromkeys((a[0], a[1]) for a in arrays.values() if a[1] is not None))
+
+
+def sum_gradients(operands, arrays, order):
+    dma = pltpu.SemaphoreType.DMA
+    vmem, hbm = pl.BlockSpec(memory_space=pltpu.VMEM), pl.BlockSpec(memory_space=pl.ANY)
     bf16 = jnp.bfloat16
-    count = len(shapes)
-    outs, wholes, scratch = [], [], []
-    narrow_width = min(operands[right].shape[1] for _, right, *_ in shapes if right is not None)
-    wide_width = max(operands[right].shape[1] for _, right, *_ in shapes if right is not None)
-    for left, right, blocks, spread, _ in shapes:
+    outs, wholes, scratch, deepest = [], {}, [], {}
+    for left, right, chunk, spread in arrays.values():
+        shard_blocks, _, blocks = chunk
         if right is None:
             width, dtype = operands[left].shape[-1], operands[left].dtype
         else:
             width, dtype = operands[right].shape[1], bf16
-            wholes.append(jax.ShapeDtypeStruct((8 * blocks, 8, width), dtype))
+            wholes[left, right] = jax.ShapeDtypeStruct((8 * shard_blocks, 8, width), dtype)
+            kind = (width, spread)
+            deepest[kind] = max(blocks, deepest.get(kind, 0))
         piece = piece_rows(blocks)
         outs.append(jax.ShapeDtypeStruct((RING, piece, 8, width), dtype))
         size = blocks // RING if spread else blocks
@@ -516,40 +510,55 @@
         else:
             leads += [(RING - 1, piece), (piece,), (1,), (1,)]
         scratch += [pltpu.VMEM(lead + (8, width), dtype) for lead in leads]
-    blocks = {spread: b for _, right, b, spread, _ in shapes if right is not None}
+    narrow_width, wide_width = (pick(width for width, _ in deepest) for pick in (min, max))
     small_shape = operands[-1].shape
+    stages = [(narrow_width, False), (wide_width, False), (narrow_width, True)]
     return pl.pallas_call(
-        functools.partial(sum_kernel, shapes),
-        out_shape=outs + wholes,
+        functools.partial(sum_kernel, arrays, order),
+        out_shape=outs + list(wholes.values()),
         in_specs=[vmem] * (len(operands) - 1) + [hbm],
-        out_specs=[hbm] * (count + len(wholes)),
+        out_specs=[hbm] * (len(outs) + len(wholes)),
         scratch_shapes=[
             dma((SUM_LINKS,)),
             dma((SUM_LINKS,)),
-            dma((count,)),
+            dma((len(outs),)),
             dma((2,)),
             dma((2,)),
             pltpu.VMEM((2, TILE // 8, 8, narrow_width), bf16),
             pltpu.VMEM((2, TILE // 8, 8, wide_width), bf16),
-            pltpu.VMEM((2, blocks[False], 8, narrow_width), bf16),
-            pltpu.VMEM((2, blocks[False], 8, wide_width), bf16),
-            pltpu.VMEM((2, blocks[True], 8, narrow_width), bf16),
-            pltpu.VMEM((2, small_shape[0] // 8) + small_shape[1:], operands[-1].dtype),
         ]
+        + [pltpu.VMEM((2, deepest[kind], 8, kind[0]), bf16) for kind in stages]
+        + [pltpu.VMEM((2, small_shape[0] // 8) + small_shape[1:], operands[-1].dtype)]
         + scratch,
         compiler_params=pltpu.CompilerParams(
             collective_id=1, has_side_effects=True, vmem_limit_bytes=62 * 1024 * 1024
         ),
         name="sum_gradients",
-    )(*operands)[:count]
-
-
-def assemble(pieces, blocks):
-    starts = [i * blocks // RING for i in range(RING + 1)]
-    joined = jnp.concatenate(
-        [pieces[i, : starts[i + 1] - starts[i]] for i in range(RING)], 0
-    ).astype(jnp.float32)
-    return joined.reshape(-1, pieces.shape[-1])
+    )(*operands)[: len(outs)]
+
+
+def assemble_kernel(names, places, *refs):
+    outs = refs[len(names) :]
+    for name, ref in zip(names, refs):
+        output, row, column, blocks = places[name]
+        width = ref.shape[-1]
+        for i in range(RING):
+            first, end = i * blocks // RING, (i + 1) * blocks // RING
+            value = ref[i, 0 : end - first].astype(jnp.float32).reshape((end - first) * 8, width)
+            outs[output][row + first * 8 : row + end * 8, column : column + width] = value
+
+
+def assemble(sums, places, shapes):
+    names = tuple(places)
+    vmem = pl.BlockSpec(memory_space=pltpu.VMEM)
+    return pl.pallas_call(
+        functools.partial(assemble_kernel, names, places),
+        out_shape=[jax.ShapeDtypeStruct(shape, jnp.float32) for shape in shapes],
+        in_specs=[vmem] * len(names),
+        out_specs=[vmem] * len(shapes),
+        compiler_params=pltpu.CompilerParams(vmem_limit_bytes=48 * 1024 * 1024),
+        name="assemble",
+    )(*(sums[name] for name in names))
 
 
 def lane_head(shape):
@@ -638,11 +647,16 @@
 FORWARD_WEIGHTS = ("q", "k", "v", "proj", "up", "down")
 
 
+def shipment(source, arrived, send, recv):
+    device = {"pipe": 1 - lax.axis_index("pipe")}
+    return lambda m: remote(source.at[m], arrived.at[m], send.at[m], recv.at[m], device)
+
+
 def forward_kernel(
-    lengths, inputs, vectors, up_bias, wq, wk, wv, wproj, wup, wdown,
-    output, hidden_out, pre_act, attn_mixed, last_q, kept, kept_last,
-    vq, vk, vv, vproj, vup, vdown, pack, last_kv, held, held_last, staged, mixed,
-    send, recv, send_last, recv_last, send_back, recv_back, local, loaded,
+    ship, lengths, inputs, vectors, up_bias, wq, wk, wv, wproj, wup, wdown,
+    output, hidden_out, pre_act, attn_mixed, last_q, kept, kept_last, arrived,
+    vq, vk, vv, vproj, vup, vdown, pack, last_kv, held, held_last, staged, mixed, leaving,
+    send, recv, send_last, recv_last, send_back, recv_back, local, loaded, send_ship, recv_ship,
 ):
     count, micros, _, rows, lanes = pack.shape
     member, ahead = peers(count)
@@ -653,7 +667,11 @@
     ]
     for load in loads:
         load.start()
-    greet([{"group": peer} for peer in ahead])
+    devices = [{"group": peer} for peer in ahead]
+    if ship:
+        devices.append({"pipe": 1 - lax.axis_index("pipe")})
+    greet(devices)
+    ship_copy = shipment(leaving, arrived, send_ship, recv_ship)
 
     def out(m, j):
         return remote(
@@ -756,36 +774,43 @@
     for copy in keep():
         copy.start()
     for m in range(micros):
+        here = slice(m * rows, (m + 1) * rows)
         own_back(m).wait()
         for j in peer_range:
             back(m, j).wait_recv()
         for d in range(count):
-            attn_mixed[m * rows : (m + 1) * rows, d * lanes : (d + 1) * lanes] = mixed[d, m]
-    loads[3].wait()
-    hidden = inputs[...] + plain(attn_mixed[...], vproj[...]) + vectors[4:5]
-    hidden_out[...] = hidden
-    unit, _ = normalize(hidden)
-    normed = (unit * vectors[5:6] + vectors[6:7]).astype(jnp.bfloat16)
-    output[...] = hidden + vectors[7:8]
-    loads[4].wait()
-    for first, size in column_chunks(pre_act.shape[1], 1152):
-        columns = slice(first, first + size)
-        value = plain(normed, vup[:, columns]) + up_bias[:, columns]
-        pre_act[:, columns] = value
-        activated, _ = gelu_parts(value)
-        if first == 0:
+            attn_mixed[here, d * lanes : (d + 1) * lanes] = mixed[d, m]
+        if m == 0:
+            loads[3].wait()
+        hidden = inputs[here] + plain(attn_mixed[here], vproj[...]) + vectors[4:5]
+        hidden_out[here] = hidden
+        unit, _ = normalize(hidden)
+        normed = (unit * vectors[5:6] + vectors[6:7]).astype(jnp.bfloat16)
+        output[here] = hidden + vectors[7:8]
+        if m == 0:
+            loads[4].wait()
             loads[5].wait()
-        output[...] += plain(activated.astype(jnp.bfloat16), vdown[columns, :])
+        for first, size in column_chunks(pre_act.shape[1], 1152):
+            columns = slice(first, first + size)
+            value = plain(normed, vup[:, columns]) + up_bias[:, columns]
+            pre_act[here, columns] = value
+            activated, _ = gelu_parts(value)
+            output[here] += plain(activated.astype(jnp.bfloat16), vdown[columns, :])
+        if ship:
+            leaving[m] = output[here].astype(jnp.bfloat16)
+            ship_copy(m).start()
     for m in range(micros):
         for j in peer_range:
             out(m, j).wait_send()
             out_last(m, j).wait_send()
             back(m, j).wait_send()
+        if ship:
+            ship_copy(m).wait()
     for copy in keep():
         copy.wait()
 
 
-def forward_layer(lengths, inputs, vectors, up_bias, weights, count, micros):
+def forward_layer(ship, lengths, inputs, vectors, up_bias, weights, count, micros):
     total, width = inputs.shape
     rows, lanes = total // micros, LANES
     hidden = weights[4].shape[1]
@@ -794,7 +819,7 @@
     dma = pltpu.SemaphoreType.DMA
     pack, blocks = (count, micros, 3, rows, lanes), (count, micros, rows, lanes)
     return pl.pallas_call(
-        forward_kernel,
+        functools.partial(forward_kernel, ship),
         out_shape=[
             jax.ShapeDtypeStruct((total, width), f32),
             jax.ShapeDtypeStruct((total, width), f32),
@@ -803,9 +828,10 @@
             jax.ShapeDtypeStruct((micros, rows, lanes), bf16),
             jax.ShapeDtypeStruct(pack, bf16),
             jax.ShapeDtypeStruct(blocks, bf16),
+            jax.ShapeDtypeStruct((micros, rows, width), bf16),
         ],
         in_specs=[pl.BlockSpec(memory_space=pltpu.SMEM)] + [vmem] * 3 + [hbm] * 6,
-        out_specs=[vmem] * 5 + [hbm] * 2,
+        out_specs=[vmem] * 5 + [hbm] * 3,
         scratch_shapes=[pltpu.VMEM(w.shape, bf16) for w in weights]
         + [
             pltpu.VMEM(pack, bf16),
@@ -814,24 +840,25 @@
             pltpu.VMEM(blocks, bf16),
             pltpu.VMEM(blocks, bf16),
             pltpu.VMEM(blocks, bf16),
+            pltpu.VMEM((micros, rows, width), bf16),
         ]
         + [dma((micros, count - 1))] * 6
-        + [dma((micros, 4)), dma((6,))],
+        + [dma((micros, 4)), dma((6,)), dma((micros,)), dma((micros,))],
         compiler_params=pltpu.CompilerParams(
-            collective_id=2, has_side_effects=True, vmem_limit_bytes=60 * 1024 * 1024
+            collective_id=4 if ship else 2, has_side_effects=True, vmem_limit_bytes=60 * 1024 * 1024
         ),
-        name="forward_layer",
+        name="forward_ship" if ship else "forward_layer",
     )(lengths, inputs, vectors, up_bias, *weights)
 
 
 def backward_kernel(
-    lengths, grad_output, inputs, hidden, vectors, pre_act, held, held_last, last_q,
+    ship, lengths, grad_output, inputs, hidden, vectors, pre_act, held, held_last, last_q,
     wq, wk, wv, wproj, wup, wdown,
     grad_in, grad_q, grad_k, grad_v, grad_one, grad_pre, activated, normed_one, normed_two,
-    vector_grads, bias_grads,
+    vector_grads, bias_grads, arrived,
     vproj, vup, vdown, vqkv, grad_norm, grad_pack, last_grad, came, staged, staged_last, grads, parts_last,
-    key_total, value_total, last_query_grad,
-    send, recv, send_back, recv_back, send_last, recv_last, local, loaded,
+    key_total, value_total, last_query_grad, leaving,
+    send, recv, send_back, recv_back, send_last, recv_last, local, loaded, send_ship, recv_ship,
 ):
     count, micros, _, rows, lanes = held.shape
     member, ahead = peers(count)
@@ -852,7 +879,11 @@
     ]
     for load in loads:
         load.start()
-    greet([{"group": peer} for peer in ahead])
+    devices = [{"group": peer} for peer in ahead]
+    if ship:
+        devices.append({"pipe": 1 - lax.axis_index("pipe")})
+    greet(devices)
+    ship_copy = shipment(leaving, arrived, send_ship, recv_ship)
 
     def out(m, j):
         return remote(
@@ -1004,25 +1035,38 @@
         for third, target in enumerate((grad_q, grad_k, grad_v)):
             for d in range(count):
                 target[here, d * lanes : (d + 1) * lanes] = grads[d, m, third]
+        if m == 0:
+            for i in (3, 4, 5):
+                loads[i].wait()
+        pulled = over_lanes(grad_q[here], vqkv[0])
+        pulled += over_lanes(grad_k[here], vqkv[1])
+        pulled += over_lanes(grad_v[here], vqkv[2])
+        from_norm, gain_sum, bias_sum = norm_back(
+            unit[here], deviation[here], vectors[0:1], pulled
+        )
+        total = grad_norm[here] + from_norm
+        grad_in[here] = total
+        if ship:
+            leaving[m] = total.astype(jnp.bfloat16)
+            ship_copy(m).start()
+        if m == 0:
+            vector_grads[0:1] = gain_sum
+            vector_grads[1:2] = bias_sum
+        else:
+            vector_grads[0:1] += gain_sum
+            vector_grads[1:2] += bias_sum
     vector_grads[2:3] = column_sum(grad_q[...])
     vector_grads[3:4] = column_sum(grad_v[...])
-    for i in (3, 4, 5):
-        loads[i].wait()
-    pulled = over_lanes(grad_q[...], vqkv[0])
-    pulled += over_lanes(grad_k[...], vqkv[1])
-    pulled += over_lanes(grad_v[...], vqkv[2])
-    from_norm, gain_sum, bias_sum = norm_back(unit, deviation, vectors[0:1], pulled)
-    vector_grads[0:1] = gain_sum
-    vector_grads[1:2] = bias_sum
-    grad_in[...] = grad_norm[...] + from_norm
     for m in range(micros):
         for j in peer_range:
             out(m, j).wait_send()
             back_last(m, j).wait_send()
             back(m, j).wait_send()
-
-
-def backward_layer(lengths, grad_output, saved, vectors, weights):
+        if ship:
+            ship_copy(m).wait()
+
+
+def backward_layer(ship, lengths, grad_output, saved, vectors, weights):
     inputs, hidden, pre_act, held, held_last, last_q = saved
     count, micros, _, rows, lanes = held.shape
     total, width = inputs.shape
@@ -1032,7 +1076,7 @@
     narrow_out, wide_out = (total, width), pre_act.shape
     blocks, pack = (count, micros, rows, lanes), (count, micros, 3, rows, lanes)
     return pl.pallas_call(
-        backward_kernel,
+        functools.partial(backward_kernel, ship),
         out_shape=[
             jax.ShapeDtypeStruct(shape, dtype)
             for shape, dtype in (
@@ -1047,10 +1091,11 @@
                 (narrow_out, bf16),
                 ((8, width), f32),
                 ((1, pre_act.shape[1]), f32),
+                ((micros, rows, width), bf16),
             )
         ],
         in_specs=[pl.BlockSpec(memory_space=pltpu.SMEM)] + [vmem] * 8 + [hbm] * 6,
-        out_specs=[vmem] * 11,
+        out_specs=[vmem] * 11 + [hbm],
         scratch_shapes=[
             pltpu.VMEM(weights[3].shape, bf16),
             pltpu.VMEM(weights[4].shape, bf16),
@@ -1067,13 +1112,14 @@
             pltpu.VMEM((count * rows, lanes), f32),
             pltpu.VMEM((count * rows, lanes), f32),
             pltpu.VMEM((micros, rows, lanes), bf16),
+            pltpu.VMEM((micros, rows, width), bf16),
         ]
         + [dma((micros, count - 1))] * 6
-        + [dma((micros, 3)), dma((6,))],
+        + [dma((micros, 3)), dma((6,)), dma((micros,)), dma((micros,))],
         compiler_params=pltpu.CompilerParams(
-            collective_id=3, has_side_effects=True, vmem_limit_bytes=62 * 1024 * 1024
+            collective_id=5 if ship else 3, has_side_effects=True, vmem_limit_bytes=62 * 1024 * 1024
         ),
-        name="backward_layer",
+        name="backward_ship" if ship else "backward_layer",
     )(lengths, grad_output, inputs, hidden, vectors, pre_act, held, held_last, last_q, *weights)
 
 
@@ -1129,22 +1175,23 @@
     up_bias = small_full[:, 1, :bias_rows].reshape(1, -1).astype(jnp.float32)
     weights = [array.reshape(-1, array.shape[-1]) for array in full]
 
-    def forward(inputs):
-        return forward_layer(lengths, inputs, vector_rows, up_bias, weights, count, micros)
+    def forward(ship, inputs):
+        return forward_layer(ship, lengths, inputs, vector_rows, up_bias, weights, count, micros)
+
+    def landed(blocks):
+        return blocks.reshape(micros * rows, width).astype(jnp.float32)
 
     first_in = block_input[:, 0].reshape(micros * rows, width).astype(jnp.float32)
-    first_out = forward(first_in)[0]
-    arrived = lax.ppermute(first_out.astype(jnp.bfloat16), "pipe", [(0, 1)])
-    inputs = jnp.where(section == 0, first_in, arrived.astype(jnp.float32))
-    output, hidden, pre_act, attn_mixed, last_q, held, held_last = forward(inputs)
+    *_, arrived = forward(True, first_in)
+    inputs = jnp.where(section == 0, first_in, landed(arrived))
+    output, hidden, pre_act, attn_mixed, last_q, held, held_last, _ = forward(False, inputs)
     saved = (inputs, hidden, pre_act, held, held_last, last_q)
-    last_grad = backward_layer(lengths, cotangent, saved, vector_rows, weights)[0]
-    arrived = lax.ppermute(last_grad.astype(jnp.bfloat16), "pipe", [(1, 0)])
-    grad_output = jnp.where(section == 1, cotangent, arrived.astype(jnp.float32))
+    *_, arrived = backward_layer(True, lengths, cotangent, saved, vector_rows, weights)
+    grad_output = jnp.where(section == 1, cotangent, landed(arrived))
     (
         grad_in, grad_q, grad_k, grad_v, grad_one, grad_pre, activated, normed_one, normed_two,
-        grad_vectors, grad_bias,
-    ) = backward_layer(lengths, grad_output, saved, vector_rows, weights)
+        grad_vectors, grad_bias, _,
+    ) = backward_layer(False, lengths, grad_output, saved, vector_rows, weights)
 
     small_grads = jnp.concatenate(
         [
@@ -1156,32 +1203,47 @@
     ).reshape(count * RING, 8, width // count)
     blocks = width // count // 8
     tall = grad_pre.shape[1] // count // 8
+    half, tall_half = (blocks + 1) // 2, tall // 8 * 4 + 4
+    arrays = {
+        "Q": (0, 1, (blocks, 0, blocks), False),
+        "K": (0, 2, (blocks, 0, blocks), False),
+        "V": (0, 3, (blocks, 0, blocks), False),
+        "P": (4, 5, (blocks, 0, blocks), False),
+        "U": (6, 7, (blocks, 0, half), False),
+        "u": (6, 7, (blocks, half, blocks - half), False),
+        "D": (8, 9, (tall, 0, tall_half), True),
+        "d": (8, 9, (tall, tall_half, tall - tall_half), True),
+        "S": (10, None, (RING, 0, RING), False),
+    }
     sums = sum_gradients(
         (
             normed_one, grad_q, grad_k, grad_v, attn_mixed, grad_one, normed_two, grad_pre, activated,
             grad_output.astype(jnp.bfloat16), small_grads,
         ),
-        (
-            (0, 1, blocks, False, 0),
-            (8, 9, tall, True, 0),
-            (6, 7, blocks, False, 1),
-            (0, 2, blocks, False, 2),
-            (0, 3, blocks, False, 3),
-            (4, 5, blocks, False, 4),
-            (10, None, RING, False, 5),
-        ),
+        arrays,
+        SUM_ORDER,
     )
-    grad_q, down, up, grad_k, grad_v, proj = (
-        assemble(total, tall if i == 1 else blocks) for i, total in enumerate(sums[:6])
-    )
-    small_total = sums[6].reshape(RING * 8, -1)
+    sums = dict(zip(arrays, sums))
+    places = {
+        "Q": (0, 0, 0, blocks),
+        "K": (0, 0, width, blocks),
+        "V": (0, 0, 2 * width, blocks),
+        "P": (1, 0, 0, blocks),
+        "U": (2, 0, 0, half),
+        "u": (2, half * 8, 0, blocks - half),
+        "D": (3, 0, 0, tall_half),
+        "d": (3, tall_half * 8, 0, tall - tall_half),
+    }
+    grad_shapes = [(w.shape[1], w.shape[2]) for w in (w_qkv, w_proj, w_up, w_down)]
+    totals = assemble(sums, places, grad_shapes)
+    small_total = sums["S"].reshape(RING * 8, -1)
     edges = jnp.where(section == 0, grad_in, output).reshape(1, micros, 1, rows, width)
     return (
         edges,
-        jnp.concatenate([grad_q, grad_k, grad_v], 1)[None],
-        proj[None],
-        up[None],
-        down[None],
+        totals[0][None],
+        totals[1][None],
+        totals[2][None],
+        totals[3][None],
         small_total[None, :8],
         small_total[8 : 8 + bias_rows].reshape(1, -1),
     )

time: 569 us -> 509 us (0.89)
  Pallas kernels: 494 us -> 469 us
  waiting for transfers between devices: 19.2 us -> 0 us
  other arithmetic: 18.1 us -> 9.79 us
  starting transfers between devices: 7.26 us -> 0 us
    pallas_call x5 -> x6, Pallas kernels: 405 us -> 381 us  [the longest x1 143 us: sum_gradients(): pl.pallas_call(functools.partial(sum_kernel, arrays, order), out_shape=ou...]
    ppermute x2 -> x0, waiting for transfers between devices: 19.2 us -> none  [the longest x1 12 us: body(): arrived = lax.ppermute(last_grad.astype(jnp.bfloat16), 'pipe', [(1, 0)])]
    unnamed x39, local copies, waits for them, and re-layouts: 2.04 us -> 10.6 us
    ppermute x2 -> x0, starting transfers between devices: 7.26 us -> none  [the longest x1 5.79 us: body(): arrived = lax.ppermute(first_out.astype(jnp.bfloat16), 'pipe', [(0, 1)])]
    convert_element_type x8 -> x0, other arithmetic: 7.05 us -> none  [the longest x6 4.32 us: assemble(): joined = jnp.concatenate([pieces[i, :starts[i + 1] - starts[i]] for i in...]
  transfers between devices with their start and end apart: 2 -> 0, of which waited for: 2 -> 0; matrix products, arithmetic and copies ran while one was open for 0% -> 0% of each run, Pallas kernels for 0% -> 0%
where the time goes in v5:
time: 509 us; the launch traced here: 499 us
  Pallas kernels  469 us (92%)
  local copies, waits for them, and re-layouts  19.7 us (4%)
  other arithmetic  9.79 us (2%)
    pallas_call x1, Pallas kernels, sum_gradients(): pl.pallas_call(functools.partial(sum_kernel, arrays, order), out_shape=ou...  143 us
    pallas_call x2, Pallas kernels, backward_layer(): pl.pallas_call(functools.partial(backward_kernel, ship), out_shape=[jax.S...  121 us
    pallas_call x2, Pallas kernels, forward_layer(): pl.pallas_call(functools.partial(forward_kernel, ship), out_shape=[jax.Sh...  113 us
    pallas_call x1, Pallas kernels, gather_weights(): pl.pallas_call(functools.partial(gather_kernel, plan, count), out_shape=[...  88.4 us
    unnamed x39, local copies, waits for them, and re-layouts  10.6 us

profile of v5, /device:TPU:1, one launch (start us, length us, event | category | flops | bytes accessed | tf_op | source)
XLA Modules:
  0.0 499.4 jit_solution(2848629432842018240)
XLA Ops:
  0.6 0.0 copy-start.16
  0.6 0.0 copy-start.15
  0.7 2.2 slice_bitcast_fusion
  2.9 0.0 copy-done.16
  2.9 0.1 reshape_squeeze.14
  3.0 0.1 pad.5.clone
  3.1 0.0 copy-done.15
  3.1 0.7 maximum_bitcast_fusion.refs_0_
  3.8 0.0 copy-start.17
  3.8 0.0 copy-start.18
  3.8 0.0 copy-start.12
  3.8 88.4 %gather_weights.1 = (bf16[8,2,8,136]{3,2,1,0:T(8,128)(2,1)}, bf16[8,17,8,1088]{3,2,1,0:T(8,128)(2,1)}, bf16[8,17,8,1088]{3,2,1,0:T(8,128)(2,1)}, bf16[8,17,8,108...) custom-call(bf16[2,8,136]{2,1,0:T(8,128)(2,1)} %maximum_bitcast_fusi, ...), custom_call_target="tpu_custom_call" | custom-call | tf_op jit(solution)/shard_map/gather_weights/pallas_call | solution.py:223
  92.2 0.8 convert_bitcast_fusion
  93.0 0.7 reshape.152.vectors
  93.7 0.8 slice_convert_fusion
  94.4 0.7 reshape.153.up_bias
  95.2 0.0 copy-done.17
  95.2 0.0 copy-done.18
  95.2 0.1 select_reduce_fusion
  95.2 0.7 fusion.lengths
  95.9 0.0 copy-done.12
  95.9 1.3 copy.23
  97.2 0.0 copy-start.14
  97.2 0.0 copy-start.13
  97.2 61.8 %forward_ship.1 = (f32[256,1088]{1,0:T(8,128)}, f32[256,1088]{1,0:T(8,128)}, f32[256,4352]{1,0:T(8,128)}, bf16[256,1088]{1,0:T(8,128)(2,1)}, bf16[2,128,128]{2,1...) custom-call(s32[2]{0:T(128)} %fusion.lengths, ...), custom_call_target="tpu_custom_call" | custom-call | tf_op jit(solution)/shard_map/forward_ship/pallas_call | solution.py:821
  159.0 0.0 copy-start.9
  159.1 0.0 copy-done.14
  159.1 0.1 compare_convert_fusion
  159.1 0.0 copy-done.13
  159.1 0.2 copy.22
  159.4 0.9 copy-done.9
  160.3 2.6 convert_select_fusion.1
  162.9 51.7 %forward_layer.1 = (f32[256,1088]{1,0:T(8,128)}, f32[256,1088]{1,0:T(8,128)}, f32[256,4352]{1,0:T(8,128)}, bf16[256,1088]{1,0:T(8,128)(2,1)}, bf16[2,128,128]{2,...) custom-call(s32[2]{0:T(128)} %fusion.lengths, ...), custom_call_target="tpu_custom_call" | custom-call | tf_op jit(solution)/shard_map/forward_layer/pallas_call | solution.py:821
  214.6 0.0 copy-start.8
  214.6 65.5 %backward_ship.1 = (f32[256,1088]{1,0:T(8,128)}, bf16[256,1088]{1,0:T(8,128)(2,1)}, bf16[256,1088]{1,0:T(8,128)(2,1)}, bf16[256,1088]{1,0:T(8,128)(2,1)}, bf16[2...) custom-call(s32[2]{0:T(128)} %fusion.lengths, ...), custom_call_target="tpu_custom_call" | custom-call | tf_op jit(solution)/shard_map/backward_ship/pallas_call | solution.py:1078
  280.1 0.0 copy-done.8
  280.1 2.4 fusion.1
  282.5 55.1 %backward_layer.1 = (f32[256,1088]{1,0:T(8,128)}, bf16[256,1088]{1,0:T(8,128)(2,1)}, bf16[256,1088]{1,0:T(8,128)(2,1)}, bf16[256,1088]{1,0:T(8,128)(2,1)}, bf16[...) custom-call(s32[2]{0:T(128)} %fusion.lengths, ...), custom_call_target="tpu_custom_call" | custom-call | tf_op jit(solution)/shard_map/backward_layer/pallas_call | solution.py:1078
  337.6 0.9 reshape.145
  338.5 0.8 reduce.1
  339.3 0.1 reshape.146
  339.4 0.1 pad.2.clone
  339.5 0.8 maximum_maximum_fusion
  340.3 143.3 %sum_gradients.1 = (bf16[4,5,8,1088]{3,2,1,0:T(8,128)(2,1)}, bf16[4,5,8,1088]{3,2,1,0:T(8,128)(2,1)}, bf16[4,5,8,1088]{3,2,1,0:T(8,128)(2,1)}, bf16[4,5,8,1088]{...) custom-call(bf16[256,1088]{1,0:T(8,128)(2,1)} %get-tuple-element.63., ...), custom_call_target="tpu_custom_call" | custom-call | tf_op jit(solution)/shard_map/sum_gradients/pallas_call | solution.py:516
  483.6 0.0 copy-start
  483.6 1.1 copy-done
  484.7 0.0 copy-start.1
  484.7 1.1 copy-done.1
  485.8 0.0 copy-start.2
  485.8 1.1 copy-done.2
  486.9 0.0 copy-start.3
  486.9 1.1 copy-done.3
  487.9 1.0 copy-done.4
  488.9 1.0 copy-done.5
  489.9 1.0 copy-done.6
  490.9 1.0 copy-done.7
  491.9 3.2 assemble.1
  495.1 1.3 slice_bitcast_fusion.3
  496.4 0.7 slice.32
  497.1 0.7 reshape.149
  497.7 0.0 copy-done.10
  497.7 0.0 copy-done.11
  497.7 0.1 broadcast_select_fusion
  497.9 1.4 copy.26
  (14 shorter events, 0.1 us)
Async XLA Ops:
  0.6 2.3 copy-start.16
  0.6 2.4 copy-start.15
  3.8 91.4 %copy-start.17 = (s32[16]{0:T(128)S(1)}, s32[16]{0:T(128)}, u32[]{:S(2)}) copy-start(s32[16]{0:T(128)} %param.18) | copy-start | bytes 196
  3.8 91.4 %copy-start.18 = (s32[16]{0:T(128)S(1)}, s32[16]{0:T(128)}, u32[]{:S(2)}) copy-start(s32[16]{0:T(128)} %param.19) | copy-start | bytes 196
  3.8 92.2 %copy-start.12 = (bf16[2,1,128,1088]{2,3,1,0:T(8,128)(2,1)S(1)}, bf16[2,1,128,1088]{2,3,1,0:T(8,128)(2,1)}, u32[]{:S(2)}) copy-start(bf16[2,1,128,1088]{2,3,1,0:T(8,128)(2,1)} %param.10) | copy-start | bytes 1671172
  97.2 61.8 %copy-start.14 = (s32[2]{0:T(128)S(1)}, s32[2]{0:T(128)}, u32[]{:S(2)}) copy-start(s32[2]{0:T(128)} %fusion.lengths) | copy-start | bytes 28
  97.2 61.9 %copy-start.13 = (bf16[2,1,128,1088]{2,3,1,0:T(8,128)(2,1)S(1)}, bf16[2,1,128,1088]{2,3,1,0:T(8,128)(2,1)}, u32[]{:S(2)}) copy-start(bf16[2,1,128,1088]{2,3,1,0:T(8,128)(2,1)} %param.11) | copy-start | bytes 1671172
  159.0 1.3 copy-start.9
  214.6 65.6 %copy-start.8 = (f32[256,1088]{1,0:T(8,128)S(1)}, f32[256,1088]{1,0:T(8,128)}, u32[]{:S(2)}) copy-start(f32[256,1088]{1,0:T(8,128)} %get-tuple-element.107.grad_output) | copy-start | bytes 3342340
  483.6 1.2 copy-start
  484.7 1.1 copy-start.1
  485.8 1.1 copy-start.2
  486.9 1.1 copy-start.3
  487.9 1.0 copy-start.4
  488.9 1.0 copy-start.5
  489.9 1.0 copy-start.6
  490.9 1.0 copy-start.7
  491.9 5.8 %copy-start.10 = (f32[256,1088]{1,0:T(8,128)S(1)}, f32[256,1088]{1,0:T(8,128)}, u32[]{:S(2)}) copy-start(f32[256,1088]{1,0:T(8,128)} %get-tuple-element.62) | copy-start | bytes 3342340
  491.9 5.8 %copy-start.11 = (f32[256,1088]{1,0:T(8,128)S(1)}, f32[256,1088]{1,0:T(8,128)}, u32[]{:S(2)}) copy-start(f32[256,1088]{1,0:T(8,128)} %get-tuple-element.61) | copy-start | bytes 3342340

commit v6 on v5

--- a/solution.py
+++ b/solution.py
@@ -192,43 +192,46 @@
 MAX_LINKS = 160
 
 
-ORDER = "SPSSSPSPSP"
-
-
-def gather_kernel(plan, count, *refs):
-    ins, outs = refs[:count], refs[count : 2 * count]
-    links = Links(*refs[2 * count :])
+GATHER_ORDER = "SPSPSSPP"
+
+
+def gather_steps(links, plan, ins, outs):
     member = lax.axis_index("group")
-    greet(list(near_devices().values()))
+    count = len(ins)
     spread = [gather_job(links, ins[i], outs[i], *rest) for i, *rest in plan if rest[-1]]
     whole = [gather_job(links, ins[i], outs[i], *rest) for i, *rest in plan if not rest[-1]]
     owns = [links.channel(near_devices()["sibling"]) for _ in range(count)]
-    for step, which in enumerate(ORDER):
+    for step, which in enumerate(GATHER_ORDER):
         for job in spread if which == "S" else whole:
             next(job)
         if step == 1:
             for i in range(count):
                 owns[i].send(ins[i], outs[i].at[member])
-    for job in spread + whole:
+    for job in whole:
         for _ in job:
             pass
     for i in range(count):
         owns[i].came(outs[i].at[member])
         owns[i].sent(ins[i])
-
-
-def gather_weights(shards, plan):
-    count = len(shards)
-    dma = pltpu.SemaphoreType.DMA
-    return pl.pallas_call(
-        functools.partial(gather_kernel, plan, count),
-        out_shape=[jax.ShapeDtypeStruct((8,) + s.shape, s.dtype) for s in shards],
-        in_specs=[pl.BlockSpec(memory_space=pl.ANY)] * count,
-        out_specs=[pl.BlockSpec(memory_space=pl.ANY)] * count,
-        scratch_shapes=[dma((MAX_LINKS,)), dma((MAX_LINKS,))],
-        compiler_params=pltpu.CompilerParams(collective_id=0, has_side_effects=True),
-        name="gather_weights",
-    )(*shards)
+    yield
+    for job in spread:
+        next(job)
+    yield
+    for job in spread:
+        for _ in job:
+            pass
+    yield
+
+
+def spread_vectors(small, vectors, up_bias):
+    members, _, _, columns = small.shape
+    bias_rows = up_bias.shape[1] // (members * columns)
+    for member in range(members):
+        first = member * columns
+        vectors[:, first : first + columns] = small[member, 0].astype(jnp.float32)
+        for row in range(bias_rows):
+            first = (member * bias_rows + row) * columns
+            up_bias[:, first : first + columns] = small[member, 1, row : row + 1].astype(jnp.float32)
 
 
 def piece_rows(blocks):
@@ -435,7 +438,7 @@
 
 
 SUM_LINKS = 200
-SUM_ORDER = "KQDKUQKuQDVKUdDKQuPVQUSudDVPKSQdKUQKQUudDUVuUPSdVuUDVDuPSVudDVPSdDPSdPSdPS"
+SUM_ORDER = ("KQDKUQKuQDVKUdDKQuPVQUSudDVPKSQdKUQKQUud", "DUVuUPSdVuUDVDuPSVudDVPSdDPSdPSdPS")
 SUM_OPERANDS = 11
 
 
@@ -475,7 +478,7 @@
         jobs[name] = sum_job(
             links, fill, whole, chunk, spread, buffers[0], stage, loads, buffers[1:], outs[i], kept.at[i]
         )
-    for name in order:
+    for name in "".join(order):
         next(jobs[name], None)
     for job in jobs.values():
         for _ in job:
@@ -538,8 +541,17 @@
 
 
 def assemble_kernel(names, places, *refs):
-    outs = refs[len(names) :]
-    for name, ref in zip(names, refs):
+    sources, refs = refs[: len(names)], refs[len(names) :]
+    loaded, sems = refs[-1 - len(names) : -1], refs[-1]
+    outs = refs[: -1 - len(names)]
+    loads = [
+        pltpu.make_async_copy(source, ref, sems.at[i])
+        for i, (source, ref) in enumerate(zip(sources, loaded))
+    ]
+    for load in loads:
+        load.start()
+    for name, ref, load in zip(names, loaded, loads):
+        load.wait()
         output, row, column, blocks = places[name]
         width = ref.shape[-1]
         for i in range(RING):
@@ -550,13 +562,15 @@
 
 def assemble(sums, places, shapes):
     names = tuple(places)
-    vmem = pl.BlockSpec(memory_space=pltpu.VMEM)
+    vmem, hbm = pl.BlockSpec(memory_space=pltpu.VMEM), pl.BlockSpec(memory_space=pl.ANY)
     return pl.pallas_call(
         functools.partial(assemble_kernel, names, places),
         out_shape=[jax.ShapeDtypeStruct(shape, jnp.float32) for shape in shapes],
-        in_specs=[vmem] * len(names),
+        in_specs=[hbm] * len(names),
         out_specs=[vmem] * len(shapes),
-        compiler_params=pltpu.CompilerParams(vmem_limit_bytes=48 * 1024 * 1024),
+        scratch_shapes=[pltpu.VMEM(sums[name].shape, sums[name].dtype) for name in names]
+        + [pltpu.SemaphoreType.DMA((len(names),))],
+        compiler_params=pltpu.CompilerParams(vmem_limit_bytes=62 * 1024 * 1024),
         name="assemble",
     )(*(sums[name] for name in names))
 
@@ -645,6 +659,77 @@
 
 
 FORWARD_WEIGHTS = ("q", "k", "v", "proj", "up", "down")
+
+
+def first_kernel(plan, count, *refs):
+    lengths, inputs = refs[:2]
+    shards, fulls = refs[2 : 2 + count], refs[2 + count : 2 + 2 * count]
+    arrived, refs = refs[2 + 2 * count], refs[3 + 2 * count :]
+    vectors, up_bias, small, send, recv, loaded, *refs = refs
+    near = near_devices()
+    member, ahead = peers(8)
+    greet(
+        [{"group": peer} for peer in ahead]
+        + [near[name] for name in ("sibling", "next", "last")]
+        + [{"pipe": 1 - lax.axis_index("pipe")}]
+    )
+    steps = gather_steps(Links(send, recv), plan, shards, fulls)
+    next(steps)
+    load = pltpu.make_async_copy(fulls[0], small, loaded)
+    load.start()
+    load.wait()
+    spread_vectors(small, vectors, up_bias)
+    outputs, scratch = refs[:7], refs[7:]
+    forward_kernel(
+        steps, lengths, inputs, vectors, up_bias, *fulls[1:], *outputs, arrived, *scratch
+    )
+
+
+def first_layer(lengths, inputs, shards, plan, count, micros):
+    total, width = inputs.shape
+    rows, lanes, hidden = total // micros, LANES, shards[5].shape[2]
+    bf16, f32 = jnp.bfloat16, jnp.float32
+    vmem, hbm = pl.BlockSpec(memory_space=pltpu.VMEM), pl.BlockSpec(memory_space=pl.ANY)
+    dma = pltpu.SemaphoreType.DMA
+    pack, blocks = (count, micros, 3, rows, lanes), (count, micros, rows, lanes)
+    return pl.pallas_call(
+        functools.partial(first_kernel, plan, len(shards)),
+        out_shape=[jax.ShapeDtypeStruct((8,) + s.shape, s.dtype) for s in shards]
+        + [jax.ShapeDtypeStruct((micros, rows, width), bf16)],
+        in_specs=[pl.BlockSpec(memory_space=pltpu.SMEM), vmem] + [hbm] * len(shards),
+        out_specs=[hbm] * (len(shards) + 1),
+        scratch_shapes=[
+            pltpu.VMEM((8, width), f32),
+            pltpu.VMEM((1, hidden), f32),
+            pltpu.VMEM((8,) + shards[0].shape, bf16),
+            dma((MAX_LINKS,)),
+            dma((MAX_LINKS,)),
+            dma,
+            pltpu.VMEM((total, width), f32),
+            pltpu.VMEM((total, width), f32),
+            pltpu.VMEM((total, hidden), f32),
+            pltpu.VMEM((total, width), bf16),
+            pltpu.VMEM((micros, rows, lanes), bf16),
+            pltpu.VMEM((8, 8), f32),
+            pltpu.VMEM((8, 8), f32),
+        ]
+        + [pltpu.VMEM((s.shape[0] * 64, s.shape[2]), bf16) for s in shards[1:]]
+        + [
+            pltpu.VMEM(pack, bf16),
+            pltpu.VMEM((micros, rows, lanes), bf16),
+            pltpu.VMEM(pack, bf16),
+            pltpu.VMEM(blocks, bf16),
+            pltpu.VMEM(blocks, bf16),
+            pltpu.VMEM(blocks, bf16),
+            pltpu.VMEM((micros, rows, width), bf16),
+        ]
+        + [dma((micros, count - 1))] * 6
+        + [dma((micros, 4)), dma((6,)), dma((micros,)), dma((micros,))],
+        compiler_params=pltpu.CompilerParams(
+            collective_id=0, has_side_effects=True, vmem_limit_bytes=62 * 1024 * 1024
+        ),
+        name="gather_forward",
+    )(lengths, inputs, *shards)
 
 
 def shipment(source, arrived, send, recv):
@@ -663,14 +748,15 @@
     wide = count * lanes
     sources, places = (wq, wk, wv, wproj, wup, wdown), (vq, vk, vv, vproj, vup, vdown)
     loads = [
-        pltpu.make_async_copy(sources[i], places[i], loaded.at[i]) for i in range(len(sources))
+        pltpu.make_async_copy(sources[i].reshape(places[i].shape), places[i], loaded.at[i])
+        if ship
+        else pltpu.make_async_copy(sources[i], places[i], loaded.at[i])
+        for i in range(len(sources))
     ]
-    for load in loads:
+    for load in loads[:4] if ship else loads:
         load.start()
-    devices = [{"group": peer} for peer in ahead]
-    if ship:
-        devices.append({"pipe": 1 - lax.axis_index("pipe")})
-    greet(devices)
+    if not ship:
+        greet([{"group": peer} for peer in ahead])
     ship_copy = shipment(leaving, arrived, send_ship, recv_ship)
 
     def out(m, j):
@@ -770,8 +856,14 @@
         attn_mixed[m * rows : (m + 1) * rows, wide:] = narrow(last_out, HEAD)
 
     for m in range(micros):
+        if ship and m == 0:
+            next(ship)
         micro(m)
-    for copy in keep():
+        if ship and m == 0:
+            next(ship)
+            for load in loads[4:]:
+                load.start()
+    for copy in () if ship else keep():
         copy.start()
     for m in range(micros):
         here = slice(m * rows, (m + 1) * rows)
@@ -806,11 +898,35 @@
             back(m, j).wait_send()
         if ship:
             ship_copy(m).wait()
-    for copy in keep():
+    for copy in () if ship else keep():
         copy.wait()
 
 
-def forward_layer(ship, lengths, inputs, vectors, up_bias, weights, count, micros):
+def results_in_scratch(kernel, inputs, results):
+    def run(*refs):
+        before, last, rest = refs[:inputs], refs[inputs], refs[inputs + 1 :]
+        kernel(*before, *rest[: results - 1], last, *rest[results - 1 :])
+
+    return run
+
+
+def layer_call(kernel, ship, operands, in_specs, results, spaces, scratch, **options):
+    kernel = functools.partial(kernel, ship)
+    if ship:
+        kernel = results_in_scratch(kernel, len(operands), len(results))
+        scratch = [pltpu.VMEM(r.shape, r.dtype) for r in results[:-1]] + scratch
+        results, spaces = results[-1:], spaces[-1:]
+    return pl.pallas_call(
+        kernel,
+        out_shape=results,
+        in_specs=in_specs,
+        out_specs=spaces,
+        scratch_shapes=scratch,
+        **options,
+    )(*operands)
+
+
+def forward_layer(lengths, inputs, vectors, up_bias, weights, count, micros):
     total, width = inputs.shape
     rows, lanes = total // micros, LANES
     hidden = weights[4].shape[1]
@@ -818,9 +934,12 @@
     vmem, hbm = pl.BlockSpec(memory_space=pltpu.VMEM), pl.BlockSpec(memory_space=pl.ANY)
     dma = pltpu.SemaphoreType.DMA
     pack, blocks = (count, micros, 3, rows, lanes), (count, micros, rows, lanes)
-    return pl.pallas_call(
-        functools.partial(forward_kernel, ship),
-        out_shape=[
+    return layer_call(
+        forward_kernel,
+        False,
+        (lengths, inputs, vectors, up_bias, *weights),
+        [pl.BlockSpec(memory_space=pltpu.SMEM)] + [vmem] * 3 + [hbm] * 6,
+        [
             jax.ShapeDtypeStruct((total, width), f32),
             jax.ShapeDtypeStruct((total, width), f32),
             jax.ShapeDtypeStruct((total, hidden), f32),
@@ -830,9 +949,8 @@
             jax.ShapeDtypeStruct(blocks, bf16),
             jax.ShapeDtypeStruct((micros, rows, width), bf16),
         ],
-        in_specs=[pl.BlockSpec(memory_space=pltpu.SMEM)] + [vmem] * 3 + [hbm] * 6,
-        out_specs=[vmem] * 5 + [hbm] * 3,
-        scratch_shapes=[pltpu.VMEM(w.shape, bf16) for w in weights]
+        [vmem] * 5 + [hbm] * 3,
+        [pltpu.VMEM(w.shape, bf16) for w in weights]
         + [
             pltpu.VMEM(pack, bf16),
             pltpu.VMEM((micros, rows, lanes), bf16),
@@ -845,10 +963,10 @@
         + [dma((micros, count - 1))] * 6
         + [dma((micros, 4)), dma((6,)), dma((micros,)), dma((micros,))],
         compiler_params=pltpu.CompilerParams(
-            collective_id=4 if ship else 2, has_side_effects=True, vmem_limit_bytes=60 * 1024 * 1024
+            collective_id=2, has_side_effects=True, vmem_limit_bytes=60 * 1024 * 1024
         ),
-        name="forward_ship" if ship else "forward_layer",
-    )(lengths, inputs, vectors, up_bias, *weights)
+        name="forward_layer",
+    )
 
 
 def backward_kernel(
@@ -1075,9 +1193,15 @@
     dma = pltpu.SemaphoreType.DMA
     narrow_out, wide_out = (total, width), pre_act.shape
     blocks, pack = (count, micros, rows, lanes), (count, micros, 3, rows, lanes)
-    return pl.pallas_call(
-        functools.partial(backward_kernel, ship),
-        out_shape=[
+    return layer_call(
+        backward_kernel,
+        ship,
+        (
+            lengths, grad_output, inputs, hidden, vectors, pre_act, held, held_last, last_q,
+            *weights,
+        ),
+        [pl.BlockSpec(memory_space=pltpu.SMEM)] + [vmem] * 8 + [hbm] * 6,
+        [
             jax.ShapeDtypeStruct(shape, dtype)
             for shape, dtype in (
                 (narrow_out, f32),
@@ -1094,9 +1218,8 @@
                 ((micros, rows, width), bf16),
             )
         ],
-        in_specs=[pl.BlockSpec(memory_space=pltpu.SMEM)] + [vmem] * 8 + [hbm] * 6,
-        out_specs=[vmem] * 11 + [hbm],
-        scratch_shapes=[
+        [vmem] * 11 + [hbm],
+        [
             pltpu.VMEM(weights[3].shape, bf16),
             pltpu.VMEM(weights[4].shape, bf16),
             pltpu.VMEM(weights[5].shape, bf16),
@@ -1120,7 +1243,7 @@
             collective_id=5 if ship else 3, has_side_effects=True, vmem_limit_bytes=62 * 1024 * 1024
         ),
         name="backward_ship" if ship else "backward_layer",
-    )(lengths, grad_output, inputs, hidden, vectors, pre_act, held, held_last, last_q, *weights)
+    )
 
 
 def in_blocks(matrix):
@@ -1158,7 +1281,10 @@
         0,
     )
     thirds = [w_qkv[0][:, i * width : (i + 1) * width] for i in range(3)]
-    small_full, *full = gather_weights(
+    first_in = block_input[:, 0].reshape(micros * rows, width).astype(jnp.float32)
+    small_full, *full, arrived = first_layer(
+        lengths,
+        first_in,
         [in_blocks(array) for array in (small, *thirds, w_proj[0], w_up[0], w_down[0])],
         (
             (6, 0, 68, True),
@@ -1170,21 +1296,20 @@
             (4, 0, 17, False),
             (5, 16, 1, False),
         ),
+        count,
+        micros,
     )
     vector_rows = small_full[:, 0].transpose(1, 0, 2).reshape(8, width).astype(jnp.float32)
     up_bias = small_full[:, 1, :bias_rows].reshape(1, -1).astype(jnp.float32)
     weights = [array.reshape(-1, array.shape[-1]) for array in full]
 
-    def forward(ship, inputs):
-        return forward_layer(ship, lengths, inputs, vector_rows, up_bias, weights, count, micros)
-
     def landed(blocks):
         return blocks.reshape(micros * rows, width).astype(jnp.float32)
 
-    first_in = block_input[:, 0].reshape(micros * rows, width).astype(jnp.float32)
-    *_, arrived = forward(True, first_in)
     inputs = jnp.where(section == 0, first_in, landed(arrived))
-    output, hidden, pre_act, attn_mixed, last_q, held, held_last, _ = forward(False, inputs)
+    output, hidden, pre_act, attn_mixed, last_q, held, held_last, _ = forward_layer(
+        lengths, inputs, vector_rows, up_bias, weights, count, micros
+    )
     saved = (inputs, hidden, pre_act, held, held_last, last_q)
     *_, arrived = backward_layer(True, lengths, cotangent, saved, vector_rows, weights)
     grad_output = jnp.where(section == 1, cotangent, landed(arrived))

time: 509 us -> 494 us (0.971)
  local copies, waits for them, and re-layouts: 19.7 us -> 11.4 us
  Pallas kernels: 469 us -> 463 us
    pallas_call x5 -> x4, Pallas kernels: 322 us -> 310 us  [the longest x3 169 us: layer_call(): pl.pallas_call(kernel, out_shape=results, in_specs=in_specs, out_specs=sp...]
    unnamed x39 -> x19, local copies, waits for them, and re-layouts: 10.6 us -> 2.3 us
where the time goes in v6:
time: 494 us; the launch traced here: 486 us
  Pallas kernels  463 us (94%)
  local copies, waits for them, and re-layouts  11.4 us (2%)
  other arithmetic  10.3 us (2%)
    pallas_call x3, Pallas kernels, layer_call(): pl.pallas_call(kernel, out_shape=results, in_specs=in_specs, out_specs=sp...  169 us
    pallas_call x1, Pallas kernels, sum_gradients(): pl.pallas_call(functools.partial(sum_kernel, arrays, order), out_shape=ou...  148 us
    pallas_call x1, Pallas kernels, first_layer(): pl.pallas_call(functools.partial(first_kernel, plan, len(shards)), out_sh...  141 us

profile of v6, /device:TPU:1, one launch (start us, length us, event | category | flops | bytes accessed | tf_op | source)
XLA Modules:
  0.0 485.8 jit_solution(16295580047608405640)
XLA Ops:
  0.6 0.0 copy-start.3
  0.7 0.8 select_reduce_fusion
  1.5 0.7 fusion.refs_0_.lengths
  2.2 2.2 slice_bitcast_fusion
  4.4 0.0 copy-start.8
  4.4 0.0 copy-start.7
  4.4 0.0 copy-done.3
  4.4 1.3 copy.23
  5.7 0.0 copy-done.8
  5.7 0.1 reshape_squeeze.14
  5.8 0.1 pad.5.clone
  5.9 0.0 copy-done.7
  5.9 0.7 maximum_bitcast_fusion.refs_2_
  6.5 0.0 copy-start.6
  6.5 0.0 copy-start.4
  6.5 141.1 %gather_forward.1 = (bf16[8,2,8,136]{3,2,1,0:T(8,128)(2,1)}, bf16[8,17,8,1088]{3,2,1,0:T(8,128)(2,1)}, bf16[8,17,8,1088]{3,2,1,0:T(8,128)(2,1)}, bf16[8,17,8,108...) custom-call(s32[2]{0:T(128)} %fusion.refs_0_.lengths, ...), custom_call_target="tpu_custom_call" | custom-call | tf_op jit(solution)/shard_map/gather_forward/pallas_call | solution.py:695
  147.7 0.0 copy-start.1
  147.7 0.0 copy-done.6
  147.7 0.1 compare_convert_fusion
  147.8 0.0 copy-done.4
  147.8 0.2 copy.22
  148.1 0.9 copy-done.1
  149.0 0.0 copy-start.5
  149.0 2.6 convert_select_fusion.1
  151.6 0.0 copy-done.5
  151.7 0.7 reshape.153.vectors.refs_4_
  152.4 0.7 reshape.154.up_bias
  153.1 52.9 %forward_layer.1 = (f32[256,1088]{1,0:T(8,128)}, f32[256,1088]{1,0:T(8,128)}, f32[256,4352]{1,0:T(8,128)}, bf16[256,1088]{1,0:T(8,128)(2,1)}, bf16[2,128,128]{2,...) custom-call(s32[2]{0:T(128)} %fusion.refs_0_.lengths, ...), custom_call_target="tpu_custom_call" | custom-call | tf_op jit(solution)/shard_map/forward_layer/pallas_call | solution.py:919
  206.1 0.0 copy-start
  206.1 60.1 %backward_ship.1 = bf16[2,128,1088]{2,1,0:T(8,128)(2,1)} custom-call(s32[2]{0:T(128)} %fusion.refs_0_.lengths, f32[256,1088]{1,0:T(8,128)} %get-tuple-element.105.refs_1_, f32[256,1088]{1,0:T(8,128)} %get-tuple-element.104.inputs.refs_2_, f32[256,1088]{1,0:T(8,128)} %get-tuple-element.54.refs_3_.hidden, f32[8,1088]{1,0:T(8,128)} %reshape.153.vectors.refs_4_, ...), custom_call_target="tpu_custom_call" | custom-call | tf_op jit(solution)/shard_map/backward_ship/pallas_call | solution.py:919
  266.2 0.0 copy-done
  266.2 2.4 fusion.1
  268.6 55.6 %backward_layer.1 = (f32[256,1088]{1,0:T(8,128)}, bf16[256,1088]{1,0:T(8,128)(2,1)}, bf16[256,1088]{1,0:T(8,128)(2,1)}, bf16[256,1088]{1,0:T(8,128)(2,1)}, bf16[...) custom-call(s32[2]{0:T(128)} %fusion.refs_0_.lengths, ...), custom_call_target="tpu_custom_call" | custom-call | tf_op jit(solution)/shard_map/backward_layer/pallas_call | solution.py:919
  324.2 0.9 reshape.145
  325.1 0.8 reduce.1
  325.9 0.1 reshape.146
  326.0 0.1 pad.2.clone
  326.1 0.8 maximum_maximum_fusion
  326.9 148.0 %sum_gradients.1 = (bf16[4,5,8,1088]{3,2,1,0:T(8,128)(2,1)}, bf16[4,5,8,1088]{3,2,1,0:T(8,128)(2,1)}, bf16[4,5,8,1088]{3,2,1,0:T(8,128)(2,1)}, bf16[4,5,8,1088]{...) custom-call(bf16[256,1088]{1,0:T(8,128)(2,1)} %get-tuple-element.61., ...), custom_call_target="tpu_custom_call" | custom-call | tf_op jit(solution)/shard_map/sum_gradients/pallas_call | solution.py:519
  474.9 0.0 copy-start.2
  474.9 5.3 %assemble.1 = (f32[136,3264]{1,0:T(8,128)}, f32[136,1088]{1,0:T(8,128)}, f32[136,4352]{1,0:T(8,128)}, f32[544,1088]{1,0:T(8,128)}) custom-call(bf16[4,5,8,1088]{3,2,1,0:T(8,128)(2,1)} %get-tuple-element.72.refs_0_, bf16[4,5,8,1088]{3,2,1,0:T(8,128)(2,1)} %get-tuple-element.73.refs_1_, bf16[4,5,8,1088]{3,2,1,0:T(8,128)(2,1)} %get-tuple-element.74.refs_2_, ...), custom_call_target="tpu_custom_call" | custom-call | tf_op jit(solution)/shard_map/assemble/pallas_call | solution.py:566
  480.2 1.3 slice_bitcast_fusion.3
  481.5 0.7 slice.32
  482.2 0.7 reshape.149
  482.9 0.0 copy-done.2
  482.9 1.4 broadcast_select_fusion
  484.3 1.4 copy.26
  (10 shorter events, 0.1 us)
Async XLA Ops:
  0.6 3.8 copy-start.3
  4.4 1.3 copy-start.8
  4.4 1.5 copy-start.7
  6.5 141.2 %copy-start.6 = (s32[2]{0:T(128)S(1)}, s32[2]{0:T(128)}, u32[]{:S(2)}) copy-start(s32[2]{0:T(128)} %fusion.refs_0_.lengths) | copy-start | bytes 28
  6.5 141.3 %copy-start.4 = (bf16[2,1,128,1088]{2,3,1,0:T(8,128)(2,1)S(1)}, bf16[2,1,128,1088]{2,3,1,0:T(8,128)(2,1)}, u32[]{:S(2)}) copy-start(bf16[2,1,128,1088]{2,3,1,0:T(8,128)(2,1)} %param.11) | copy-start | bytes 1671172
  147.7 1.3 copy-start.1
  149.0 2.6 copy-start.5
  206.1 60.1 %copy-start = (f32[256,1088]{1,0:T(8,128)S(1)}, f32[256,1088]{1,0:T(8,128)}, u32[]{:S(2)}) copy-start(f32[256,1088]{1,0:T(8,128)} %get-tuple-element.105.refs_1_) | copy-start | bytes 3342340
  474.9 8.0 %copy-start.2 = (f32[256,1088]{1,0:T(8,128)S(1)}, f32[256,1088]{1,0:T(8,128)}, u32[]{:S(2)}) copy-start(f32[256,1088]{1,0:T(8,128)} %get-tuple-element.60) | copy-start | bytes 3342340

commit v7 on v6

--- a/solution.py
+++ b/solution.py
@@ -1046,22 +1046,26 @@
 
     peer_range = range(count - 1)
     grad_two = grad_output[...].astype(jnp.bfloat16)
-    vector_grads[7:8] = column_sum(grad_two)
+    if not ship:
+        vector_grads[7:8] = column_sum(grad_two)
     loads[0].wait()
     for first, size in column_chunks(pre_act.shape[1], 1152):
         columns = slice(first, first + size)
         value, slope = gelu_parts(pre_act[:, columns])
-        activated[:, columns] = value.astype(jnp.bfloat16)
+        if not ship:
+            activated[:, columns] = value.astype(jnp.bfloat16)
         part = (slope * over_lanes(grad_two, vdown[columns, :])).astype(jnp.bfloat16)
         grad_pre[:, columns] = part
-        bias_grads[:, columns] = column_sum(part)
+        if not ship:
+            bias_grads[:, columns] = column_sum(part)
         if first == 0:
             loads[1].wait()
             grad_norm[...] = over_lanes(part, vup[:, columns])
         else:
             grad_norm[...] += over_lanes(part, vup[:, columns])
     unit, deviation = normalize(hidden[...])
-    normed_two[...] = (unit * vectors[5:6] + vectors[6:7]).astype(jnp.bfloat16)
+    if not ship:
+        normed_two[...] = (unit * vectors[5:6] + vectors[6:7]).astype(jnp.bfloat16)
     from_norm, gain_sum, bias_sum = norm_back(unit, deviation, vectors[5:6], grad_norm[...])
     vector_grads[5:6] = gain_sum
     vector_grads[6:7] = bias_sum
@@ -1069,7 +1073,8 @@
     grad_norm[...] = grad_hidden
     one = grad_hidden.astype(jnp.bfloat16)
     grad_one[...] = one
-    vector_grads[4:5] = column_sum(one)
+    if not ship:
+        vector_grads[4:5] = column_sum(one)
     loads[2].wait()
     grad_mixed = over_lanes(one, vproj[...]).astype(jnp.bfloat16)
     for m in range(micros):
@@ -1139,7 +1144,8 @@
     for m in range(micros):
         micro(m)
     unit, deviation = normalize(inputs[...])
-    normed_one[...] = (unit * vectors[0:1] + vectors[1:2]).astype(jnp.bfloat16)
+    if not ship:
+        normed_one[...] = (unit * vectors[0:1] + vectors[1:2]).astype(jnp.bfloat16)
     for m in range(micros):
         here = slice(m * rows, (m + 1) * rows)
         for copy in own_back(m):
@@ -1173,8 +1179,10 @@
         else:
             vector_grads[0:1] += gain_sum
             vector_grads[1:2] += bias_sum
-    vector_grads[2:3] = column_sum(grad_q[...])
-    vector_grads[3:4] = column_sum(grad_v[...])
+    if not ship:
+        vector_grads[2:3] = column_sum(grad_q[...])
+    if not ship:
+        vector_grads[3:4] = column_sum(grad_v[...])
     for m in range(micros):
         for j in peer_range:
             out(m, j).wait_send()

time: 494 us -> 494 us (level)
  no operation moved by 1% of the time
where the time goes in v7:
time: 494 us; the launch traced here: 485 us
  Pallas kernels  463 us (94%)
  local copies, waits for them, and re-layouts  11.4 us (2%)
  other arithmetic  10.3 us (2%)
    pallas_call x3, Pallas kernels, layer_call(): pl.pallas_call(kernel, out_shape=results, in_specs=in_specs, out_specs=sp...  168 us
    pallas_call x1, Pallas kernels, sum_gradients(): pl.pallas_call(functools.partial(sum_kernel, arrays, order), out_shape=ou...  148 us
    pallas_call x1, Pallas kernels, first_layer(): pl.pallas_call(functools.partial(first_kernel, plan, len(shards)), out_sh...  141 us

profile of v7, /device:TPU:1, one launch (start us, length us, event | category | flops | bytes accessed | tf_op | source)
XLA Modules:
  0.0 485.5 jit_solution(13298054655119370772)
XLA Ops:
  0.6 0.0 copy-start.3
  0.7 0.8 select_reduce_fusion
  1.5 0.7 fusion.refs_0_.lengths
  2.2 2.2 slice_bitcast_fusion
  4.4 0.0 copy-start.8
  4.4 0.0 copy-start.7
  4.4 0.0 copy-done.3
  4.4 1.3 copy.23
  5.7 0.0 copy-done.8
  5.7 0.1 reshape_squeeze.14
  5.8 0.1 pad.5.clone
  5.9 0.0 copy-done.7
  5.9 0.7 maximum_bitcast_fusion.refs_2_
  6.5 0.0 copy-start.6
  6.5 0.0 copy-start.4
  6.5 141.1 %gather_forward.1 = (bf16[8,2,8,136]{3,2,1,0:T(8,128)(2,1)}, bf16[8,17,8,1088]{3,2,1,0:T(8,128)(2,1)}, bf16[8,17,8,1088]{3,2,1,0:T(8,128)(2,1)}, bf16[8,17,8,108...) custom-call(s32[2]{0:T(128)} %fusion.refs_0_.lengths, ...), custom_call_target="tpu_custom_call" | custom-call | tf_op jit(solution)/shard_map/gather_forward/pallas_call | solution.py:695
  147.7 0.0 copy-start.1
  147.7 0.0 copy-done.6
  147.7 0.1 compare_convert_fusion
  147.8 0.0 copy-done.4
  147.8 0.2 copy.22
  148.1 0.9 copy-done.1
  149.0 0.0 copy-start.5
  149.0 2.6 convert_select_fusion.1
  151.6 0.0 copy-done.5
  151.7 0.7 reshape.153.vectors.refs_4_
  152.4 0.7 reshape.154.up_bias
  153.1 52.9 %forward_layer.1 = (f32[256,1088]{1,0:T(8,128)}, f32[256,1088]{1,0:T(8,128)}, f32[256,4352]{1,0:T(8,128)}, bf16[256,1088]{1,0:T(8,128)(2,1)}, bf16[2,128,128]{2,...) custom-call(s32[2]{0:T(128)} %fusion.refs_0_.lengths, ...), custom_call_target="tpu_custom_call" | custom-call | tf_op jit(solution)/shard_map/forward_layer/pallas_call | solution.py:919
  206.1 0.0 copy-start
  206.1 59.8 %backward_ship.1 = bf16[2,128,1088]{2,1,0:T(8,128)(2,1)} custom-call(s32[2]{0:T(128)} %fusion.refs_0_.lengths, f32[256,1088]{1,0:T(8,128)} %get-tuple-element.105.refs_1_, f32[256,1088]{1,0:T(8,128)} %get-tuple-element.104.inputs.refs_2_, f32[256,1088]{1,0:T(8,128)} %get-tuple-element.54.refs_3_.hidden, f32[8,1088]{1,0:T(8,128)} %reshape.153.vectors.refs_4_, ...), custom_call_target="tpu_custom_call" | custom-call | tf_op jit(solution)/shard_map/backward_ship/pallas_call | solution.py:919
  265.9 0.0 copy-done
  265.9 2.4 fusion.1
  268.3 55.6 %backward_layer.1 = (f32[256,1088]{1,0:T(8,128)}, bf16[256,1088]{1,0:T(8,128)(2,1)}, bf16[256,1088]{1,0:T(8,128)(2,1)}, bf16[256,1088]{1,0:T(8,128)(2,1)}, bf16[...) custom-call(s32[2]{0:T(128)} %fusion.refs_0_.lengths, ...), custom_call_target="tpu_custom_call" | custom-call | tf_op jit(solution)/shard_map/backward_layer/pallas_call | solution.py:919
  323.9 0.9 reshape.145
  324.8 0.8 reduce.1
  325.5 0.1 reshape.146
  325.7 0.1 pad.2.clone
  325.7 0.8 maximum_maximum_fusion
  326.5 148.0 %sum_gradients.1 = (bf16[4,5,8,1088]{3,2,1,0:T(8,128)(2,1)}, bf16[4,5,8,1088]{3,2,1,0:T(8,128)(2,1)}, bf16[4,5,8,1088]{3,2,1,0:T(8,128)(2,1)}, bf16[4,5,8,1088]{...) custom-call(bf16[256,1088]{1,0:T(8,128)(2,1)} %get-tuple-element.61., ...), custom_call_target="tpu_custom_call" | custom-call | tf_op jit(solution)/shard_map/sum_gradients/pallas_call | solution.py:519
  474.5 0.0 copy-start.2
  474.5 5.3 %assemble.1 = (f32[136,3264]{1,0:T(8,128)}, f32[136,1088]{1,0:T(8,128)}, f32[136,4352]{1,0:T(8,128)}, f32[544,1088]{1,0:T(8,128)}) custom-call(bf16[4,5,8,1088]{3,2,1,0:T(8,128)(2,1)} %get-tuple-element.72.refs_0_, bf16[4,5,8,1088]{3,2,1,0:T(8,128)(2,1)} %get-tuple-element.73.refs_1_, bf16[4,5,8,1088]{3,2,1,0:T(8,128)(2,1)} %get-tuple-element.74.refs_2_, ...), custom_call_target="tpu_custom_call" | custom-call | tf_op jit(solution)/shard_map/assemble/pallas_call | solution.py:566
  479.9 1.3 slice_bitcast_fusion.3
  481.2 0.7 slice.32
  481.9 0.7 reshape.149
  482.5 0.0 copy-done.2
  482.5 1.4 broadcast_select_fusion
  483.9 1.4 copy.26
  (10 shorter events, 0.1 us)
Async XLA Ops:
  0.6 3.8 copy-start.3
  4.4 1.3 copy-start.8
  4.4 1.5 copy-start.7
  6.5 141.2 %copy-start.6 = (s32[2]{0:T(128)S(1)}, s32[2]{0:T(128)}, u32[]{:S(2)}) copy-start(s32[2]{0:T(128)} %fusion.refs_0_.lengths) | copy-start | bytes 28
  6.5 141.3 %copy-start.4 = (bf16[2,1,128,1088]{2,3,1,0:T(8,128)(2,1)S(1)}, bf16[2,1,128,1088]{2,3,1,0:T(8,128)(2,1)}, u32[]{:S(2)}) copy-start(bf16[2,1,128,1088]{2,3,1,0:T(8,128)(2,1)} %param.11) | copy-start | bytes 1671172
  147.7 1.3 copy-start.1
  149.0 2.6 copy-start.5
  206.1 59.8 %copy-start = (f32[256,1088]{1,0:T(8,128)S(1)}, f32[256,1088]{1,0:T(8,128)}, u32[]{:S(2)}) copy-start(f32[256,1088]{1,0:T(8,128)} %get-tuple-element.105.refs_1_) | copy-start | bytes 3342340
  474.5 8.0 %copy-start.2 = (f32[256,1088]{1,0:T(8,128)S(1)}, f32[256,1088]{1,0:T(8,128)}, u32[]{:S(2)}) copy-start(f32[256,1088]{1,0:T(8,128)} %get-tuple-element.60) | copy-start | bytes 3342340
